TPU v7x, 512 devices: a whole 4x4x16 slice. The times are simulated.
512 devices in a mesh: space: 16 (over y, z_lo), mem: 32 (over z_hi, x, core).
Axes of the slice: x: 4, y: 4, z: 16 (z_hi: 4, z_lo: 4; z = z_hi * 4 + z_lo), core: 2. Of those that a mesh axis runs over, the one named last changes fastest.
Arguments:
- increment: bfloat16 [1, 1024, 2304], P(None, 'space'), may hold values from -6 to 6
- mask: int32 [1, 1024, 2304], P(None, 'space'), may hold values 0 or 1
- members: bfloat16 [32, 1, 1024, 2304], P('mem', None, 'space'), may hold values from -12 to 12
- weight: float32 [1024, 2304], P('space'), may hold values from 0.5 to 2
- x_inverse: bfloat16 [18, 128, 128], replicated, may hold values from -0.0755 to 1.15
- x_coupling: float32 [17], replicated, may hold values from 0.1 to 0.5
- y_inverse: bfloat16 [8, 128, 128], replicated, may hold values from -0.0755 to 1.15
- y_coupling: float32 [7], replicated, may hold values from 0.1 to 0.5
Outputs:
- covariance_product: bfloat16 [1, 1024, 2304], P(None, 'space')
All inputs are finite; a program needn't handle non-finite values. No bound on the sum of `mask` on one device may be relied on, other than what follows from the above.
Results may differ from a plain program's by a relative error of at most 0.013.
Values may be sent and summed in bfloat16 or wider, within the bound.
No kernel may reach another device: no remote copies, remote signals or barrier semaphores. Data moves between devices by JAX's collectives and lax.ppermute only.
A program may use at most 64 MiB of HBM per device.

v0:
```python
import jax
import jax.numpy as jnp
from jax import lax
from jax.sharding import PartitionSpec as P

BLOCK = 128
NSTEP = 7


def products(blocked, inverse, adjoint, lines_last):
    if lines_last:
        pattern = "ankl,nkj->anjl" if adjoint else "ankl,njk->anjl"
    else:
        pattern = "alnk,nkj->alnj" if adjoint else "alnk,njk->alnj"
    return jnp.einsum(pattern, blocked, inverse, preferred_element_type=jnp.float32)


def entries(product, position, lines_last):
    if lines_last:
        return jnp.moveaxis(product[:, :, position, :], 1, 0)
    return jnp.moveaxis(product[:, :, :, position], 2, 0)


def spread(scalars, column, lines_last):
    if lines_last:
        return jnp.moveaxis(scalars, 0, 1)[:, :, None, :] * column[None, :, :, None]
    return jnp.moveaxis(scalars, 0, 2)[:, :, :, None] * column[None, None, :, :]


def recur_step(carried, inputs):
    source, factor, coupler = inputs
    updated = coupler * (source + factor * carried)
    return (updated, updated)


def run_upward(sources, factor, coupling):
    anchor = jnp.zeros_like(sources[0])
    _, following = lax.scan(recur_step, anchor, (sources[:-1], factor[:-1], coupling), unroll=True)
    return jnp.concatenate([jnp.zeros_like(sources[:1]), following], 0)


def run_downward(sources, factor, coupling):
    anchor = jnp.zeros_like(sources[0])
    _, earlier = lax.scan(
        recur_step, anchor, (sources[1:], factor[1:], coupling), reverse=True, unroll=True
    )
    return jnp.concatenate([earlier, jnp.zeros_like(sources[:1])], 0)


def forward_solve(blocked, inverse, coupling, lines_last):
    ending = inverse.shape[1] - 1
    inv_float = inverse.astype(jnp.float32)
    product = products(blocked, inverse, False, lines_last)
    leading = run_upward(entries(product, ending, lines_last), inv_float[:, ending, 0], coupling)
    first_row = entries(product, 0, lines_last) + leading * inv_float[:, 0, 0][:, None, None]
    trailing = run_downward(first_row, inv_float[:, 0, ending], coupling)
    result = (
        product
        + spread(leading, inv_float[:, :, 0], lines_last)
        + spread(trailing, inv_float[:, :, ending], lines_last)
    )
    return result.astype(jnp.bfloat16)


def adjoint_solve(blocked, inverse, coupling, lines_last):
    ending = inverse.shape[1] - 1
    inv_float = inverse.astype(jnp.float32)
    product = products(blocked, inverse, True, lines_last)
    leading = run_upward(entries(product, ending, lines_last), inv_float[:, 0, ending], coupling)
    first_row = entries(product, 0, lines_last) + leading * inv_float[:, 0, 0][:, None, None]
    trailing = run_downward(first_row, inv_float[:, ending, 0], coupling)
    result = (
        product
        + spread(leading, inv_float[:, 0, :], lines_last)
        + spread(trailing, inv_float[:, ending, :], lines_last)
    )
    return result.astype(jnp.bfloat16)


def local(increment, mask, members, weight, x_inverse, x_coupling, y_inverse, y_coupling):
    local_members, levels, row_count, col_count = members.shape
    land_sea = mask.astype(jnp.float32)
    member_float = members.astype(jnp.float32)
    values = (
        weight[None, None] * land_sea[None] * member_float * increment.astype(jnp.float32)[None]
    ).astype(jnp.bfloat16)
    blocked = values.reshape(local_members * levels, row_count, col_count // BLOCK, BLOCK)
    for repeat in range(NSTEP):
        blocked = adjoint_solve(blocked, x_inverse, x_coupling, False)
    flat_rows = blocked.reshape(local_members * levels, row_count, col_count)
    slab_piece = lax.all_to_all(flat_rows, "space", split_axis=2, concat_axis=1, tiled=True)
    item_count, lat_rows, line_width = slab_piece.shape
    column_blocks = slab_piece.reshape(item_count, lat_rows // BLOCK, BLOCK, line_width)
    for along_repeat in range(NSTEP):
        column_blocks = adjoint_solve(column_blocks, y_inverse, y_coupling, True)
    for along_repeat in range(NSTEP):
        column_blocks = forward_solve(column_blocks, y_inverse, y_coupling, True)
    returned = column_blocks.reshape(item_count, lat_rows, line_width)
    flat_rows = lax.all_to_all(returned, "space", split_axis=1, concat_axis=2, tiled=True)
    blocked = flat_rows.reshape(local_members * levels, row_count, col_count // BLOCK, BLOCK)
    for repeat in range(NSTEP):
        blocked = forward_solve(blocked, x_inverse, x_coupling, False)
    smoothed = blocked.reshape(local_members, levels, row_count, col_count).astype(jnp.float32)
    member_terms = jnp.sum(member_float * weight[None, None] * smoothed, axis=0)
    member_total = local_members * lax.axis_size("mem")
    summed = lax.psum(member_terms, "mem")
    return (land_sea * summed / (member_total - 1)).astype(jnp.bfloat16)


def solution(mesh):
    placed = (
        P(None, "space", None),
        P(None, "space", None),
        P("mem", None, "space", None),
        P("space", None),
        P(),
        P(),
        P(),
        P(),
    )
    return jax.shard_map(
        local, mesh=mesh, in_specs=placed, out_specs=P(None, "space", None), check_vma=False
    )
```

profile of v0, /device:TPU:1, one launch (start us, length us, event | category | flops | bytes accessed | tf_op | source)
XLA Modules:
  0.0 1569.8 jit_solution(4468150742239789127)
XLA Ops:
  43.9 20.3 %constant_dynamic-update-slice_fusion.35 = (f32[18,1,64]{2,1,0:T(1,128)S(1)}, f32[1,1,64]{2,1,0:T(1,128)S(1)}, f32[1,1,64]{2,1,0:T(1,128)S(1)}, f32[1,1,64]{2,1,...) fusion(f32[18,1,64]{2,1,0:T(1,128)S(1)} %bitcast_add_fusion.27,, ...), kind=kLoop, calls=%fused_computation.35 | loop fusion | flops 3199 | bytes 12680
  87.2 20.3 %constant_dynamic-update-slice_fusion.71 = (f32[18,1,64]{2,1,0:T(1,128)S(1)}, f32[1,1,64]{2,1,0:T(1,128)S(1)}, f32[1,1,64]{2,1,0:T(1,128)S(1)}, f32[1,1,64]{2,1,...) fusion(f32[18,1,64]{2,1,0:T(1,128)S(1)} %bitcast_add_fusion.26,, ...), kind=kLoop, calls=%fused_computation.71 | loop fusion | flops 3199 | bytes 12680
  130.6 20.3 %constant_dynamic-update-slice_fusion.107 = (f32[18,1,64]{2,1,0:T(1,128)S(1)}, f32[1,1,64]{2,1,0:T(1,128)S(1)}, f32[1,1,64]{2,1,0:T(1,128)S(1)}, f32[1,1,64]{2,1...) fusion(f32[18,1,64]{2,1,0:T(1,128)S(1)} %bitcast_add_fusion.25,, ...), kind=kLoop, calls=%fused_computation.107 | loop fusion | flops 3199 | bytes 12680
  174.0 20.3 %constant_dynamic-update-slice_fusion.143 = (f32[18,1,64]{2,1,0:T(1,128)S(1)}, f32[1,1,64]{2,1,0:T(1,128)S(1)}, f32[1,1,64]{2,1,0:T(1,128)S(1)}, f32[1,1,64]{2,1...) fusion(f32[18,1,64]{2,1,0:T(1,128)S(1)} %bitcast_add_fusion.24,, ...), kind=kLoop, calls=%fused_computation.143 | loop fusion | flops 3199 | bytes 12680
  217.3 20.3 %constant_dynamic-update-slice_fusion.179 = (f32[18,1,64]{2,1,0:T(1,128)S(1)}, f32[1,1,64]{2,1,0:T(1,128)S(1)}, f32[1,1,64]{2,1,0:T(1,128)S(1)}, f32[1,1,64]{2,1...) fusion(f32[18,1,64]{2,1,0:T(1,128)S(1)} %bitcast_add_fusion.23,, ...), kind=kLoop, calls=%fused_computation.179 | loop fusion | flops 3199 | bytes 12680
  260.7 20.3 %constant_dynamic-update-slice_fusion.215 = (f32[18,1,64]{2,1,0:T(1,128)S(1)}, f32[1,1,64]{2,1,0:T(1,128)S(1)}, f32[1,1,64]{2,1,0:T(1,128)S(1)}, f32[1,1,64]{2,1...) fusion(f32[18,1,64]{2,1,0:T(1,128)S(1)} %bitcast_add_fusion.22,, ...), kind=kLoop, calls=%fused_computation.215 | loop fusion | flops 3199 | bytes 12680
  304.0 20.3 %constant_dynamic-update-slice_fusion.251 = (f32[18,1,64]{2,1,0:T(1,128)S(1)}, f32[1,1,64]{2,1,0:T(1,128)S(1)}, f32[1,1,64]{2,1,0:T(1,128)S(1)}, f32[1,1,64]{2,1...) fusion(f32[18,1,64]{2,1,0:T(1,128)S(1)} %bitcast_add_fusion.21,, ...), kind=kLoop, calls=%fused_computation.251 | loop fusion | flops 3199 | bytes 12680
  328.4 13.9 reduce.438
  343.4 9.2 all-to-all-start
  400.3 8.2 constant_dynamic-update-slice_fusion.275
  435.7 8.2 constant_dynamic-update-slice_fusion.299
  471.2 8.2 constant_dynamic-update-slice_fusion.323
  506.6 8.2 constant_dynamic-update-slice_fusion.347
  542.1 8.2 constant_dynamic-update-slice_fusion.371
  577.7 8.2 constant_dynamic-update-slice_fusion.395
  613.1 8.2 constant_dynamic-update-slice_fusion.419
  936.2 20.2 %constant_dynamic-update-slice_fusion.623 = (f32[18,1,64]{2,1,0:T(1,128)S(1)}, f32[1,1,64]{2,1,0:T(1,128)S(1)}, f32[1,1,64]{2,1,0:T(1,128)S(1)}, f32[1,1,64]{2,1...) fusion(f32[18,1,64]{2,1,0:T(1,128)S(1)} %bitcast_add_fusion.20,, ...), kind=kLoop, calls=%fused_computation.623 | loop fusion | flops 3199 | bytes 12680
  979.5 20.2 %constant_dynamic-update-slice_fusion.659 = (f32[18,1,64]{2,1,0:T(1,128)S(1)}, f32[1,1,64]{2,1,0:T(1,128)S(1)}, f32[1,1,64]{2,1,0:T(1,128)S(1)}, f32[1,1,64]{2,1...) fusion(f32[18,1,64]{2,1,0:T(1,128)S(1)} %bitcast_add_fusion.19,, ...), kind=kLoop, calls=%fused_computation.659 | loop fusion | flops 3199 | bytes 12680
  1022.9 20.2 %constant_dynamic-update-slice_fusion.695 = (f32[18,1,64]{2,1,0:T(1,128)S(1)}, f32[1,1,64]{2,1,0:T(1,128)S(1)}, f32[1,1,64]{2,1,0:T(1,128)S(1)}, f32[1,1,64]{2,1...) fusion(f32[18,1,64]{2,1,0:T(1,128)S(1)} %bitcast_add_fusion.18,, ...), kind=kLoop, calls=%fused_computation.695 | loop fusion | flops 3199 | bytes 12680
  1066.2 20.2 %constant_dynamic-update-slice_fusion.731 = (f32[18,1,64]{2,1,0:T(1,128)S(1)}, f32[1,1,64]{2,1,0:T(1,128)S(1)}, f32[1,1,64]{2,1,0:T(1,128)S(1)}, f32[1,1,64]{2,1...) fusion(f32[18,1,64]{2,1,0:T(1,128)S(1)} %bitcast_add_fusion.17,, ...), kind=kLoop, calls=%fused_computation.731 | loop fusion | flops 3199 | bytes 12680
  1109.6 20.2 %constant_dynamic-update-slice_fusion.767 = (f32[18,1,64]{2,1,0:T(1,128)S(1)}, f32[1,1,64]{2,1,0:T(1,128)S(1)}, f32[1,1,64]{2,1,0:T(1,128)S(1)}, f32[1,1,64]{2,1...) fusion(f32[18,1,64]{2,1,0:T(1,128)S(1)} %bitcast_add_fusion.16,, ...), kind=kLoop, calls=%fused_computation.767 | loop fusion | flops 3199 | bytes 12680
  1152.9 20.2 %constant_dynamic-update-slice_fusion.803 = (f32[18,1,64]{2,1,0:T(1,128)S(1)}, f32[1,1,64]{2,1,0:T(1,128)S(1)}, f32[1,1,64]{2,1,0:T(1,128)S(1)}, f32[1,1,64]{2,1...) fusion(f32[18,1,64]{2,1,0:T(1,128)S(1)} %bitcast_add_fusion.15,, ...), kind=kLoop, calls=%fused_computation.803 | loop fusion | flops 3199 | bytes 12680
  1196.3 20.2 %constant_dynamic-update-slice_fusion.839 = (f32[18,1,64]{2,1,0:T(1,128)S(1)}, f32[1,1,64]{2,1,0:T(1,128)S(1)}, f32[1,1,64]{2,1,0:T(1,128)S(1)}, f32[1,1,64]{2,1...) fusion(f32[18,1,64]{2,1,0:T(1,128)S(1)} %bitcast_add_fusion.14,, ...), kind=kLoop, calls=%fused_computation.839 | loop fusion | flops 3199 | bytes 12680
  1219.7 340.9 %all-reduce.2.cloned.1.call-done = f32[1,64,2304]{2,1,0:T(8,128)} async-done(((f32[1,64,2304]{2,1,0:T(8,128)}), f32[1,64,2304]{2,1,0:T(8,128)}) %all-reduce.2.cloned.1.call-update) | async-done | bytes 589840 | tf_op jit(solution)/shard_map/psum | solution.py:106
  (1123 shorter events, 842.1 us)
Async XLA Ops:
  9.0 295.0 %copy-start.11 = (f32[18]{0:T(128)}, f32[18]{0:T(128)S(1)}, u32[]{:S(2)}) copy-start(f32[18]{0:T(128)S(1)} %slice_reduce_fusion.126) | copy-start | bytes 220
  328.4 32.2 %copy-start.1 = (bf16[8,128,128]{2,1,0:T(8,128)(2,1)S(1)}, bf16[8,128,128]{2,1,0:T(8,128)(2,1)}, u32[]{:S(2)}) copy-start(bf16[8,128,128]{2,1,0:T(8,128)(2,1)} %param.14) | copy-start | bytes 786436
  343.4 32.6 %all-to-all-start = ((bf16[16,2,4608]{2,1,0:T(2,128)(2,1)}), bf16[16,2,4608]{2,1,0:T(2,128)(2,1)}, u32[]{:S(2)}, u32[]{:S(2)}) async-start(bf16[16,2,4608]{2,1,0:T(2,128)(2,1)} %reshape.22085), calls=%async_computation | async-start | bytes 589824 | tf_op jit(solution)/shard_map/all_to_all | solution.py:91
  361.4 13.9 copy-start.15
  384.1 11.0 copy-start.29
  384.1 16.1 %copy-start.13 = (f32[8]{0:T(128)S(1)}, f32[8]{0:T(128)}, u32[]{:S(2)}) copy-start(f32[8]{0:T(128)} %slice_reduce_fusion.127) | copy-start | bytes 100
  419.1 11.5 copy-start.28
  454.6 11.5 copy-start.27
  490.0 11.5 copy-start.26
  525.5 11.5 copy-start.25
  560.9 10.4 copy-start.38
  560.9 11.6 copy-start.24
  596.5 11.5 copy-start.23
  632.0 11.4 copy-start.22
  667.5 11.4 copy-start.21
  703.1 11.4 copy-start.20
  738.7 11.4 copy-start.19
  774.3 11.4 copy-start.18
  809.9 11.6 copy-start.17
  845.7 11.4 copy-start.16
  893.3 15.7 %all-to-all-start.1 = ((bf16[16,2,4608]{2,1,0:T(2,128)(2,1)}), bf16[16,2,4608]{2,1,0:T(2,128)(2,1)S(1)}, u32[]{:S(2)}, u32[]{:S(2)}) async-start(bf16[16,2,4608]{2,1,0:T(2,128)(2,1)} %reshape.22087), calls=%async_computation.1 | async-start | bytes 589824 | tf_op jit(solution)/shard_map/all_to_all | solution.py:99
  900.3 660.4 %all-reduce.2.cloned.1.call-start = ((), (), s32[]{:S(2)}) async-start(), calls=%async_computation.2 | async-start | bytes 1179648 | tf_op jit(solution)/shard_map/psum | solution.py:106
  913.8 22.3 %copy-start.12 = (f32[18]{0:T(128)S(1)}, f32[18]{0:T(128)}, u32[]{:S(2)}) copy-start(f32[18]{0:T(128)} %copy-done.11) | copy-start | bytes 220
  1218.8 341.8 %copy-start.6 = (s32[1,64,2304]{2,1,0:T(8,128)S(1)}, s32[1,64,2304]{2,1,0:T(8,128)}, u32[]{:S(2)}) copy-start(s32[1,64,2304]{2,1,0:T(8,128)} %param.9) | copy-start | bytes 1769476
  (23 other events, 156.8 us)
Sparse Core Ops, SparseCore 0:
  1219.8 340.7 all-reduce.1
where the time goes:
time: 1600 us; the launch traced here: 1570 us
  other arithmetic  1100 us (69%)
  waiting for transfers between devices  344 us (22%)
  local copies, waits for them, and re-layouts  68 us (4%)
  between operations  22.5 us (1%)
  matrix products  16.7 us (1%)
  starting transfers between devices  16.2 us (1%)
    unnamed x394, other arithmetic  891 us
    psum x1, waiting for transfers between devices, local(): summed = lax.psum(member_terms, 'mem')  341 us
    concatenate x42, other arithmetic, run_upward(): return jnp.concatenate([jnp.zeros_like(sources[:1]), following], 0)  77.5 us
    mul x14, other arithmetic, recur_step(): updated = coupler * (source + factor * carried)  64.6 us
    slice x14, other arithmetic, run_upward(): lax.scan(recur_step, anchor, (sources[:-1], factor[:-1], coupling), unrol...  61.6 us
  transfers between devices with their start and end apart: 3, of which 2 were waited for; matrix products, arithmetic and copies ran while one was open for 2% of the time, Pallas kernels for 0%

commit v1 on v0

v1 whole, which is shorter than its diff:
```python
import functools

import jax
import jax.numpy as jnp
from jax import lax
from jax.experimental import pallas as pl
from jax.experimental.pallas import tpu as pltpu
from jax.sharding import PartitionSpec as P


BLOCK = 128
LAST = BLOCK - 1
NSTEP = 7
HALF = 64
EXTRA = 16
F32 = jnp.float32
BF16 = jnp.bfloat16
VMEM_LIMIT = 50 * 2**20


def dot(a, b):
    return lax.dot_general(a, b, (((1,), (0,)), ((), ())), preferred_element_type=F32)


def dot_nt(a, b):
    return lax.dot_general(a, b, (((1,), (1,)), ((), ())), preferred_element_type=F32)


def round_up(value, unit):
    return (value + unit - 1) // unit * unit


def coupling_rows(nb, depth):
    return round_up(2 * NSTEP * nb, depth)


def prepare_kernel(nb, group, c_ref, g_ref, pow_ref, kta_ref, ktf_ref, rb_ref, cb_ref,
                   rs, cs, big, rmat, qmat, ct):
    pad = round_up(nb, 8)
    kp = ct.shape[0]
    width = nb * BLOCK
    select = jnp.where(
        lax.broadcasted_iota(jnp.int32, (16, BLOCK), 1)
        == lax.broadcasted_iota(jnp.int32, (16, BLOCK), 0) * LAST, 1.0, 0.0).astype(BF16)
    rs[...] = jnp.zeros_like(rs)
    cs[...] = jnp.zeros_like(cs)

    def one(j):
        g = g_ref[j]
        powers = {1: (g, g.astype(F32))}

        def mul(k, a, b):
            full = dot(powers[a][0], powers[b][0])
            powers[k] = (full.astype(BF16), full)

        mul(2, 1, 1)
        mul(3, 2, 1)
        mul(4, 2, 2)
        mul(5, 3, 2)
        mul(6, 4, 2)
        mul(7, 4, 3)
        pow_ref[j] = powers[NSTEP][0]
        for k in range(1, NSTEP + 1):
            low, full = powers[k]
            rs[k - 1, 0, pl.ds(j, 1), :] = full[0:1, :]
            rs[k - 1, 1, pl.ds(j, 1), :] = full[LAST:BLOCK, :]
            columns = dot_nt(select, low)
            cs[k - 1, 0, pl.ds(j, 1), :] = columns[0:1, :]
            cs[k - 1, 1, pl.ds(j, 1), :] = columns[1:2, :]

    def some(i, carry):
        for offset in range(group):
            one(i * group + offset)
        return carry

    lax.fori_loop(0, nb // group, some, 0)

    own = (lax.broadcasted_iota(jnp.int32, (nb, width), 1) // BLOCK
           == lax.broadcasted_iota(jnp.int32, (nb, width), 0))
    for source, target in ((rs, rb_ref), (cs, cb_ref)):
        big[...] = jnp.zeros_like(big)
        for k in range(1, NSTEP + 1):
            for kind in range(2):
                stacked = source[k - 1, 1 - kind, 0:nb, :]
                wide = jnp.concatenate([stacked] * nb, axis=1)
                at = ((k - 1) * 2 + kind) * nb
                big[at:at + nb, :] = jnp.where(own, wide, 0.0)
        target[...] = big[...].astype(BF16)

    lane = lax.broadcasted_iota(jnp.int32, (1, BLOCK), 1)
    row = lax.broadcasted_iota(jnp.int32, (pad, kp), 0)
    lanes = lax.broadcasted_iota(jnp.int32, (pad, kp), 1)
    for adjoint, kt_ref, edge_ref in ((True, kta_ref, cb_ref), (False, ktf_ref, rb_ref)):
        def corner(k, a, b):
            if not adjoint:
                a, b = b, a
            return rs[k - 1, a, :, 0:1] if b == 0 else rs[k - 1, a, :, LAST:BLOCK]

        gain_s = jnp.broadcast_to(corner(1, 0, 1), (pad, BLOCK))
        gain_t = jnp.broadcast_to(corner(1, 1, 0), (pad, BLOCK))
        gain_0 = jnp.broadcast_to(corner(1, 0, 0), (pad, BLOCK))
        rmat[...] = jnp.zeros_like(rmat)
        s_row = jnp.zeros((1, BLOCK), F32)
        p_rows = []
        for j in range(nb):
            p_rows.append(jnp.where(lane == pad + j, 1.0, 0.0) + gain_0[j:j + 1] * s_row)
            if j + 1 < nb:
                s_row = c_ref[j] * (jnp.where(lane == j, 1.0, 0.0) + gain_s[j:j + 1] * s_row)
                rmat[j + 1:j + 2, :] = s_row
        t_row = jnp.zeros((1, BLOCK), F32)
        for j in range(nb - 2, -1, -1):
            t_row = c_ref[j] * (p_rows[j + 1] + gain_t[j + 1:j + 2] * t_row)
            rmat[pad + j:pad + j + 1, :] = t_row
        spread = rmat[...]

        qmat[...] = jnp.zeros_like(qmat)
        ct[...] = jnp.zeros_like(ct)
        sources, trailing = [], []
        for k in range(NSTEP):
            at = 2 * k * nb
            real = row < nb
            q_last = jnp.where(real & (lanes == at + row), 1.0, 0.0)
            q_first = jnp.where(real & (lanes == at + nb + row), 1.0, 0.0)
            for m in range(k):
                q_last += corner(k - m + 1, 0, 1) * sources[m] + corner(k - m + 1, 1, 1) * trailing[m]
                q_first += corner(k - m + 1, 0, 0) * sources[m] + corner(k - m + 1, 1, 0) * trailing[m]
            qmat[0:pad, :] = q_last
            qmat[pad:2 * pad, :] = q_first
            both = lax.dot_general(spread, qmat[...], (((1,), (0,)), ((), ())),
                                   precision=lax.Precision.HIGHEST, preferred_element_type=F32)
            s_now, t_now = both[0:pad], both[pad:2 * pad]
            sources.append(s_now)
            trailing.append(t_now)
            place = (NSTEP - 1 - k) * 2 * nb
            ct[place:place + nb, :] = t_now[0:nb]
            ct[place + nb:place + 2 * nb, :] = s_now[0:nb]
        kt_ref[...] = dot(ct[...].astype(BF16), edge_ref[...]).astype(BF16)


def prepare(inverse, coupling, group):
    nb = inverse.shape[0]
    width = nb * BLOCK
    kp = coupling_rows(nb, BLOCK)
    pad = round_up(nb, 8)
    vmem = pl.BlockSpec(memory_space=pltpu.VMEM)
    table = jax.ShapeDtypeStruct((kp, width), BF16)
    return pl.pallas_call(
        functools.partial(prepare_kernel, nb, group),
        out_shape=(jax.ShapeDtypeStruct((nb, BLOCK, BLOCK), BF16), table, table, table, table),
        in_specs=[pl.BlockSpec(memory_space=pltpu.SMEM), vmem],
        out_specs=(vmem,) * 5,
        scratch_shapes=[
            pltpu.VMEM((NSTEP, 2, pad, BLOCK), F32),
            pltpu.VMEM((NSTEP, 2, pad, BLOCK), F32),
            pltpu.VMEM((kp, width), F32),
            pltpu.VMEM((2 * pad, BLOCK), F32),
            pltpu.VMEM((BLOCK, kp), F32),
            pltpu.VMEM((kp, kp), F32),
        ],
        compiler_params=pltpu.CompilerParams(vmem_limit_bytes=VMEM_LIMIT),
        cost_estimate=pl.CostEstimate(
            flops=nb * 20 * 2 * BLOCK**3, bytes_accessed=10 * kp * width, transcendentals=0),
    )(coupling, inverse)


def run_steps(lines, nb, pow_ref, kt_ref, out_ref, adjoint):
    coupled = dot_nt(lines[...], kt_ref[...]).astype(BF16)
    results = []
    for j in range(nb):
        at = slice(j * BLOCK, (j + 1) * BLOCK)
        own = (dot if adjoint else dot_nt)(lines[:, at], pow_ref[j])
        results.append(own + dot(coupled, out_ref[:, at]))
    return results


def start_kernel(increment_ref, mask_ref, members_ref, weight_ref, out_ref):
    values = (weight_ref[...] * mask_ref[0].astype(F32) * members_ref[0, 0].astype(F32)
              * increment_ref[0].astype(F32))
    shares = out_ref.shape[0]
    for s in range(shares):
        out_ref[s, 0:HALF, :] = values[:, s * BLOCK:(s + 1) * BLOCK].astype(BF16)
    for half in range(2):
        at = (shares + half) * BLOCK
        tail = values[:, at:at + BLOCK]
        turned = jnp.concatenate([tail, tail], axis=0).T
        for s in range(8):
            out_ref[half * 8 + s, HALF:HALF + EXTRA, :] = turned[s * EXTRA:(s + 1) * EXTRA].astype(BF16)


def column_kernel(nb, in_ref, pow_ref, kta_ref, ktf_ref, rb_ref, cb_ref, out_ref, lines):
    for j in range(nb):
        at = slice(j * BLOCK, (j + 1) * BLOCK)
        square = jnp.concatenate([in_ref[2 * j, 0:HALF, :], in_ref[2 * j + 1, 0:HALF, :]], axis=0)
        lines[0:BLOCK, at] = square.astype(F32).T.astype(BF16)
        lane = lax.broadcasted_iota(jnp.int32, (EXTRA, BLOCK), 1)
        tail = jnp.where(lane < HALF, in_ref[2 * j, HALF:HALF + EXTRA, :].astype(F32),
                         in_ref[2 * j + 1, HALF:HALF + EXTRA, :].astype(F32))
        lines[BLOCK:BLOCK + EXTRA, at] = tail.astype(BF16)
    for j, block in enumerate(run_steps(lines, nb, pow_ref, kta_ref, rb_ref, True)):
        lines[:, j * BLOCK:(j + 1) * BLOCK] = block.astype(BF16)
    for j, block in enumerate(run_steps(lines, nb, pow_ref, ktf_ref, cb_ref, False)):
        square = block[0:BLOCK].T.astype(BF16)
        tail = block[BLOCK:BLOCK + EXTRA].astype(BF16)
        for half in range(2):
            out_ref[2 * j + half, 0:HALF, :] = square[half * HALF:(half + 1) * HALF]
            out_ref[2 * j + half, HALF:HALF + EXTRA, :] = tail


def row_kernel(nb, parity_ref, in_ref, members_ref, weight_ref, pow_ref, kta_ref, ktf_ref, rb_ref, cb_ref,
               out_ref, lines):
    shares = in_ref.shape[0]
    for s in range(shares):
        lines[:, s * BLOCK:(s + 1) * BLOCK] = in_ref[s, 0:HALF, :]
    odd = parity_ref[0] == 1
    for half in range(2):
        tail = jnp.concatenate(
            [in_ref[half * 8 + s, HALF:HALF + EXTRA, :] for s in range(8)], axis=0).astype(F32).T
        tail = jnp.where(odd, tail[HALF:BLOCK], tail[0:HALF])
        at = (shares + half) * BLOCK
        lines[:, at:at + BLOCK] = tail.astype(BF16)
    for j, block in enumerate(run_steps(lines, nb, pow_ref, kta_ref, rb_ref, True)):
        lines[:, j * BLOCK:(j + 1) * BLOCK] = block.astype(BF16)
    takers, middle = out_ref.shape[0], nb // 2
    blocks = run_steps(lines, nb, pow_ref, ktf_ref, cb_ref, False)
    for j in range(middle):
        left, right = slice(j * BLOCK, (j + 1) * BLOCK), slice((middle + j) * BLOCK, (middle + j + 1) * BLOCK)
        term_left = members_ref[0, 0, :, left].astype(F32) * weight_ref[:, left] * blocks[j]
        term_right = members_ref[0, 0, :, right].astype(F32) * weight_ref[:, right] * blocks[middle + j]
        for taker in range(takers):
            rows = slice(taker * 8, taker * 8 + 8)
            out_ref[taker, :, left] = jnp.concatenate([term_left[rows], term_right[rows]], axis=0).astype(BF16)


def sum_kernel(scale, in_ref, out_ref):
    total = in_ref[0].astype(F32)
    for source in range(1, in_ref.shape[0]):
        total += in_ref[source].astype(F32)
    if scale is not None:
        total = total / scale
    total = total.astype(BF16)
    for target in range(out_ref.shape[0]):
        out_ref[target] = total


def final_kernel(mask_ref, in_ref, out_ref):
    shares, _, width = in_ref.shape
    for pair in range(shares // 2):
        one, two = in_ref[2 * pair].astype(F32), in_ref[2 * pair + 1].astype(F32)
        rows = slice(pair * 16, pair * 16 + 16)
        left = jnp.concatenate([one[0:8], two[0:8]], axis=0)
        right = jnp.concatenate([one[8:16], two[8:16]], axis=0)
        out_ref[0, rows, 0:width] = (left * mask_ref[0, rows, 0:width].astype(F32)).astype(BF16)
        out_ref[0, rows, width:2 * width] = (right * mask_ref[0, rows, width:2 * width].astype(F32)).astype(BF16)


def call(kernel, out_shape, operands, scratch=(), scalars=0, flops=1000000):
    vmem = pl.BlockSpec(memory_space=pltpu.VMEM)
    smem = pl.BlockSpec(memory_space=pltpu.SMEM)
    return pl.pallas_call(
        kernel,
        out_shape=jax.ShapeDtypeStruct(out_shape, BF16),
        in_specs=[smem] * scalars + [vmem] * (len(operands) - scalars),
        out_specs=vmem,
        scratch_shapes=list(scratch),
        compiler_params=pltpu.CompilerParams(vmem_limit_bytes=VMEM_LIMIT),
        cost_estimate=pl.CostEstimate(flops=flops, bytes_accessed=2000000, transcendentals=0),
    )(*operands)


def exchange(array, axis, groups=None):
    return lax.all_to_all(array, axis, split_axis=0, concat_axis=0, tiled=True, axis_index_groups=groups)


def local(increment, mask, members, weight, x_inverse, x_coupling, y_inverse, y_coupling):
    _, _, rows, columns = members.shape
    space, mem = lax.axis_size("space"), lax.axis_size("mem")
    x_blocks, y_blocks = x_inverse.shape[0], y_inverse.shape[0]
    near = 8
    far = mem // near
    near_groups = [[z * near + i for i in range(near)] for z in range(far)]
    far_groups = [[z * near + i for z in range(far)] for i in range(near)]
    share = (HALF + EXTRA, BLOCK)

    y_tables = prepare(y_inverse, y_coupling, 8)
    x_tables = prepare(x_inverse, x_coupling, 6)

    sent = call(start_kernel, (space,) + share, (increment, mask, members, weight))
    got = exchange(sent, "space")
    sent = call(functools.partial(column_kernel, y_blocks), (space,) + share, (got,) + tuple(y_tables),
                [pltpu.VMEM((BLOCK + EXTRA, y_blocks * BLOCK), BF16)])
    got = exchange(sent, "space")
    parity = (lax.axis_index("space") % 2).astype(jnp.int32)[None]
    packed = (16, columns // 2)
    terms = call(functools.partial(row_kernel, x_blocks), (near,) + packed,
                 (parity, got, members, weight) + tuple(x_tables),
                 [pltpu.VMEM((rows, columns), BF16)], scalars=1)
    terms = exchange(terms, "mem", near_groups)
    terms = call(functools.partial(sum_kernel, None), (far,) + packed, (terms,))
    terms = exchange(terms, "mem", far_groups)
    terms = call(functools.partial(sum_kernel, float(mem - 1)), (near,) + packed, (terms,))
    terms = exchange(terms, "mem", near_groups)
    return call(final_kernel, (1, rows, columns), (mask, terms))


def solution(mesh):
    placed = (
        P(None, "space", None),
        P(None, "space", None),
        P("mem", None, "space", None),
        P("space", None),
        P(),
        P(),
        P(),
        P(),
    )
    return jax.shard_map(
        local, mesh=mesh, in_specs=placed, out_specs=P(None, "space", None), check_vma=False
    )
```

time: 1600 us -> 106 us (0.07); the launches traced: 1570 us -> 105 us
  other arithmetic: 1100 us -> 0 us
  waiting for transfers between devices: 344 us -> 5.04 us
  local copies, waits for them, and re-layouts: 68 us -> 6.17 us
  blocking collectives: 0 us -> 52.7 us
  Pallas kernels: 0 us -> 28.3 us
  between operations: 22.5 us -> 0.1 us
  matrix products: 16.7 us -> 0 us
    unnamed x394 -> x0, other arithmetic: 891 us -> none
    psum x1 -> x0, waiting for transfers between devices: 341 us -> none  [local(): summed = lax.psum(member_terms, 'mem')]
    concatenate x42 -> x0, other arithmetic: 77.5 us -> none  [run_upward(): return jnp.concatenate([jnp.zeros_like(sources[:1]), following], 0)]
    mul x14 -> x0, other arithmetic: 64.6 us -> none  [recur_step(): updated = coupler * (source + factor * carried)]
    slice x14 -> x0, other arithmetic: 61.6 us -> none  [run_upward(): lax.scan(recur_step, anchor, (sources[:-1], factor[:-1], coupling), unrol...]
    all_to_all x0 -> x3, blocking collectives: none -> 52.7 us  [exchange(): lax.all_to_all(array, axis, split_axis=0, concat_axis=0, tiled=True, axis...]
    pallas_call x0 -> x8, Pallas kernels: none -> 28.3 us  [the longest x2 19.6 us: prepare(): pl.pallas_call(functools.partial(prepare_kernel, nb, group), out_shape=(j...]
    slice x41 -> x0, local copies, waits for them, and re-layouts: 23.7 us -> none  [the longest x14 7.7 us: entries(): return jnp.moveaxis(product[:, :, :, position], 2, 0)]
  transfers between devices with their start and end apart: 3 -> 2, of which waited for: 2 -> 1; matrix products, arithmetic and copies ran while one was open for 2% -> 0% of each run, Pallas kernels for 0% -> 19%
where the time goes in v1:
time: 106 us; the launch traced here: 105 us
  blocking collectives  52.7 us (50%)
  Pallas kernels  28.3 us (27%)
  starting transfers between devices  12.7 us (12%)
  local copies, waits for them, and re-layouts  6.17 us (6%)
  waiting for transfers between devices  5.04 us (5%)
    all_to_all x3, blocking collectives, exchange(): lax.all_to_all(array, axis, split_axis=0, concat_axis=0, tiled=True, axis...  52.7 us
    pallas_call x2, Pallas kernels, prepare(): pl.pallas_call(functools.partial(prepare_kernel, nb, group), out_shape=(j...  19.6 us
    all_to_all x2, starting transfers between devices, exchange(): lax.all_to_all(array, axis, split_axis=0, concat_axis=0, tiled=True, axis...  12.7 us
    pallas_call x6, Pallas kernels, call(): pl.pallas_call(kernel, out_shape=jax.ShapeDtypeStruct(out_shape, BF16), i...  8.69 us
    unnamed x24, local copies, waits for them, and re-layouts  6.17 us
    all_to_all x2, waiting for transfers between devices, exchange(): lax.all_to_all(array, axis, split_axis=0, concat_axis=0, tiled=True, axis...  5.04 us
  transfers between devices with their start and end apart: 2, of which 1 were waited for; matrix products, arithmetic and copies ran while one was open for 0% of the time, Pallas kernels for 19%

profile of v1, /device:TPU:1, one launch (start us, length us, event | category | flops | bytes accessed | tf_op | source)
XLA Modules:
  0.0 105.0 jit_solution(7067021892450084481)
XLA Ops:
  0.0 1.1 %copy-done = s32[1,64,2304]{2,1,0:T(8,128)S(1)} copy-done((s32[1,64,2304]{2,1,0:T(8,128)S(1)}, s32[1,64,2304]{2,1,0:T(8,128)}, u32[]{:S(2)}) %copy-start) | copy-done | bytes 589848
  1.1 1.1 %copy-done.2 = f32[64,2304]{1,0:T(8,128)S(1)} copy-done((f32[64,2304]{1,0:T(8,128)S(1)}, f32[64,2304]{1,0:T(8,128)}, u32[]{:S(2)}) %copy-start.2) | copy-done | bytes 589848
  2.1 1.0 copy-done.5
  3.1 1.0 copy-done.7
  4.1 1.0 shard_map.82
  5.0 9.2 %all-to-all-start = ((bf16[16,80,128]{2,1,0:T(8,128)(2,1)}), bf16[16,80,128]{2,1,0:T(8,128)(2,1)S(1)}, u32[]{:S(2)}, u32[]{:S(2)}) async-start(bf16[16,80,128]{2,1,0:T(8,128)(2,1)} %shard_map.82), calls=%async_computation | async-start | bytes 655360 | tf_op jit(solution)/shard_map/all_to_all | solution.py:271
  14.2 0.0 copy-done.9
  14.2 6.2 %shard_map.83 = (bf16[8,128,128]{2,1,0:T(8,128)(2,1)S(1)}, bf16[128,1024]{1,0:T(8,128)(2,1)S(1)}, bf16[128,1024]{1,0:T(8,128)(2,1)S(1)}, bf16[128,1024]{1,0:T(8,128)(2,1)S(1)}, bf16[128,1024]{1,0:T(8,128)(2,1)S(1)}) custom-call(f32[7]{0:T(128)S(1)} %copy-done.10, bf16[8,128,128]{2,1,0:T(8,128)(2,1)S(1)} %copy-done.9), custom_call_target="tpu_custom_call" | custom-call | flops 671088640 | bytes 1310720 | tf_op jit(solution)/shard_map/pallas_call | solution.py:147
  20.4 5.0 %all-to-all-done.in_ref = bf16[16,80,128]{2,1,0:T(8,128)(2,1)S(1)} async-done(((bf16[16,80,128]{2,1,0:T(8,128)(2,1)}), bf16[16,80,128]{2,1,0:T(8,128)(2,1)S(1)}, u32[]{:S(2)}, u32[]{:S(2)}) %all-to-all-start) | async-done | bytes 327712 | tf_op jit(solution)/shard_map/all_to_all | solution.py:271
  25.5 2.3 %shard_map.84 = bf16[16,80,128]{2,1,0:T(8,128)(2,1)} custom-call(bf16[16,80,128]{2,1,0:T(8,128)(2,1)S(1)} %all-to-all-done.in_ref, bf16[8,128,128]{2,1,0:T(8,128)(2,1)S(1)} %get-tuple-element.15.pow_ref, bf16[128,1024]{1,0:T(8,128)(2,1)S(1)} %get-tuple-element.16.kta_ref, bf16[128,1024]{1,0:T(8,128)(2,1)S(1)} %get-tuple-element.17.ktf_ref, ...), custom_call_target="tpu_custom_call" | custom-call | flops 1000000 | bytes 2000000 | tf_op jit(solution)/shard_map/pallas_call | solution.py:259
  27.8 3.6 %all-to-all-start.1 = ((bf16[16,80,128]{2,1,0:T(8,128)(2,1)}), bf16[16,80,128]{2,1,0:T(8,128)(2,1)S(1)}, u32[]{:S(2)}, u32[]{:S(2)}) async-start(bf16[16,80,128]{2,1,0:T(8,128)(2,1)} %shard_map.84), calls=%async_computation.1 | async-start | bytes 655360 | tf_op jit(solution)/shard_map/all_to_all | solution.py:271
  31.4 0.0 copy-start.8
  31.4 1.1 %copy-done.8 = bf16[18,128,128]{2,1,0:T(8,128)(2,1)S(1)} copy-done((bf16[18,128,128]{2,1,0:T(8,128)(2,1)S(1)}, bf16[18,128,128]{2,1,0:T(8,128)(2,1)}, u32[]{:S(2)}) %copy-start.8) | copy-done | bytes 589848
  32.4 13.4 %shard_map.85 = (bf16[18,128,128]{2,1,0:T(8,128)(2,1)S(1)}, bf16[256,2304]{1,0:T(8,128)(2,1)S(1)}, bf16[256,2304]{1,0:T(8,128)(2,1)S(1)}, bf16[256,2304]{1,0:T(8,128)(2,1)}, bf16[256,2304]{1,0:T(8,128)(2,1)}) custom-call(f32[17]{0:T(128)S(1)} %copy-done.11, bf16[18,128,128]{2,1,0:T(8,128)(2,1)S(1)} %copy-done.8), custom_call_target="tpu_custom_call" | custom-call | flops 1509949440 | bytes 5898240 | tf_op jit(solution)/shard_map/pallas_call | solution.py:147
  45.8 1.0 copy-done.4
  46.9 0.0 all-to-all-done.1.in_ref
  46.9 0.0 copy-done.3
  46.9 4.6 %shard_map.86 = bf16[8,16,1152]{2,1,0:T(8,128)(2,1)S(1)} custom-call(s32[1]{0:T(128)} %bitcast.parity_ref, bf16[16,80,128]{2,1,0:T(8,128)(2,1)S(1)} %all-to-all-done.1.in_ref, bf16[1,1,64,2304]{3,2,1,0:T(8,128)(2,1)S(1)} %copy-done.6, f32[64,2304]{1,0:T(8,128)S(1)} %copy-done.3, bf16[18,128,128]{2,1,0:T(8,128)(2,1)S(1)} %get-tuple-element.20.pow_ref, ...), custom_call_target="tpu_custom_call" | custom-call | flops 1000000 | bytes 2000000 | tf_op jit(solution)/shard_map/pallas_call | solution.py:259
  51.5 0.0 copy-start.1
  51.5 13.5 %all_to_all.25.in_ref = bf16[8,16,1152]{2,1,0:T(8,128)(2,1)S(1)} all-to-all(bf16[8,16,1152]{2,1,0:T(8,128)(2,1)S(1)} %shard_map.86), channel_id=1, replica_groups={{0,1,2,3,4,5,6,7},{8,9,10,11,12,13,14,15},{16,17,18,19,20,21,22,23},{24..., dimensions={0} | all-to-all | bytes 589824 | tf_op jit(solution)/shard_map/all_to_all | solution.py:271
  65.0 24.6 %all_to_all.26.in_ref = bf16[4,16,1152]{2,1,0:T(8,128)(2,1)S(1)} all-to-all(bf16[4,16,1152]{2,1,0:T(8,128)(2,1)S(1)} %shard_map.87), channel_id=1, replica_groups={{0,8,16,24},{1,9,17,25},{2,10,18,26},{3,11,19,27},{4,12,20,28},{5,13,21..., dimensions={0} | all-to-all | bytes 294912 | tf_op jit(solution)/shard_map/all_to_all | solution.py:271
  89.6 14.6 %all_to_all.27.in_ref = bf16[8,16,1152]{2,1,0:T(8,128)(2,1)S(1)} all-to-all(bf16[8,16,1152]{2,1,0:T(8,128)(2,1)S(1)} %shard_map.88), channel_id=1, replica_groups={{0,1,2,3,4,5,6,7},{8,9,10,11,12,13,14,15},{16,17,18,19,20,21,22,23},{24..., dimensions={0} | all-to-all | bytes 589824 | tf_op jit(solution)/shard_map/all_to_all | solution.py:271
  104.3 0.0 copy-done.1
  104.3 0.8 shard_map.89
  (15 shorter events, 0.1 us)
Async XLA Ops:
  0.0 1.1 %copy-start = (s32[1,64,2304]{2,1,0:T(8,128)S(1)}, s32[1,64,2304]{2,1,0:T(8,128)}, u32[]{:S(2)}) copy-start(s32[1,64,2304]{2,1,0:T(8,128)} %mask_ref.3) | copy-start | bytes 1769476
  1.1 1.1 %copy-start.2 = (f32[64,2304]{1,0:T(8,128)S(1)}, f32[64,2304]{1,0:T(8,128)}, u32[]{:S(2)}) copy-start(f32[64,2304]{1,0:T(8,128)} %weight_ref.3) | copy-start | bytes 1769476
  2.1 1.0 copy-start.5
  3.1 1.0 copy-start.7
  4.1 10.2 %copy-start.9 = (bf16[8,128,128]{2,1,0:T(8,128)(2,1)S(1)}, bf16[8,128,128]{2,1,0:T(8,128)(2,1)}, u32[]{:S(2)}) copy-start(bf16[8,128,128]{2,1,0:T(8,128)(2,1)} %g_ref.2) | copy-start | bytes 786436
  4.1 10.2 %copy-start.10 = (f32[7]{0:T(128)S(1)}, f32[7]{0:T(128)}, u32[]{:S(2)}) copy-start(f32[7]{0:T(128)} %c_ref.2) | copy-start | bytes 88
  5.0 20.5 %all-to-all-start = ((bf16[16,80,128]{2,1,0:T(8,128)(2,1)}), bf16[16,80,128]{2,1,0:T(8,128)(2,1)S(1)}, u32[]{:S(2)}, u32[]{:S(2)}) async-start(bf16[16,80,128]{2,1,0:T(8,128)(2,1)} %shard_map.82), calls=%async_computation | async-start | bytes 655360 | tf_op jit(solution)/shard_map/all_to_all | solution.py:271
  25.5 5.9 %copy-start.11 = (f32[17]{0:T(128)S(1)}, f32[17]{0:T(128)}, u32[]{:S(2)}) copy-start(f32[17]{0:T(128)} %c_ref.3) | copy-start | bytes 208
  27.8 19.1 %all-to-all-start.1 = ((bf16[16,80,128]{2,1,0:T(8,128)(2,1)}), bf16[16,80,128]{2,1,0:T(8,128)(2,1)S(1)}, u32[]{:S(2)}, u32[]{:S(2)}) async-start(bf16[16,80,128]{2,1,0:T(8,128)(2,1)} %shard_map.84), calls=%async_computation.1 | async-start | bytes 655360 | tf_op jit(solution)/shard_map/all_to_all | solution.py:271
  31.4 1.1 %copy-start.8 = (bf16[18,128,128]{2,1,0:T(8,128)(2,1)S(1)}, bf16[18,128,128]{2,1,0:T(8,128)(2,1)}, u32[]{:S(2)}) copy-start(bf16[18,128,128]{2,1,0:T(8,128)(2,1)} %g_ref.3) | copy-start | bytes 1769476
  32.4 14.4 %copy-start.3 = (f32[64,2304]{1,0:T(8,128)S(1)}, f32[64,2304]{1,0:T(8,128)}, u32[]{:S(2)}) copy-start(f32[64,2304]{1,0:T(8,128)} %weight_ref.3) | copy-start | bytes 1769476
  32.4 14.4 %copy-start.6 = (bf16[1,1,64,2304]{3,2,1,0:T(8,128)(2,1)S(1)}, bf16[1,1,64,2304]{3,2,1,0:T(8,128)(2,1)}, u32[]{:S(2)}) copy-start(bf16[1,1,64,2304]{3,2,1,0:T(8,128)(2,1)} %members_ref.3) | copy-start | bytes 884740
  45.8 1.0 copy-start.4
  51.5 52.8 %copy-start.1 = (s32[1,64,2304]{2,1,0:T(8,128)S(1)}, s32[1,64,2304]{2,1,0:T(8,128)}, u32[]{:S(2)}) copy-start(s32[1,64,2304]{2,1,0:T(8,128)} %mask_ref.3) | copy-start | bytes 1769476

commit v2 on v1

v2 whole, which is shorter than its diff:
```python
import functools

import jax
import jax.numpy as jnp
from jax import lax
from jax.experimental import pallas as pl
from jax.experimental.pallas import tpu as pltpu
from jax.sharding import PartitionSpec as P


BLOCK = 128
LAST = BLOCK - 1
NSTEP = 7
HALF = 64
EXTRA = 16
F32 = jnp.float32
BF16 = jnp.bfloat16
VMEM_LIMIT = 24 * 2**20
WIDE_LIMIT = 60 * 2**20


def dot(a, b):
    return lax.dot_general(a, b, (((1,), (0,)), ((), ())), preferred_element_type=F32)


def dot_nt(a, b):
    return lax.dot_general(a, b, (((1,), (1,)), ((), ())), preferred_element_type=F32)


def round_up(value, unit):
    return (value + unit - 1) // unit * unit


def coupling_rows(nb, depth):
    return round_up(2 * NSTEP * nb, depth)


def prepare_kernel(nb, precise, c_ref, g_ref, *refs):
    fill_tables(nb, precise, c_ref, g_ref, *refs, lambda at: None)


def prepare_far_kernel(nb, precise, c_ref, g_ref, *refs):
    far, near, (left, *scratch) = refs[:5], refs[5:10], refs[10:]
    copies = [pltpu.make_async_copy(near[at], far[at], left.at[at]) for at in range(5)]
    fill_tables(nb, precise, c_ref, g_ref, *near, *scratch, lambda at: copies[at].start())
    for copy in copies:
        copy.wait()


def fill_tables(nb, precise, c_ref, g_ref, pow_ref, kta_ref, ktf_ref, rb_ref, cb_ref,
                   edges, big_rows, big_columns, rmat, qmat, ct,
                   high2, low2, high3, low3, high4, low4, few_rows, few_columns, ready):
    pad = round_up(nb, 8)
    kp = kta_ref.shape[0]
    lane = lax.broadcasted_iota(jnp.int32, (16, BLOCK), 1)
    row = lax.broadcasted_iota(jnp.int32, (16, BLOCK), 0)
    select = jnp.where((row < 2) & (lane == row * LAST), 1.0, 0.0)
    edges[...] = jnp.zeros_like(edges)
    big_rows[...] = jnp.zeros_like(big_rows)
    big_columns[...] = jnp.zeros_like(big_columns)

    def stack(first, *pairs):
        out = first
        for at, (top, bottom) in enumerate(pairs):
            out = jnp.where(row == 2 * at + 2, top, jnp.where(row == 2 * at + 3, bottom, out))
        return out.astype(BF16)

    def split(full):
        high = full.astype(BF16)
        return high, (full - high.astype(F32)).astype(BF16)

    def put_row(j, k, top, bottom):
        at = slice(j * BLOCK, (j + 1) * BLOCK)
        big_rows[(2 * k - 2) * nb + j:(2 * k - 2) * nb + j + 1, at] = bottom
        big_rows[(2 * k - 1) * nb + j:(2 * k - 1) * nb + j + 1, at] = top
        edges[k - 1, 0, j:j + 1, :] = top
        edges[k - 1, 1, j:j + 1, :] = bottom

    def put_column(j, k, left, right):
        at = slice(j * BLOCK, (j + 1) * BLOCK)
        big_columns[(2 * k - 2) * nb + j:(2 * k - 2) * nb + j + 1, at] = right
        big_columns[(2 * k - 1) * nb + j:(2 * k - 1) * nb + j + 1, at] = left

    def ends(full):
        return full[0:1], full[LAST:BLOCK]

    def pair(rows, first):
        return rows[first:first + 1], rows[first + 1:first + 2]

    for j in range(nb):
        g = g_ref[j]
        g_full = g.astype(F32)
        second = dot(g, g)
        high2[j], low2[j] = split(second)
        put_row(j, 1, *ends(g_full))
        put_row(j, 2, *ends(second))
        few_rows[j] = stack(jnp.zeros((16, BLOCK), F32), ends(g_full), ends(second))
        columns = dot_nt(select.astype(BF16), g)
        put_column(j, 1, *pair(columns, 0))
        few_columns[j] = stack(select, pair(columns, 0)).astype(F32)

    for j in range(nb):
        both = jnp.concatenate([g_ref[j], high2[j]], axis=0)
        if precise:
            result = dot(jnp.concatenate([both, both], axis=1),
                         jnp.concatenate([high2[j], low2[j]], axis=0))
            third, fourth = result[0:BLOCK], result[BLOCK:2 * BLOCK] + dot(low2[j], high2[j])
        else:
            result = dot(both, high2[j])
            third, fourth = result[0:BLOCK], result[BLOCK:2 * BLOCK]
        high3[j], low3[j] = split(third)
        high4[j], low4[j] = split(fourth)
        put_row(j, 3, *ends(third))
        put_row(j, 4, *ends(fourth))
        old = few_columns[j]
        columns = dot_nt(old.astype(BF16), high2[j])
        put_column(j, 2, *pair(columns, 0))
        put_column(j, 3, *pair(columns, 2))
        few_columns[j] = stack(old, pair(old, 2), pair(columns, 0), pair(columns, 2)).astype(F32)

    for j in range(nb):
        left = jnp.concatenate([high3[j], few_rows[j]], axis=0)
        if precise:
            result = dot(jnp.concatenate([left, left], axis=1),
                         jnp.concatenate([high4[j], low4[j]], axis=0))
            seventh = result[0:BLOCK] + dot(low3[j], high4[j])
        else:
            result = dot(left, high4[j])
            seventh = result[0:BLOCK]
        pow_ref[j] = seventh.astype(BF16)
        put_row(j, 5, *pair(result, BLOCK + 2))
        put_row(j, 6, *pair(result, BLOCK + 4))
        put_row(j, 7, *ends(seventh))
        columns = dot_nt(few_columns[j].astype(BF16), high4[j])
        for k in range(4):
            put_column(j, 4 + k, *pair(columns, 2 * k))

    ready(0)
    rb_ref[...] = big_rows[...].astype(BF16)
    ready(3)
    cb_ref[...] = big_columns[...].astype(BF16)
    ready(4)

    def corner(run, k, a, b):
        if run == 1:
            a, b = b, a
        return edges[k - 1, a, :, 0:1] if b == 0 else edges[k - 1, a, :, LAST:BLOCK]

    unit = lax.broadcasted_iota(jnp.int32, (1, BLOCK), 1)
    runs = range(2)
    gain_s = [jnp.broadcast_to(corner(run, 1, 0, 1), (pad, BLOCK)) for run in runs]
    gain_t = [jnp.broadcast_to(corner(run, 1, 1, 0), (pad, BLOCK)) for run in runs]
    gain_0 = jnp.broadcast_to(corner(0, 1, 0, 0), (pad, BLOCK))
    rmat[...] = jnp.zeros_like(rmat)
    qmat[...] = jnp.zeros_like(qmat)
    ct[...] = jnp.zeros_like(ct)
    s_row = [jnp.zeros((1, BLOCK), F32) for run in runs]
    p_rows = [[], []]
    for j in range(nb):
        for run in runs:
            p_rows[run].append(jnp.where(unit == pad + j, 1.0, 0.0) + gain_0[j:j + 1] * s_row[run])
            if j + 1 < nb:
                s_row[run] = c_ref[j] * (jnp.where(unit == j, 1.0, 0.0) + gain_s[run][j:j + 1] * s_row[run])
                rmat[run, j + 1:j + 2, :] = s_row[run]
    t_row = [jnp.zeros((1, BLOCK), F32) for run in runs]
    for j in range(nb - 2, -1, -1):
        for run in runs:
            t_row[run] = c_ref[j] * (p_rows[run][j + 1] + gain_t[run][j + 1:j + 2] * t_row[run])
            rmat[run, pad + j:pad + j + 1, :] = t_row[run]

    block = lax.broadcasted_iota(jnp.int32, (pad, kp), 0)
    lanes = lax.broadcasted_iota(jnp.int32, (pad, kp), 1)
    sources, trailing = [[], []], [[], []]
    for k in range(NSTEP):
        at = 2 * k * nb
        place = (NSTEP - 1 - k) * 2 * nb
        for run in runs:
            q_last = jnp.where((block < nb) & (lanes == at + block), 1.0, 0.0)
            q_first = jnp.where((block < nb) & (lanes == at + nb + block), 1.0, 0.0)
            for m in range(k):
                s_old, t_old = sources[run][m], trailing[run][m]
                q_last += corner(run, k - m + 1, 0, 1) * s_old + corner(run, k - m + 1, 1, 1) * t_old
                q_first += corner(run, k - m + 1, 0, 0) * s_old + corner(run, k - m + 1, 1, 0) * t_old
            qmat[run, 0:pad, :] = q_last
            qmat[run, pad:2 * pad, :] = q_first
        for run in runs:
            now = lax.dot_general(rmat[run], qmat[run], (((1,), (0,)), ((), ())),
                                  precision=lax.Precision.HIGHEST, preferred_element_type=F32)
            sources[run].append(now[0:pad])
            trailing[run].append(now[pad:2 * pad])
            ct[run, place:place + nb, :] = now[pad:pad + nb]
            ct[run, place + nb:place + 2 * nb, :] = now[0:nb]
    kta_ref[...] = dot(ct[0].astype(BF16), cb_ref[...]).astype(BF16)
    ready(1)
    ktf_ref[...] = dot(ct[1].astype(BF16), rb_ref[...]).astype(BF16)
    ready(2)


def prepare(inverse, coupling, precise, far):
    nb = inverse.shape[0]
    width = nb * BLOCK
    kp = coupling_rows(nb, BLOCK)
    pad = round_up(nb, 8)
    vmem = pl.BlockSpec(memory_space=pltpu.VMEM)
    table = jax.ShapeDtypeStruct((kp, width), BF16)
    tables = (jax.ShapeDtypeStruct((nb, BLOCK, BLOCK), BF16), table, table, table, table)
    staging = [pltpu.VMEM(array.shape, array.dtype) for array in tables] + [pltpu.SemaphoreType.DMA((5,))]
    return pl.pallas_call(
        functools.partial(prepare_far_kernel if far else prepare_kernel, nb, precise),
        out_shape=tables,
        in_specs=[pl.BlockSpec(memory_space=pltpu.SMEM), vmem],
        out_specs=(pl.BlockSpec(memory_space=pltpu.HBM) if far else vmem,) * 5,
        scratch_shapes=(staging if far else []) + [
            pltpu.VMEM((NSTEP, 2, pad, BLOCK), F32),
            pltpu.VMEM((kp, width), F32),
            pltpu.VMEM((kp, width), F32),
            pltpu.VMEM((2, 2 * pad, BLOCK), F32),
            pltpu.VMEM((2, BLOCK, kp), F32),
            pltpu.VMEM((2, kp, kp), F32),
        ] + [pltpu.VMEM((nb, BLOCK, BLOCK), BF16)] * 6 + [
            pltpu.VMEM((nb, 16, BLOCK), BF16),
            pltpu.VMEM((nb, 16, BLOCK), F32),
        ],
        compiler_params=pltpu.CompilerParams(vmem_limit_bytes=WIDE_LIMIT if far else VMEM_LIMIT),
        cost_estimate=pl.CostEstimate(
            flops=nb * 20 * 2 * BLOCK**3, bytes_accessed=10 * kp * width, transcendentals=0),
    )(coupling, inverse)


def run_steps(lines, nb, pow_ref, kt_ref, out_ref, adjoint, arrive=lambda *refs: None):
    arrive(kt_ref)
    coupled = dot_nt(lines[...], kt_ref[...]).astype(BF16)
    arrive(pow_ref, out_ref)
    results = []
    for j in range(nb):
        at = slice(j * BLOCK, (j + 1) * BLOCK)
        own = (dot if adjoint else dot_nt)(lines[:, at], pow_ref[j])
        results.append(own + dot(coupled, out_ref[:, at]))
    return results


def start_kernel(increment_hbm, mask_hbm, members_hbm, weight_hbm, out_ref,
                 increment_ref, mask_ref, members_ref, weight_ref, arrived):
    copies = [
        pltpu.make_async_copy(source, target, arrived.at[at])
        for at, (source, target) in enumerate((
            (increment_hbm, increment_ref), (mask_hbm, mask_ref),
            (members_hbm, members_ref), (weight_hbm, weight_ref)))
    ]
    for copy in copies:
        copy.start()
    for copy in copies:
        copy.wait()
    shares = out_ref.shape[0]

    def values(at):
        return (weight_ref[:, at] * mask_ref[0, :, at].astype(F32) * members_ref[0, 0, :, at].astype(F32)
                * increment_ref[0, :, at].astype(F32))

    for half in range(2):
        tail = values(slice((shares + half) * BLOCK, (shares + half + 1) * BLOCK))
        turned = jnp.concatenate([tail, tail], axis=0).T
        for s in range(8):
            out_ref[half * 8 + s, HALF:HALF + EXTRA, :] = turned[s * EXTRA:(s + 1) * EXTRA].astype(BF16)
    for s in range(shares):
        out_ref[s, 0:HALF, :] = values(slice(s * BLOCK, (s + 1) * BLOCK)).astype(BF16)


def column_kernel(nb, in_ref, pow_ref, kta_ref, ktf_ref, rb_ref, cb_ref, out_ref, lines):
    for j in range(nb):
        at = slice(j * BLOCK, (j + 1) * BLOCK)
        square = jnp.concatenate([in_ref[2 * j, 0:HALF, :], in_ref[2 * j + 1, 0:HALF, :]], axis=0)
        lines[0:BLOCK, at] = square.astype(F32).T.astype(BF16)
        lane = lax.broadcasted_iota(jnp.int32, (EXTRA, BLOCK), 1)
        tail = jnp.where(lane < HALF, in_ref[2 * j, HALF:HALF + EXTRA, :].astype(F32),
                         in_ref[2 * j + 1, HALF:HALF + EXTRA, :].astype(F32))
        lines[BLOCK:BLOCK + EXTRA, at] = tail.astype(BF16)
    for j, block in enumerate(run_steps(lines, nb, pow_ref, kta_ref, rb_ref, True)):
        lines[:, j * BLOCK:(j + 1) * BLOCK] = block.astype(BF16)
    for j, block in enumerate(run_steps(lines, nb, pow_ref, ktf_ref, cb_ref, False)):
        square = block[0:BLOCK].T.astype(BF16)
        tail = block[BLOCK:BLOCK + EXTRA].astype(BF16)
        for half in range(2):
            out_ref[2 * j + half, 0:HALF, :] = square[half * HALF:(half + 1) * HALF]
            out_ref[2 * j + half, HALF:HALF + EXTRA, :] = tail


def row_kernel(nb, parity_ref, in_ref, *refs):
    far, out_ref, near, lines, arrived = refs[:7], refs[7], refs[8:15], refs[15], refs[16]
    members_ref, weight_ref, pow_ref, kta_ref, ktf_ref, rb_ref, cb_ref = near
    copies = {id(near[at]): pltpu.make_async_copy(far[at], near[at], arrived.at[at]) for at in range(7)}
    for ref in (kta_ref, pow_ref, rb_ref, ktf_ref, cb_ref, members_ref, weight_ref):
        copies[id(ref)].start()

    def arrive(*wanted):
        for ref in wanted:
            if id(ref) in copies:
                copies.pop(id(ref)).wait()

    shares = in_ref.shape[0]
    for s in range(shares):
        lines[:, s * BLOCK:(s + 1) * BLOCK] = in_ref[s, 0:HALF, :]
    odd = parity_ref[0] == 1
    for half in range(2):
        tail = jnp.concatenate(
            [in_ref[half * 8 + s, HALF:HALF + EXTRA, :] for s in range(8)], axis=0).astype(F32).T
        tail = jnp.where(odd, tail[HALF:BLOCK], tail[0:HALF])
        at = (shares + half) * BLOCK
        lines[:, at:at + BLOCK] = tail.astype(BF16)
    for j, block in enumerate(run_steps(lines, nb, pow_ref, kta_ref, rb_ref, True, arrive)):
        lines[:, j * BLOCK:(j + 1) * BLOCK] = block.astype(BF16)
    takers, middle = out_ref.shape[0], nb // 2
    blocks = run_steps(lines, nb, pow_ref, ktf_ref, cb_ref, False, arrive)
    arrive(members_ref, weight_ref)
    for j in range(middle):
        left, right = slice(j * BLOCK, (j + 1) * BLOCK), slice((middle + j) * BLOCK, (middle + j + 1) * BLOCK)
        term_left = members_ref[0, 0, :, left].astype(F32) * weight_ref[:, left] * blocks[j]
        term_right = members_ref[0, 0, :, right].astype(F32) * weight_ref[:, right] * blocks[middle + j]
        for taker in range(takers):
            rows = slice(taker * 8, taker * 8 + 8)
            out_ref[taker, :, left] = jnp.concatenate([term_left[rows], term_right[rows]], axis=0).astype(BF16)


def sum_kernel(scale, in_ref, out_ref):
    total = in_ref[0].astype(F32)
    for source in range(1, in_ref.shape[0]):
        total += in_ref[source].astype(F32)
    if scale is not None:
        total = total / scale
    total = total.astype(BF16)
    for target in range(out_ref.shape[0]):
        out_ref[target] = total


def final_kernel(mask_ref, in_ref, out_ref):
    shares, _, width = in_ref.shape
    for pair in range(shares // 2):
        one, two = in_ref[2 * pair].astype(F32), in_ref[2 * pair + 1].astype(F32)
        rows = slice(pair * 16, pair * 16 + 16)
        left = jnp.concatenate([one[0:8], two[0:8]], axis=0)
        right = jnp.concatenate([one[8:16], two[8:16]], axis=0)
        out_ref[0, rows, 0:width] = (left * mask_ref[0, rows, 0:width].astype(F32)).astype(BF16)
        out_ref[0, rows, width:2 * width] = (right * mask_ref[0, rows, width:2 * width].astype(F32)).astype(BF16)


def call(kernel, out_shape, operands, scratch=(), spaces=(), limit=VMEM_LIMIT):
    spaces = tuple(spaces) + (pltpu.VMEM,) * (len(operands) - len(spaces))
    return pl.pallas_call(
        kernel,
        out_shape=jax.ShapeDtypeStruct(out_shape, BF16),
        in_specs=[pl.BlockSpec(memory_space=space) for space in spaces],
        out_specs=pl.BlockSpec(memory_space=pltpu.VMEM),
        scratch_shapes=list(scratch),
        compiler_params=pltpu.CompilerParams(vmem_limit_bytes=limit),
        cost_estimate=pl.CostEstimate(flops=1000000, bytes_accessed=2000000, transcendentals=0),
    )(*operands)


def landing(arrays):
    return [pltpu.VMEM(array.shape, array.dtype) for array in arrays], pltpu.SemaphoreType.DMA((len(arrays),))


def exchange(array, axis, groups=None):
    return lax.all_to_all(array, axis, split_axis=0, concat_axis=0, tiled=True, axis_index_groups=groups)


def local(increment, mask, members, weight, x_inverse, x_coupling, y_inverse, y_coupling):
    _, _, rows, columns = members.shape
    space, mem = lax.axis_size("space"), lax.axis_size("mem")
    x_blocks, y_blocks = x_inverse.shape[0], y_inverse.shape[0]
    close = 8
    apart = mem // close
    near_groups = [[z * close + i for i in range(close)] for z in range(apart)]
    far_groups = [[z * close + i for z in range(apart)] for i in range(close)]
    share = (HALF + EXTRA, BLOCK)

    y_tables = prepare(y_inverse, y_coupling, True, False)
    x_tables = prepare(x_inverse, x_coupling, True, True)

    inputs = (increment, mask, members, weight)
    near, arrived = landing(inputs)
    sent = call(start_kernel, (space,) + share, inputs,
                near + [arrived], [pltpu.HBM] * 4, WIDE_LIMIT)
    got = exchange(sent, "space")
    sent = call(functools.partial(column_kernel, y_blocks), (space,) + share, (got,) + tuple(y_tables),
                [pltpu.VMEM((BLOCK + EXTRA, y_blocks * BLOCK), BF16)])
    got = exchange(sent, "space")
    parity = (lax.axis_index("space") % 2).astype(jnp.int32)[None]
    packed = (16, columns // 2)
    inputs = (members, weight) + tuple(x_tables)
    near, arrived = landing(inputs)
    terms = call(functools.partial(row_kernel, x_blocks), (close,) + packed, (parity, got) + inputs,
                 near + [pltpu.VMEM((rows, columns), BF16), arrived],
                 [pltpu.SMEM, pltpu.VMEM] + [pltpu.HBM] * 7, WIDE_LIMIT)
    terms = exchange(terms, "mem", near_groups)
    terms = call(functools.partial(sum_kernel, None), (apart,) + packed, (terms,))
    terms = exchange(terms, "mem", far_groups)
    terms = call(functools.partial(sum_kernel, float(mem - 1)), (close,) + packed, (terms,))
    terms = exchange(terms, "mem", near_groups)
    return call(final_kernel, (1, rows, columns), (mask, terms))


def solution(mesh):
    placed = (
        P(None, "space", None),
        P(None, "space", None),
        P("mem", None, "space", None),
        P("space", None),
        P(),
        P(),
        P(),
        P(),
    )
    return jax.shard_map(
        local, mesh=mesh, in_specs=placed, out_specs=P(None, "space", None), check_vma=False
    )
```

time: 106 us -> 100 us (0.943)
  waiting for transfers between devices: 5.04 us -> 11.5 us
  Pallas kernels: 28.3 us -> 22.4 us
  local copies, waits for them, and re-layouts: 6.17 us -> 0.76 us
    pallas_call x2, Pallas kernels: 19.6 us -> 10.6 us  [prepare(): pl.pallas_call(functools.partial(prepare_far_kernel if far else prepare_k...]
    all_to_all x2, waiting for transfers between devices: 5.04 us -> 11.5 us  [exchange(): lax.all_to_all(array, axis, split_axis=0, concat_axis=0, tiled=True, axis...]
    unnamed x24 -> x8, local copies, waits for them, and re-layouts: 6.17 us -> 0.76 us
    pallas_call x6, Pallas kernels: 8.69 us -> 11.8 us  [call(): pl.pallas_call(kernel, out_shape=jax.ShapeDtypeStruct(out_shape, BF16), i...]
  transfers between devices with their start and end apart: 2 -> 2, of which waited for: 1 -> 2; matrix products, arithmetic and copies ran while one was open for 0% -> 0% of each run, Pallas kernels for 19% -> 11%
where the time goes in v2:
time: 100 us; the launch traced here: 99.5 us
  blocking collectives  52 us (52%)
  Pallas kernels  22.4 us (22%)
  starting transfers between devices  12.8 us (13%)
  waiting for transfers between devices  11.5 us (12%)
    all_to_all x3, blocking collectives, exchange(): lax.all_to_all(array, axis, split_axis=0, concat_axis=0, tiled=True, axis...  52 us
    all_to_all x2, starting transfers between devices, exchange(): lax.all_to_all(array, axis, split_axis=0, concat_axis=0, tiled=True, axis...  12.8 us
    pallas_call x6, Pallas kernels, call(): pl.pallas_call(kernel, out_shape=jax.ShapeDtypeStruct(out_shape, BF16), i...  11.8 us
    all_to_all x2, waiting for transfers between devices, exchange(): lax.all_to_all(array, axis, split_axis=0, concat_axis=0, tiled=True, axis...  11.5 us
    pallas_call x2, Pallas kernels, prepare(): pl.pallas_call(functools.partial(prepare_far_kernel if far else prepare_k...  10.6 us
  transfers between devices with their start and end apart: 2, of which 2 were waited for; matrix products, arithmetic and copies ran while one was open for 0% of the time, Pallas kernels for 11%

profile of v2, /device:TPU:1, one launch (start us, length us, event | category | flops | bytes accessed | tf_op | source)
XLA Modules:
  0.0 99.5 jit_solution(5983882835859267845)
XLA Ops:
  0.0 0.0 copy-start.2
  0.0 0.0 copy-start.1
  0.0 2.4 %shard_map.82 = bf16[16,80,128]{2,1,0:T(8,128)(2,1)} custom-call(bf16[1,64,2304]{2,1,0:T(8,128)(2,1)} %increment_hbm.1, s32[1,64,2304]{2,1,0:T(8,128)} %mask_ref.1, bf16[1,1,64,2304]{3,2,1,0:T(8,128)(2,1)} %refs_0_.1, f32[64,2304]{1,0:T(8,128)} %refs_1_.1), custom_call_target="tpu_custom_call" | custom-call | flops 1000000 | bytes 2000000 | tf_op jit(solution)/shard_map/pallas_call | solution.py:348
  2.4 9.2 %all-to-all-start = ((bf16[16,80,128]{2,1,0:T(8,128)(2,1)}), bf16[16,80,128]{2,1,0:T(8,128)(2,1)S(1)}, u32[]{:S(2)}, u32[]{:S(2)}) async-start(bf16[16,80,128]{2,1,0:T(8,128)(2,1)} %shard_map.82), calls=%async_computation | async-start | bytes 655360 | tf_op jit(solution)/shard_map/all_to_all | solution.py:364
  11.6 0.0 copy-done.2
  11.6 0.0 copy-done.1
  11.6 3.0 %shard_map.83 = (bf16[8,128,128]{2,1,0:T(8,128)(2,1)S(1)}, bf16[128,1024]{1,0:T(8,128)(2,1)S(1)}, bf16[128,1024]{1,0:T(8,128)(2,1)S(1)}, bf16[128,1024]{1,0:T(8,128)(2,1)S(1)}, bf16[128,1024]{1,0:T(8,128)(2,1)S(1)}) custom-call(f32[7]{0:T(128)S(1)} %copy-done.2, bf16[8,128,128]{2,1,0:T(8,128)(2,1)S(1)} %copy-done.1), custom_call_target="tpu_custom_call" | custom-call | flops 671088640 | bytes 1310720 | tf_op jit(solution)/shard_map/pallas_call | solution.py:208
  14.6 8.2 %all-to-all-done.in_ref = bf16[16,80,128]{2,1,0:T(8,128)(2,1)S(1)} async-done(((bf16[16,80,128]{2,1,0:T(8,128)(2,1)}), bf16[16,80,128]{2,1,0:T(8,128)(2,1)S(1)}, u32[]{:S(2)}, u32[]{:S(2)}) %all-to-all-start) | async-done | bytes 327712 | tf_op jit(solution)/shard_map/all_to_all | solution.py:364
  22.9 2.3 %shard_map.84 = bf16[16,80,128]{2,1,0:T(8,128)(2,1)} custom-call(bf16[16,80,128]{2,1,0:T(8,128)(2,1)S(1)} %all-to-all-done.in_ref, bf16[8,128,128]{2,1,0:T(8,128)(2,1)S(1)} %get-tuple-element.15.pow_ref, bf16[128,1024]{1,0:T(8,128)(2,1)S(1)} %get-tuple-element.16.kta_ref, bf16[128,1024]{1,0:T(8,128)(2,1)S(1)} %get-tuple-element.17.ktf_ref, ...), custom_call_target="tpu_custom_call" | custom-call | flops 1000000 | bytes 2000000 | tf_op jit(solution)/shard_map/pallas_call | solution.py:348
  25.2 3.6 %all-to-all-start.1 = ((bf16[16,80,128]{2,1,0:T(8,128)(2,1)}), bf16[16,80,128]{2,1,0:T(8,128)(2,1)S(1)}, u32[]{:S(2)}, u32[]{:S(2)}) async-start(bf16[16,80,128]{2,1,0:T(8,128)(2,1)} %shard_map.84), calls=%async_computation.1 | async-start | bytes 655360 | tf_op jit(solution)/shard_map/all_to_all | solution.py:364
  28.7 7.5 %shard_map.85 = (bf16[18,128,128]{2,1,0:T(8,128)(2,1)}, bf16[256,2304]{1,0:T(8,128)(2,1)}, bf16[256,2304]{1,0:T(8,128)(2,1)}, bf16[256,2304]{1,0:T(8,128)(2,1)}, bf16[256,2304]{1,0:T(8,128)(2,1)}) custom-call(f32[17]{0:T(128)} %c_ref.3, bf16[18,128,128]{2,1,0:T(8,128)(2,1)} %g_ref.3), custom_call_target="tpu_custom_call" | custom-call | flops 1509949440 | bytes 5898240 | tf_op jit(solution)/shard_map/pallas_call | solution.py:208
  36.3 3.3 %all-to-all-done.1.in_ref = bf16[16,80,128]{2,1,0:T(8,128)(2,1)S(1)} async-done(((bf16[16,80,128]{2,1,0:T(8,128)(2,1)}), bf16[16,80,128]{2,1,0:T(8,128)(2,1)S(1)}, u32[]{:S(2)}, u32[]{:S(2)}) %all-to-all-start.1) | async-done | bytes 327712 | tf_op jit(solution)/shard_map/all_to_all | solution.py:364
  39.6 0.0 copy-start.3
  39.6 0.7 copy-done.3
  40.3 6.3 %shard_map.86 = bf16[8,16,1152]{2,1,0:T(8,128)(2,1)} custom-call(s32[1]{0:T(128)} %bitcast.parity_ref, bf16[16,80,128]{2,1,0:T(8,128)(2,1)} %copy-done.3, bf16[1,1,64,2304]{3,2,1,0:T(8,128)(2,1)} %refs_0_.1, f32[64,2304]{1,0:T(8,128)} %refs_1_.1, bf16[18,128,128]{2,1,0:T(8,128)(2,1)} %get-tuple-element.20.refs_2_, ...), custom_call_target="tpu_custom_call" | custom-call | flops 1000000 | bytes 2000000 | tf_op jit(solution)/shard_map/pallas_call | solution.py:348
  46.6 0.0 copy-start
  46.6 14.2 %all_to_all.25.in_ref = bf16[8,16,1152]{2,1,0:T(8,128)(2,1)S(1)} all-to-all(bf16[8,16,1152]{2,1,0:T(8,128)(2,1)} %shard_map.86), channel_id=1, replica_groups={{0,1,2,3,4,5,6,7},{8,9,10,11,12,13,14,15},{16,17,18,19,20,21,22,23},{24..., dimensions={0} | all-to-all | bytes 589824 | tf_op jit(solution)/shard_map/all_to_all | solution.py:364
  60.9 24.5 %all_to_all.26.in_ref = bf16[4,16,1152]{2,1,0:T(8,128)(2,1)S(1)} all-to-all(bf16[4,16,1152]{2,1,0:T(8,128)(2,1)S(1)} %shard_map.87), channel_id=1, replica_groups={{0,8,16,24},{1,9,17,25},{2,10,18,26},{3,11,19,27},{4,12,20,28},{5,13,21..., dimensions={0} | all-to-all | bytes 294912 | tf_op jit(solution)/shard_map/all_to_all | solution.py:364
  85.5 13.2 %all_to_all.27.in_ref = bf16[8,16,1152]{2,1,0:T(8,128)(2,1)S(1)} all-to-all(bf16[8,16,1152]{2,1,0:T(8,128)(2,1)S(1)} %shard_map.88), channel_id=1, replica_groups={{0,1,2,3,4,5,6,7},{8,9,10,11,12,13,14,15},{16,17,18,19,20,21,22,23},{24..., dimensions={0} | all-to-all | bytes 589824 | tf_op jit(solution)/shard_map/all_to_all | solution.py:364
  98.7 0.0 copy-done
  98.7 0.8 shard_map.89
  (2 shorter events, 0.1 us)
Async XLA Ops:
  0.0 11.6 %copy-start.2 = (f32[7]{0:T(128)S(1)}, f32[7]{0:T(128)}, u32[]{:S(2)}) copy-start(f32[7]{0:T(128)} %c_ref.2) | copy-start | bytes 88
  0.0 11.6 %copy-start.1 = (bf16[8,128,128]{2,1,0:T(8,128)(2,1)S(1)}, bf16[8,128,128]{2,1,0:T(8,128)(2,1)}, u32[]{:S(2)}) copy-start(bf16[8,128,128]{2,1,0:T(8,128)(2,1)} %g_ref.2) | copy-start | bytes 786436
  2.4 20.5 %all-to-all-start = ((bf16[16,80,128]{2,1,0:T(8,128)(2,1)}), bf16[16,80,128]{2,1,0:T(8,128)(2,1)S(1)}, u32[]{:S(2)}, u32[]{:S(2)}) async-start(bf16[16,80,128]{2,1,0:T(8,128)(2,1)} %shard_map.82), calls=%async_computation | async-start | bytes 655360 | tf_op jit(solution)/shard_map/all_to_all | solution.py:364
  25.2 14.4 %all-to-all-start.1 = ((bf16[16,80,128]{2,1,0:T(8,128)(2,1)}), bf16[16,80,128]{2,1,0:T(8,128)(2,1)S(1)}, u32[]{:S(2)}, u32[]{:S(2)}) async-start(bf16[16,80,128]{2,1,0:T(8,128)(2,1)} %shard_map.84), calls=%async_computation.1 | async-start | bytes 655360 | tf_op jit(solution)/shard_map/all_to_all | solution.py:364
  39.6 0.7 copy-start.3
  46.6 52.0 %copy-start = (s32[1,64,2304]{2,1,0:T(8,128)S(1)}, s32[1,64,2304]{2,1,0:T(8,128)}, u32[]{:S(2)}) copy-start(s32[1,64,2304]{2,1,0:T(8,128)} %mask_ref.1) | copy-start | bytes 1769476

commit v3 on v2

--- a/solution.py
+++ b/solution.py
@@ -15,6 +15,7 @@
 EXTRA = 16
 F32 = jnp.float32
 BF16 = jnp.bfloat16
+GROUP = BLOCK // (2 * NSTEP)
 VMEM_LIMIT = 24 * 2**20
 WIDE_LIMIT = 60 * 2**20
 
@@ -31,33 +32,25 @@
     return (value + unit - 1) // unit * unit
 
 
-def coupling_rows(nb, depth):
-    return round_up(2 * NSTEP * nb, depth)
-
-
-def prepare_kernel(nb, precise, c_ref, g_ref, *refs):
-    fill_tables(nb, precise, c_ref, g_ref, *refs, lambda at: None)
-
-
-def prepare_far_kernel(nb, precise, c_ref, g_ref, *refs):
-    far, near, (left, *scratch) = refs[:5], refs[5:10], refs[10:]
-    copies = [pltpu.make_async_copy(near[at], far[at], left.at[at]) for at in range(5)]
-    fill_tables(nb, precise, c_ref, g_ref, *near, *scratch, lambda at: copies[at].start())
-    for copy in copies:
-        copy.wait()
-
-
-def fill_tables(nb, precise, c_ref, g_ref, pow_ref, kta_ref, ktf_ref, rb_ref, cb_ref,
-                   edges, big_rows, big_columns, rmat, qmat, ct,
-                   high2, low2, high3, low3, high4, low4, few_rows, few_columns, ready):
+def groups_of(nb):
+    return (nb + GROUP - 1) // GROUP
+
+
+def place(j):
+    return j // GROUP * BLOCK + j % GROUP * 2 * NSTEP
+
+
+def prepare_kernel(nb, c_ref, g_ref, pow_ref, map_a_ref, map_f_ref, rows_ref, columns_ref, turned_ref,
+                   edges, rows, columns, rmat, qmat, ct, high2, low2, high3, low3, high4, low4,
+                   few_rows, few_columns):
     pad = round_up(nb, 8)
-    kp = kta_ref.shape[0]
+    kp = map_a_ref.shape[0]
     lane = lax.broadcasted_iota(jnp.int32, (16, BLOCK), 1)
     row = lax.broadcasted_iota(jnp.int32, (16, BLOCK), 0)
     select = jnp.where((row < 2) & (lane == row * LAST), 1.0, 0.0)
     edges[...] = jnp.zeros_like(edges)
-    big_rows[...] = jnp.zeros_like(big_rows)
-    big_columns[...] = jnp.zeros_like(big_columns)
+    rows[...] = jnp.zeros_like(rows)
+    columns[...] = jnp.zeros_like(columns)
 
     def stack(first, *pairs):
         out = first
@@ -70,16 +63,16 @@
         return high, (full - high.astype(F32)).astype(BF16)
 
     def put_row(j, k, top, bottom):
-        at = slice(j * BLOCK, (j + 1) * BLOCK)
-        big_rows[(2 * k - 2) * nb + j:(2 * k - 2) * nb + j + 1, at] = bottom
-        big_rows[(2 * k - 1) * nb + j:(2 * k - 1) * nb + j + 1, at] = top
+        at = place(j) + 2 * k - 2
+        rows[at:at + 1, :] = bottom
+        rows[at + 1:at + 2, :] = top
         edges[k - 1, 0, j:j + 1, :] = top
         edges[k - 1, 1, j:j + 1, :] = bottom
 
     def put_column(j, k, left, right):
-        at = slice(j * BLOCK, (j + 1) * BLOCK)
-        big_columns[(2 * k - 2) * nb + j:(2 * k - 2) * nb + j + 1, at] = right
-        big_columns[(2 * k - 1) * nb + j:(2 * k - 1) * nb + j + 1, at] = left
+        at = place(j) + 2 * k - 2
+        columns[at:at + 1, :] = right
+        columns[at + 1:at + 2, :] = left
 
     def ends(full):
         return full[0:1], full[LAST:BLOCK]
@@ -95,51 +88,40 @@
         put_row(j, 1, *ends(g_full))
         put_row(j, 2, *ends(second))
         few_rows[j] = stack(jnp.zeros((16, BLOCK), F32), ends(g_full), ends(second))
-        columns = dot_nt(select.astype(BF16), g)
-        put_column(j, 1, *pair(columns, 0))
-        few_columns[j] = stack(select, pair(columns, 0)).astype(F32)
+        found = dot_nt(select.astype(BF16), g)
+        put_column(j, 1, *pair(found, 0))
+        few_columns[j] = stack(select, pair(found, 0)).astype(F32)
 
     for j in range(nb):
         both = jnp.concatenate([g_ref[j], high2[j]], axis=0)
-        if precise:
-            result = dot(jnp.concatenate([both, both], axis=1),
-                         jnp.concatenate([high2[j], low2[j]], axis=0))
-            third, fourth = result[0:BLOCK], result[BLOCK:2 * BLOCK] + dot(low2[j], high2[j])
-        else:
-            result = dot(both, high2[j])
-            third, fourth = result[0:BLOCK], result[BLOCK:2 * BLOCK]
+        result = dot(jnp.concatenate([both, both], axis=1), jnp.concatenate([high2[j], low2[j]], axis=0))
+        third, fourth = result[0:BLOCK], result[BLOCK:2 * BLOCK] + dot(low2[j], high2[j])
         high3[j], low3[j] = split(third)
         high4[j], low4[j] = split(fourth)
         put_row(j, 3, *ends(third))
         put_row(j, 4, *ends(fourth))
         old = few_columns[j]
-        columns = dot_nt(old.astype(BF16), high2[j])
-        put_column(j, 2, *pair(columns, 0))
-        put_column(j, 3, *pair(columns, 2))
-        few_columns[j] = stack(old, pair(old, 2), pair(columns, 0), pair(columns, 2)).astype(F32)
+        found = dot_nt(old.astype(BF16), high2[j])
+        put_column(j, 2, *pair(found, 0))
+        put_column(j, 3, *pair(found, 2))
+        few_columns[j] = stack(old, pair(old, 2), pair(found, 0), pair(found, 2)).astype(F32)
 
     for j in range(nb):
         left = jnp.concatenate([high3[j], few_rows[j]], axis=0)
-        if precise:
-            result = dot(jnp.concatenate([left, left], axis=1),
-                         jnp.concatenate([high4[j], low4[j]], axis=0))
-            seventh = result[0:BLOCK] + dot(low3[j], high4[j])
-        else:
-            result = dot(left, high4[j])
-            seventh = result[0:BLOCK]
+        result = dot(jnp.concatenate([left, left], axis=1), jnp.concatenate([high4[j], low4[j]], axis=0))
+        seventh = result[0:BLOCK] + dot(low3[j], high4[j])
         pow_ref[j] = seventh.astype(BF16)
         put_row(j, 5, *pair(result, BLOCK + 2))
         put_row(j, 6, *pair(result, BLOCK + 4))
         put_row(j, 7, *ends(seventh))
-        columns = dot_nt(few_columns[j].astype(BF16), high4[j])
+        found = dot_nt(few_columns[j].astype(BF16), high4[j])
         for k in range(4):
-            put_column(j, 4 + k, *pair(columns, 2 * k))
-
-    ready(0)
-    rb_ref[...] = big_rows[...].astype(BF16)
-    ready(3)
-    cb_ref[...] = big_columns[...].astype(BF16)
-    ready(4)
+            put_column(j, 4 + k, *pair(found, 2 * k))
+
+    rows_ref[...] = rows[...].astype(BF16)
+    columns_ref[...] = columns[...].astype(BF16)
+    for group in range(groups_of(nb)):
+        turned_ref[group] = columns[group * BLOCK:(group + 1) * BLOCK, :].T.astype(BF16)
 
     def corner(run, k, a, b):
         if run == 1:
@@ -169,14 +151,15 @@
             rmat[run, pad + j:pad + j + 1, :] = t_row[run]
 
     block = lax.broadcasted_iota(jnp.int32, (pad, kp), 0)
-    lanes = lax.broadcasted_iota(jnp.int32, (pad, kp), 1)
+    first = block * (2 * NSTEP)
+    for group in range(1, groups_of(nb)):
+        first += jnp.where(block >= group * GROUP, BLOCK - GROUP * 2 * NSTEP, 0)
+    first = lax.broadcasted_iota(jnp.int32, (pad, kp), 1) - first
     sources, trailing = [[], []], [[], []]
     for k in range(NSTEP):
-        at = 2 * k * nb
-        place = (NSTEP - 1 - k) * 2 * nb
         for run in runs:
-            q_last = jnp.where((block < nb) & (lanes == at + block), 1.0, 0.0)
-            q_first = jnp.where((block < nb) & (lanes == at + nb + block), 1.0, 0.0)
+            q_last = jnp.where((block < nb) & (first == 2 * k), 1.0, 0.0)
+            q_first = jnp.where((block < nb) & (first == 2 * k + 1), 1.0, 0.0)
             for m in range(k):
                 s_old, t_old = sources[run][m], trailing[run][m]
                 q_last += corner(run, k - m + 1, 0, 1) * s_old + corner(run, k - m + 1, 1, 1) * t_old
@@ -188,32 +171,28 @@
                                   precision=lax.Precision.HIGHEST, preferred_element_type=F32)
             sources[run].append(now[0:pad])
             trailing[run].append(now[pad:2 * pad])
-            ct[run, place:place + nb, :] = now[pad:pad + nb]
-            ct[run, place + nb:place + 2 * nb, :] = now[0:nb]
-    kta_ref[...] = dot(ct[0].astype(BF16), cb_ref[...]).astype(BF16)
-    ready(1)
-    ktf_ref[...] = dot(ct[1].astype(BF16), rb_ref[...]).astype(BF16)
-    ready(2)
-
-
-def prepare(inverse, coupling, precise, far):
+            for j in range(nb):
+                at = place(j) + (NSTEP - 1 - k) * 2
+                ct[run, at:at + 1, :] = now[pad + j:pad + j + 1]
+                ct[run, at + 1:at + 2, :] = now[j:j + 1]
+    map_a_ref[...] = ct[0].astype(BF16)
+    map_f_ref[...] = ct[1].astype(BF16)
+
+
+def prepare(inverse, coupling):
     nb = inverse.shape[0]
-    width = nb * BLOCK
-    kp = coupling_rows(nb, BLOCK)
-    pad = round_up(nb, 8)
+    kp, pad = groups_of(nb) * BLOCK, round_up(nb, 8)
     vmem = pl.BlockSpec(memory_space=pltpu.VMEM)
-    table = jax.ShapeDtypeStruct((kp, width), BF16)
-    tables = (jax.ShapeDtypeStruct((nb, BLOCK, BLOCK), BF16), table, table, table, table)
-    staging = [pltpu.VMEM(array.shape, array.dtype) for array in tables] + [pltpu.SemaphoreType.DMA((5,))]
+    shapes = [(nb, BLOCK, BLOCK), (kp, kp), (kp, kp), (kp, BLOCK), (kp, BLOCK), (groups_of(nb), BLOCK, BLOCK)]
     return pl.pallas_call(
-        functools.partial(prepare_far_kernel if far else prepare_kernel, nb, precise),
-        out_shape=tables,
+        functools.partial(prepare_kernel, nb),
+        out_shape=tuple(jax.ShapeDtypeStruct(shape, BF16) for shape in shapes),
         in_specs=[pl.BlockSpec(memory_space=pltpu.SMEM), vmem],
-        out_specs=(pl.BlockSpec(memory_space=pltpu.HBM) if far else vmem,) * 5,
-        scratch_shapes=(staging if far else []) + [
+        out_specs=(vmem,) * len(shapes),
+        scratch_shapes=[
             pltpu.VMEM((NSTEP, 2, pad, BLOCK), F32),
-            pltpu.VMEM((kp, width), F32),
-            pltpu.VMEM((kp, width), F32),
+            pltpu.VMEM((kp, BLOCK), F32),
+            pltpu.VMEM((kp, BLOCK), F32),
             pltpu.VMEM((2, 2 * pad, BLOCK), F32),
             pltpu.VMEM((2, BLOCK, kp), F32),
             pltpu.VMEM((2, kp, kp), F32),
@@ -221,22 +200,42 @@
             pltpu.VMEM((nb, 16, BLOCK), BF16),
             pltpu.VMEM((nb, 16, BLOCK), F32),
         ],
-        compiler_params=pltpu.CompilerParams(vmem_limit_bytes=WIDE_LIMIT if far else VMEM_LIMIT),
+        compiler_params=pltpu.CompilerParams(vmem_limit_bytes=VMEM_LIMIT),
         cost_estimate=pl.CostEstimate(
-            flops=nb * 20 * 2 * BLOCK**3, bytes_accessed=10 * kp * width, transcendentals=0),
+            flops=nb * 400 * BLOCK**3, bytes_accessed=4000000, transcendentals=0),
     )(coupling, inverse)
 
 
-def run_steps(lines, nb, pow_ref, kt_ref, out_ref, adjoint, arrive=lambda *refs: None):
-    arrive(kt_ref)
-    coupled = dot_nt(lines[...], kt_ref[...]).astype(BF16)
-    arrive(pow_ref, out_ref)
+def run_steps(lines, nb, pow_ref, map_ref, in_ref, out_ref, adjoint):
+    count = lines.shape[0]
+    lane = lax.broadcasted_iota(jnp.int32, (count, BLOCK), 1)
+    owned = [(lane >= at * 2 * NSTEP) & (lane < (at + 1) * 2 * NSTEP) for at in range(min(nb, GROUP))]
+    blocks = [slice(j * BLOCK, (j + 1) * BLOCK) for j in range(nb)]
+    products = []
+    for group in range(groups_of(nb)):
+        edge = in_ref[group * BLOCK:(group + 1) * BLOCK, :]
+        kept = jnp.zeros((count, BLOCK), F32)
+        for j in range(group * GROUP, min(nb, (group + 1) * GROUP)):
+            kept = jnp.where(owned[j % GROUP], dot_nt(lines[:, blocks[j]], edge), kept)
+        products.append(kept.astype(BF16))
+    coupled = dot_nt(jnp.concatenate(products, axis=1), map_ref[...])
     results = []
     for j in range(nb):
-        at = slice(j * BLOCK, (j + 1) * BLOCK)
-        own = (dot if adjoint else dot_nt)(lines[:, at], pow_ref[j])
-        results.append(own + dot(coupled, out_ref[:, at]))
+        group = j // GROUP
+        mine = jnp.where(owned[j % GROUP], coupled[:, group * BLOCK:(group + 1) * BLOCK], 0.0).astype(BF16)
+        left = jnp.concatenate([lines[:, blocks[j]], mine], axis=1)
+        if adjoint:
+            edge = out_ref[group * BLOCK:(group + 1) * BLOCK, :]
+            results.append(dot(left, jnp.concatenate([pow_ref[j], edge], axis=0)))
+        else:
+            results.append(dot_nt(left, jnp.concatenate([pow_ref[j], out_ref[group]], axis=1)))
     return results
+
+
+def run_both(lines, nb, pow_ref, map_a_ref, map_f_ref, rows_ref, columns_ref, turned_ref):
+    for j, block in enumerate(run_steps(lines, nb, pow_ref, map_a_ref, columns_ref, rows_ref, True)):
+        lines[:, j * BLOCK:(j + 1) * BLOCK] = block.astype(BF16)
+    return run_steps(lines, nb, pow_ref, map_f_ref, rows_ref, turned_ref, False)
 
 
 def start_kernel(increment_hbm, mask_hbm, members_hbm, weight_hbm, out_ref,
@@ -266,7 +265,8 @@
         out_ref[s, 0:HALF, :] = values(slice(s * BLOCK, (s + 1) * BLOCK)).astype(BF16)
 
 
-def column_kernel(nb, in_ref, pow_ref, kta_ref, ktf_ref, rb_ref, cb_ref, out_ref, lines):
+def column_kernel(nb, in_ref, *refs):
+    *tables, out_ref, lines = refs
     for j in range(nb):
         at = slice(j * BLOCK, (j + 1) * BLOCK)
         square = jnp.concatenate([in_ref[2 * j, 0:HALF, :], in_ref[2 * j + 1, 0:HALF, :]], axis=0)
@@ -275,9 +275,7 @@
         tail = jnp.where(lane < HALF, in_ref[2 * j, HALF:HALF + EXTRA, :].astype(F32),
                          in_ref[2 * j + 1, HALF:HALF + EXTRA, :].astype(F32))
         lines[BLOCK:BLOCK + EXTRA, at] = tail.astype(BF16)
-    for j, block in enumerate(run_steps(lines, nb, pow_ref, kta_ref, rb_ref, True)):
-        lines[:, j * BLOCK:(j + 1) * BLOCK] = block.astype(BF16)
-    for j, block in enumerate(run_steps(lines, nb, pow_ref, ktf_ref, cb_ref, False)):
+    for j, block in enumerate(run_both(lines, nb, *tables)):
         square = block[0:BLOCK].T.astype(BF16)
         tail = block[BLOCK:BLOCK + EXTRA].astype(BF16)
         for half in range(2):
@@ -286,17 +284,11 @@
 
 
 def row_kernel(nb, parity_ref, in_ref, *refs):
-    far, out_ref, near, lines, arrived = refs[:7], refs[7], refs[8:15], refs[15], refs[16]
-    members_ref, weight_ref, pow_ref, kta_ref, ktf_ref, rb_ref, cb_ref = near
-    copies = {id(near[at]): pltpu.make_async_copy(far[at], near[at], arrived.at[at]) for at in range(7)}
-    for ref in (kta_ref, pow_ref, rb_ref, ktf_ref, cb_ref, members_ref, weight_ref):
-        copies[id(ref)].start()
-
-    def arrive(*wanted):
-        for ref in wanted:
-            if id(ref) in copies:
-                copies.pop(id(ref)).wait()
-
+    members_hbm, weight_hbm, *tables, out_ref, members_ref, weight_ref, lines, arrived = refs
+    copies = [pltpu.make_async_copy(members_hbm, members_ref, arrived.at[0]),
+              pltpu.make_async_copy(weight_hbm, weight_ref, arrived.at[1])]
+    for copy in copies:
+        copy.start()
     shares = in_ref.shape[0]
     for s in range(shares):
         lines[:, s * BLOCK:(s + 1) * BLOCK] = in_ref[s, 0:HALF, :]
@@ -307,11 +299,10 @@
         tail = jnp.where(odd, tail[HALF:BLOCK], tail[0:HALF])
         at = (shares + half) * BLOCK
         lines[:, at:at + BLOCK] = tail.astype(BF16)
-    for j, block in enumerate(run_steps(lines, nb, pow_ref, kta_ref, rb_ref, True, arrive)):
-        lines[:, j * BLOCK:(j + 1) * BLOCK] = block.astype(BF16)
     takers, middle = out_ref.shape[0], nb // 2
-    blocks = run_steps(lines, nb, pow_ref, ktf_ref, cb_ref, False, arrive)
-    arrive(members_ref, weight_ref)
+    blocks = run_both(lines, nb, *tables)
+    for copy in copies:
+        copy.wait()
     for j in range(middle):
         left, right = slice(j * BLOCK, (j + 1) * BLOCK), slice((middle + j) * BLOCK, (middle + j + 1) * BLOCK)
         term_left = members_ref[0, 0, :, left].astype(F32) * weight_ref[:, left] * blocks[j]
@@ -374,8 +365,8 @@
     far_groups = [[z * close + i for z in range(apart)] for i in range(close)]
     share = (HALF + EXTRA, BLOCK)
 
-    y_tables = prepare(y_inverse, y_coupling, True, False)
-    x_tables = prepare(x_inverse, x_coupling, True, True)
+    y_tables = prepare(y_inverse, y_coupling)
+    x_tables = prepare(x_inverse, x_coupling)
 
     inputs = (increment, mask, members, weight)
     near, arrived = landing(inputs)
@@ -387,11 +378,12 @@
     got = exchange(sent, "space")
     parity = (lax.axis_index("space") % 2).astype(jnp.int32)[None]
     packed = (16, columns // 2)
-    inputs = (members, weight) + tuple(x_tables)
+    inputs = (members, weight)
     near, arrived = landing(inputs)
-    terms = call(functools.partial(row_kernel, x_blocks), (close,) + packed, (parity, got) + inputs,
+    terms = call(functools.partial(row_kernel, x_blocks), (close,) + packed,
+                 (parity, got) + inputs + tuple(x_tables),
                  near + [pltpu.VMEM((rows, columns), BF16), arrived],
-                 [pltpu.SMEM, pltpu.VMEM] + [pltpu.HBM] * 7, WIDE_LIMIT)
+                 [pltpu.SMEM, pltpu.VMEM, pltpu.HBM, pltpu.HBM], WIDE_LIMIT)
     terms = exchange(terms, "mem", near_groups)
     terms = call(functools.partial(sum_kernel, None), (apart,) + packed, (terms,))
     terms = exchange(terms, "mem", far_groups)

time: 100 us -> 97.7 us (0.977)
  Pallas kernels: 22.4 us -> 16.4 us
  local copies, waits for them, and re-layouts: 0.76 us -> 5.35 us
  waiting for transfers between devices: 11.5 us -> 10.3 us
    unnamed x8 -> x24, local copies, waits for them, and re-layouts: 0.76 us -> 5.35 us
    pallas_call x2, Pallas kernels: 10.6 us -> 7.14 us  [prepare(): pl.pallas_call(functools.partial(prepare_kernel, nb), out_shape=tuple((ja...]
    pallas_call x6, Pallas kernels: 11.8 us -> 9.28 us  [call(): pl.pallas_call(kernel, out_shape=jax.ShapeDtypeStruct(out_shape, BF16), i...]
    all_to_all x2, waiting for transfers between devices: 11.5 us -> 10.3 us  [exchange(): lax.all_to_all(array, axis, split_axis=0, concat_axis=0, tiled=True, axis...]
  transfers between devices with their start and end apart: 2 -> 2, of which waited for: 2 -> 2; matrix products, arithmetic and copies ran while one was open for 0% -> 0% of each run, Pallas kernels for 11% -> 7%
where the time goes in v3:
time: 97.7 us; the launch traced here: 97.2 us
  blocking collectives  52 us (53%)
  Pallas kernels  16.4 us (17%)
  starting transfers between devices  13 us (13%)
  waiting for transfers between devices  10.3 us (11%)
  local copies, waits for them, and re-layouts  5.35 us (5%)
    all_to_all x3, blocking collectives, exchange(): lax.all_to_all(array, axis, split_axis=0, concat_axis=0, tiled=True, axis...  52 us
    all_to_all x2, starting transfers between devices, exchange(): lax.all_to_all(array, axis, split_axis=0, concat_axis=0, tiled=True, axis...  13 us
    all_to_all x2, waiting for transfers between devices, exchange(): lax.all_to_all(array, axis, split_axis=0, concat_axis=0, tiled=True, axis...  10.3 us
    pallas_call x6, Pallas kernels, call(): pl.pallas_call(kernel, out_shape=jax.ShapeDtypeStruct(out_shape, BF16), i...  9.28 us
    pallas_call x2, Pallas kernels, prepare(): pl.pallas_call(functools.partial(prepare_kernel, nb), out_shape=tuple((ja...  7.14 us
    unnamed x24, local copies, waits for them, and re-layouts  5.35 us
  transfers between devices with their start and end apart: 2, of which 2 were waited for; matrix products, arithmetic and copies ran while one was open for 0% of the time, Pallas kernels for 7%

profile of v3, /device:TPU:1, one launch (start us, length us, event | category | flops | bytes accessed | tf_op | source)
XLA Modules:
  0.0 97.2 jit_solution(2972319951033836726)
XLA Ops:
  0.0 2.3 %shard_map.82 = bf16[16,80,128]{2,1,0:T(8,128)(2,1)} custom-call(bf16[1,64,2304]{2,1,0:T(8,128)(2,1)} %increment_hbm.1, s32[1,64,2304]{2,1,0:T(8,128)} %mask_ref.1, bf16[1,1,64,2304]{3,2,1,0:T(8,128)(2,1)} %refs_0_.1, f32[64,2304]{1,0:T(8,128)} %refs_1_.1), custom_call_target="tpu_custom_call" | custom-call | flops 1000000 | bytes 2000000 | tf_op jit(solution)/shard_map/pallas_call | solution.py:339
  2.3 0.0 copy-start.8
  2.3 9.3 %all-to-all-start = ((bf16[16,80,128]{2,1,0:T(8,128)(2,1)}), bf16[16,80,128]{2,1,0:T(8,128)(2,1)S(1)}, u32[]{:S(2)}, u32[]{:S(2)}) async-start(bf16[16,80,128]{2,1,0:T(8,128)(2,1)} %shard_map.82), calls=%async_computation | async-start | bytes 655360 | tf_op jit(solution)/shard_map/all_to_all | solution.py:355
  11.7 0.0 copy-start.9
  11.7 0.6 copy-done.9
  12.3 2.6 %shard_map.83 = (bf16[8,128,128]{2,1,0:T(8,128)(2,1)S(1)}, bf16[128,128]{1,0:T(8,128)(2,1)S(1)}, bf16[128,128]{1,0:T(8,128)(2,1)S(1)}, bf16[128,128]{1,0:T(8,128...) custom-call(f32[7]{0:T(128)S(1)} %copy-done.9, bf16[8,128,128]{2,1,0:T(8,128)(2,1)S(1)} %copy-done.8), custom_call_target="tpu_custom_call" | custom-call | flops 6710886400 | bytes 4000000 | tf_op jit(solution)/shard_map/pallas_call | solution.py:187
  15.0 8.0 %all-to-all-done.in_ref = bf16[16,80,128]{2,1,0:T(8,128)(2,1)S(1)} async-done(((bf16[16,80,128]{2,1,0:T(8,128)(2,1)}), bf16[16,80,128]{2,1,0:T(8,128)(2,1)S(1)}, u32[]{:S(2)}, u32[]{:S(2)}) %all-to-all-start) | async-done | bytes 327712 | tf_op jit(solution)/shard_map/all_to_all | solution.py:355
  23.0 2.1 %shard_map.84 = bf16[16,80,128]{2,1,0:T(8,128)(2,1)} custom-call(bf16[16,80,128]{2,1,0:T(8,128)(2,1)S(1)} %all-to-all-done.in_ref, bf16[8,128,128]{2,1,0:T(8,128)(2,1)S(1)} %get-tuple-element.17.refs_0_, bf16[128,128]{1,0:T(8,128)(2,1)S(1)} %get-tuple-element.18.refs_1_, bf16[128,128]{1,0:T(8,128)(2,1)S(1)} %get-tuple-element.19.refs_2_, ...), custom_call_target="tpu_custom_call" | custom-call | flops 1000000 | bytes 2000000 | tf_op jit(solution)/shard_map/pallas_call | solution.py:339
  25.0 3.7 %all-to-all-start.1 = ((bf16[16,80,128]{2,1,0:T(8,128)(2,1)}), bf16[16,80,128]{2,1,0:T(8,128)(2,1)S(1)}, u32[]{:S(2)}, u32[]{:S(2)}) async-start(bf16[16,80,128]{2,1,0:T(8,128)(2,1)} %shard_map.84), calls=%async_computation.1 | async-start | bytes 655360 | tf_op jit(solution)/shard_map/all_to_all | solution.py:355
  28.7 4.5 %shard_map.85 = (bf16[18,128,128]{2,1,0:T(8,128)(2,1)S(1)}, bf16[256,256]{1,0:T(8,128)(2,1)S(1)}, bf16[256,256]{1,0:T(8,128)(2,1)S(1)}, bf16[256,128]{1,0:T(8,12...) custom-call(f32[17]{0:T(128)S(1)} %copy-done.10, bf16[18,128,128]{2,1,0:T(8,128)(2,1)S(1)} %copy-done.7), custom_call_target="tpu_custom_call" | custom-call | flops 15099494400 | bytes 4000000 | tf_op jit(solution)/shard_map/pallas_call | solution.py:187
  33.3 0.8 copy-done.1
  34.1 0.7 copy-done.2
  34.7 0.6 copy-done.3
  35.4 0.6 copy-done.4
  36.0 0.6 copy-done.5
  36.6 0.6 copy-done.6
  37.2 2.3 %all-to-all-done.1.in_ref = bf16[16,80,128]{2,1,0:T(8,128)(2,1)S(1)} async-done(((bf16[16,80,128]{2,1,0:T(8,128)(2,1)}), bf16[16,80,128]{2,1,0:T(8,128)(2,1)S(1)}, u32[]{:S(2)}, u32[]{:S(2)}) %all-to-all-start.1) | async-done | bytes 327712 | tf_op jit(solution)/shard_map/all_to_all | solution.py:355
  39.6 0.7 copy-done.11
  40.3 4.0 %shard_map.86 = bf16[8,16,1152]{2,1,0:T(8,128)(2,1)} custom-call(s32[1]{0:T(128)} %bitcast.parity_ref, bf16[16,80,128]{2,1,0:T(8,128)(2,1)} %copy-done.11, bf16[1,1,64,2304]{3,2,1,0:T(8,128)(2,1)} %refs_0_.1, f32[64,2304]{1,0:T(8,128)} %refs_1_.1, bf16[18,128,128]{2,1,0:T(8,128)(2,1)} %copy-done.1, bf16[256,256]{1,0:T(8,128)(2,1)} %copy-done.2, ...), custom_call_target="tpu_custom_call" | custom-call | flops 1000000 | bytes 2000000 | tf_op jit(solution)/shard_map/pallas_call | solution.py:339
  44.3 14.1 %all_to_all.25.in_ref = bf16[8,16,1152]{2,1,0:T(8,128)(2,1)S(1)} all-to-all(bf16[8,16,1152]{2,1,0:T(8,128)(2,1)} %shard_map.86), channel_id=1, replica_groups={{0,1,2,3,4,5,6,7},{8,9,10,11,12,13,14,15},{16,17,18,19,20,21,22,23},{24..., dimensions={0} | all-to-all | bytes 589824 | tf_op jit(solution)/shard_map/all_to_all | solution.py:355
  58.5 0.0 copy-start
  58.5 24.3 %all_to_all.26.in_ref = bf16[4,16,1152]{2,1,0:T(8,128)(2,1)S(1)} all-to-all(bf16[4,16,1152]{2,1,0:T(8,128)(2,1)S(1)} %shard_map.87), channel_id=1, replica_groups={{0,8,16,24},{1,9,17,25},{2,10,18,26},{3,11,19,27},{4,12,20,28},{5,13,21..., dimensions={0} | all-to-all | bytes 294912 | tf_op jit(solution)/shard_map/all_to_all | solution.py:355
  82.8 13.6 %all_to_all.27.in_ref = bf16[8,16,1152]{2,1,0:T(8,128)(2,1)S(1)} all-to-all(bf16[8,16,1152]{2,1,0:T(8,128)(2,1)S(1)} %shard_map.88), channel_id=1, replica_groups={{0,1,2,3,4,5,6,7},{8,9,10,11,12,13,14,15},{16,17,18,19,20,21,22,23},{24..., dimensions={0} | all-to-all | bytes 589824 | tf_op jit(solution)/shard_map/all_to_all | solution.py:355
  96.4 0.8 shard_map.89
  (15 shorter events, 0.1 us)
Async XLA Ops:
  2.3 9.4 %copy-start.8 = (bf16[8,128,128]{2,1,0:T(8,128)(2,1)S(1)}, bf16[8,128,128]{2,1,0:T(8,128)(2,1)}, u32[]{:S(2)}) copy-start(bf16[8,128,128]{2,1,0:T(8,128)(2,1)} %g_ref.2) | copy-start | bytes 786436
  2.3 20.6 %all-to-all-start = ((bf16[16,80,128]{2,1,0:T(8,128)(2,1)}), bf16[16,80,128]{2,1,0:T(8,128)(2,1)S(1)}, u32[]{:S(2)}, u32[]{:S(2)}) async-start(bf16[16,80,128]{2,1,0:T(8,128)(2,1)} %shard_map.82), calls=%async_computation | async-start | bytes 655360 | tf_op jit(solution)/shard_map/all_to_all | solution.py:355
  11.7 0.7 copy-start.9
  25.0 3.7 %copy-start.7 = (bf16[18,128,128]{2,1,0:T(8,128)(2,1)S(1)}, bf16[18,128,128]{2,1,0:T(8,128)(2,1)}, u32[]{:S(2)}) copy-start(bf16[18,128,128]{2,1,0:T(8,128)(2,1)} %g_ref.3) | copy-start | bytes 1769476
  25.0 3.7 %copy-start.10 = (f32[17]{0:T(128)S(1)}, f32[17]{0:T(128)}, u32[]{:S(2)}) copy-start(f32[17]{0:T(128)} %c_ref.3) | copy-start | bytes 208
  25.0 14.5 %all-to-all-start.1 = ((bf16[16,80,128]{2,1,0:T(8,128)(2,1)}), bf16[16,80,128]{2,1,0:T(8,128)(2,1)S(1)}, u32[]{:S(2)}, u32[]{:S(2)}) async-start(bf16[16,80,128]{2,1,0:T(8,128)(2,1)} %shard_map.84), calls=%async_computation.1 | async-start | bytes 655360 | tf_op jit(solution)/shard_map/all_to_all | solution.py:355
  33.3 0.8 copy-start.1
  34.1 0.7 copy-start.2
  34.7 0.7 copy-start.3
  35.4 0.6 copy-start.4
  36.0 0.6 copy-start.5
  36.6 0.6 copy-start.6
  39.6 0.7 copy-start.11
  58.5 37.9 %copy-start = (s32[1,64,2304]{2,1,0:T(8,128)S(1)}, s32[1,64,2304]{2,1,0:T(8,128)}, u32[]{:S(2)}) copy-start(s32[1,64,2304]{2,1,0:T(8,128)} %mask_ref.1) | copy-start | bytes 1769476

commit v4 on v3

--- a/solution.py
+++ b/solution.py
@@ -16,7 +16,7 @@
 F32 = jnp.float32
 BF16 = jnp.bfloat16
 GROUP = BLOCK // (2 * NSTEP)
-VMEM_LIMIT = 24 * 2**20
+VMEM_LIMIT = 16 * 2**20
 WIDE_LIMIT = 60 * 2**20
 
 
@@ -215,8 +215,14 @@
     for group in range(groups_of(nb)):
         edge = in_ref[group * BLOCK:(group + 1) * BLOCK, :]
         kept = jnp.zeros((count, BLOCK), F32)
-        for j in range(group * GROUP, min(nb, (group + 1) * GROUP)):
-            kept = jnp.where(owned[j % GROUP], dot_nt(lines[:, blocks[j]], edge), kept)
+        mine = range(group * GROUP, min(nb, (group + 1) * GROUP))
+        if count < BLOCK:
+            stacked = dot_nt(jnp.concatenate([lines[:, blocks[j]] for j in mine], axis=0), edge)
+            found = [stacked[at * count:(at + 1) * count] for at in range(len(mine))]
+        else:
+            found = [dot_nt(lines[:, blocks[j]], edge) for j in mine]
+        for at in range(len(mine)):
+            kept = jnp.where(owned[at], found[at], kept)
         products.append(kept.astype(BF16))
     coupled = dot_nt(jnp.concatenate(products, axis=1), map_ref[...])
     results = []
@@ -323,6 +329,15 @@
         out_ref[target] = total
 
 
+def add_kernel(scale, one_ref, two_ref, out_ref):
+    total = one_ref[0].astype(F32) + two_ref[0].astype(F32)
+    if scale is not None:
+        total = total / scale
+    total = total.astype(BF16)
+    for target in range(out_ref.shape[0]):
+        out_ref[target] = total
+
+
 def final_kernel(mask_ref, in_ref, out_ref):
     shares, _, width = in_ref.shape
     for pair in range(shares // 2):
@@ -383,11 +398,18 @@
     terms = call(functools.partial(row_kernel, x_blocks), (close,) + packed,
                  (parity, got) + inputs + tuple(x_tables),
                  near + [pltpu.VMEM((rows, columns), BF16), arrived],
-                 [pltpu.SMEM, pltpu.VMEM, pltpu.HBM, pltpu.HBM], WIDE_LIMIT)
+                 [pltpu.SMEM, pltpu.VMEM, pltpu.HBM, pltpu.HBM])
     terms = exchange(terms, "mem", near_groups)
-    terms = call(functools.partial(sum_kernel, None), (apart,) + packed, (terms,))
-    terms = exchange(terms, "mem", far_groups)
-    terms = call(functools.partial(sum_kernel, float(mem - 1)), (close,) + packed, (terms,))
+    part = call(functools.partial(sum_kernel, None), (1,) + packed, (terms,))
+    for step in range(2):
+        pairs = []
+        for device in range(mem):
+            z, odd = device // close, (device + step) % 2
+            pairs.append((device, ((z ^ 1) if odd == 0 else ((z - 1) ^ 1) + 1) % apart * close + device % close))
+        other = lax.ppermute(part, "mem", pairs)
+        copies, scale = (1, None) if step == 0 else (close, float(mem - 1))
+        part = call(functools.partial(add_kernel, scale), (copies,) + packed, (part, other))
+    terms = part
     terms = exchange(terms, "mem", near_groups)
     return call(final_kernel, (1, rows, columns), (mask, terms))
 

time: 97.7 us -> 89.1 us (0.912)
  blocking collectives: 52 us -> 25.5 us
  starting transfers between devices: 13 us -> 29.9 us
  waiting for transfers between devices: 10.3 us -> 18.3 us
  local copies, waits for them, and re-layouts: 5.35 us -> 0.67 us
  Pallas kernels: 16.4 us -> 14.1 us
    all_to_all x3 -> x2, blocking collectives: 52 us -> 25.5 us  [exchange(): lax.all_to_all(array, axis, split_axis=0, concat_axis=0, tiled=True, axis...]
    ppermute x0 -> x2, starting transfers between devices: none -> 16.9 us  [local(): other = lax.ppermute(part, 'mem', pairs)]
    unnamed x24 -> x14, local copies, waits for them, and re-layouts: 5.35 us -> 0.67 us
    ppermute x0 -> x2, waiting for transfers between devices: none -> 4.04 us  [local(): other = lax.ppermute(part, 'mem', pairs)]
    all_to_all x2, waiting for transfers between devices: 10.3 us -> 14.2 us  [exchange(): lax.all_to_all(array, axis, split_axis=0, concat_axis=0, tiled=True, axis...]
    pallas_call x6 -> x7, Pallas kernels: 9.28 us -> 7 us  [call(): pl.pallas_call(kernel, out_shape=jax.ShapeDtypeStruct(out_shape, BF16), i...]
  transfers between devices with their start and end apart: 2 -> 4, of which waited for: 2 -> 4; matrix products, arithmetic and copies ran while one was open for 0% -> 0% of each run, Pallas kernels for 7% -> 8%
where the time goes in v4:
time: 89.1 us; the launch traced here: 88.6 us
  starting transfers between devices  29.9 us (34%)
  blocking collectives  25.5 us (29%)
  waiting for transfers between devices  18.3 us (21%)
  Pallas kernels  14.1 us (16%)
    all_to_all x2, blocking collectives, exchange(): lax.all_to_all(array, axis, split_axis=0, concat_axis=0, tiled=True, axis...  25.5 us
    ppermute x2, starting transfers between devices, local(): other = lax.ppermute(part, 'mem', pairs)  16.9 us
    all_to_all x2, waiting for transfers between devices, exchange(): lax.all_to_all(array, axis, split_axis=0, concat_axis=0, tiled=True, axis...  14.2 us
    all_to_all x2, starting transfers between devices, exchange(): lax.all_to_all(array, axis, split_axis=0, concat_axis=0, tiled=True, axis...  13 us
    pallas_call x2, Pallas kernels, prepare(): pl.pallas_call(functools.partial(prepare_kernel, nb), out_shape=tuple((ja...  7.14 us
    pallas_call x7, Pallas kernels, call(): pl.pallas_call(kernel, out_shape=jax.ShapeDtypeStruct(out_shape, BF16), i...  7 us
    ppermute x2, waiting for transfers between devices, local(): other = lax.ppermute(part, 'mem', pairs)  4.04 us
  transfers between devices with their start and end apart: 4, of which 4 were waited for; matrix products, arithmetic and copies ran while one was open for 0% of the time, Pallas kernels for 8%

profile of v4, /device:TPU:1, one launch (start us, length us, event | category | flops | bytes accessed | tf_op | source)
XLA Modules:
  0.0 88.6 jit_solution(10709168223489281809)
XLA Ops:
  0.0 2.3 %shard_map.82 = bf16[16,80,128]{2,1,0:T(8,128)(2,1)} custom-call(bf16[1,64,2304]{2,1,0:T(8,128)(2,1)} %increment_hbm.1, s32[1,64,2304]{2,1,0:T(8,128)} %mask_ref.1, bf16[1,1,64,2304]{3,2,1,0:T(8,128)(2,1)} %refs_0_.1, f32[64,2304]{1,0:T(8,128)} %refs_1_.1), custom_call_target="tpu_custom_call" | custom-call | flops 1000000 | bytes 2000000 | tf_op jit(solution)/shard_map/pallas_call | solution.py:354
  2.3 0.0 copy-start.4
  2.4 9.3 %all-to-all-start = ((bf16[16,80,128]{2,1,0:T(8,128)(2,1)}), bf16[16,80,128]{2,1,0:T(8,128)(2,1)S(1)}, u32[]{:S(2)}, u32[]{:S(2)}) async-start(bf16[16,80,128]{2,1,0:T(8,128)(2,1)} %shard_map.82), calls=%async_computation | async-start | bytes 655360 | tf_op jit(solution)/shard_map/all_to_all | solution.py:370
  11.7 0.0 copy-start.5
  11.7 0.0 copy-done.4
  11.7 0.6 copy-done.5
  12.4 2.6 %shard_map.83 = (bf16[8,128,128]{2,1,0:T(8,128)(2,1)S(1)}, bf16[128,128]{1,0:T(8,128)(2,1)S(1)}, bf16[128,128]{1,0:T(8,128)(2,1)S(1)}, bf16[128,128]{1,0:T(8,128...) custom-call(f32[7]{0:T(128)S(1)} %copy-done.5, bf16[8,128,128]{2,1,0:T(8,128)(2,1)S(1)} %copy-done.4), custom_call_target="tpu_custom_call" | custom-call | flops 6710886400 | bytes 4000000 | tf_op jit(solution)/shard_map/pallas_call | solution.py:187
  15.0 8.0 %all-to-all-done.in_ref = bf16[16,80,128]{2,1,0:T(8,128)(2,1)S(1)} async-done(((bf16[16,80,128]{2,1,0:T(8,128)(2,1)}), bf16[16,80,128]{2,1,0:T(8,128)(2,1)S(1)}, u32[]{:S(2)}, u32[]{:S(2)}) %all-to-all-start) | async-done | bytes 327712 | tf_op jit(solution)/shard_map/all_to_all | solution.py:370
  23.0 2.1 %shard_map.84 = bf16[16,80,128]{2,1,0:T(8,128)(2,1)} custom-call(bf16[16,80,128]{2,1,0:T(8,128)(2,1)S(1)} %all-to-all-done.in_ref, bf16[8,128,128]{2,1,0:T(8,128)(2,1)S(1)} %get-tuple-element.17.refs_0_, bf16[128,128]{1,0:T(8,128)(2,1)S(1)} %get-tuple-element.18.refs_1_, bf16[128,128]{1,0:T(8,128)(2,1)S(1)} %get-tuple-element.19.refs_2_, ...), custom_call_target="tpu_custom_call" | custom-call | flops 1000000 | bytes 2000000 | tf_op jit(solution)/shard_map/pallas_call | solution.py:354
  25.0 3.7 %all-to-all-start.1 = ((bf16[16,80,128]{2,1,0:T(8,128)(2,1)}), bf16[16,80,128]{2,1,0:T(8,128)(2,1)S(1)}, u32[]{:S(2)}, u32[]{:S(2)}) async-start(bf16[16,80,128]{2,1,0:T(8,128)(2,1)} %shard_map.84), calls=%async_computation.1 | async-start | bytes 655360 | tf_op jit(solution)/shard_map/all_to_all | solution.py:370
  28.8 0.0 copy-start.1
  28.8 0.0 copy-start.2
  28.8 4.5 %shard_map.85 = (bf16[18,128,128]{2,1,0:T(8,128)(2,1)S(1)}, bf16[256,256]{1,0:T(8,128)(2,1)S(1)}, bf16[256,256]{1,0:T(8,128)(2,1)S(1)}, bf16[256,128]{1,0:T(8,12...) custom-call(f32[17]{0:T(128)S(1)} %copy-done.6, bf16[18,128,128]{2,1,0:T(8,128)(2,1)S(1)} %copy-done.3), custom_call_target="tpu_custom_call" | custom-call | flops 15099494400 | bytes 4000000 | tf_op jit(solution)/shard_map/pallas_call | solution.py:187
  33.3 6.3 %all-to-all-done.1.in_ref = bf16[16,80,128]{2,1,0:T(8,128)(2,1)S(1)} async-done(((bf16[16,80,128]{2,1,0:T(8,128)(2,1)}), bf16[16,80,128]{2,1,0:T(8,128)(2,1)S(1)}, u32[]{:S(2)}, u32[]{:S(2)}) %all-to-all-start.1) | async-done | bytes 327712 | tf_op jit(solution)/shard_map/all_to_all | solution.py:370
  39.6 0.0 copy-done.2
  39.6 1.7 %shard_map.86 = bf16[8,16,1152]{2,1,0:T(8,128)(2,1)S(1)} custom-call(s32[1]{0:T(128)} %bitcast.parity_ref, bf16[16,80,128]{2,1,0:T(8,128)(2,1)S(1)} %all-to-all-done.1.in_ref, bf16[1,1,64,2304]{3,2,1,0:T(8,128)(2,1)S(1)} %copy-done.2, f32[64,2304]{1,0:T(8,128)S(1)} %copy-done.1, bf16[18,128,128]{2,1,0:T(8,128)(2,1)S(1)} %get-tuple-element.23.refs_2_, ...), custom_call_target="tpu_custom_call" | custom-call | flops 1000000 | bytes 2000000 | tf_op jit(solution)/shard_map/pallas_call | solution.py:354
  41.3 13.9 %all_to_all.20.in_ref = bf16[8,16,1152]{2,1,0:T(8,128)(2,1)S(1)} all-to-all(bf16[8,16,1152]{2,1,0:T(8,128)(2,1)S(1)} %shard_map.86), channel_id=1, replica_groups={{0,1,2,3,4,5,6,7},{8,9,10,11,12,13,14,15},{16,17,18,19,20,21,22,23},{24..., dimensions={0} | all-to-all | bytes 589824 | tf_op jit(solution)/shard_map/all_to_all | solution.py:370
  55.3 0.0 copy-start
  55.3 9.9 %collective-permute-start = (bf16[1,16,1152]{2,1,0:T(8,128)(2,1)S(1)}, bf16[1,16,1152]{2,1,0:T(8,128)(2,1)S(1)}, u32[]{:S(2)}, u32[]{:S(2)}) collective-permute-start(bf16[1,16,1152]{2,1,0:T(8,128)(2,1)S(1)} %shard_map.87.one_ref), channel_id=1, source_target_pairs={{0,8},{1,25},{2,10},{3,27},{4,12},{5,29},{6,14},{7,31},{8,0},{9,17... | collective-permute-start | bytes 110600 | tf_op jit(solution)/shard_map/ppermute | solution.py:409
  65.2 1.6 %collective-permute-done.two_ref = bf16[1,16,1152]{2,1,0:T(8,128)(2,1)S(1)} collective-permute-done((bf16[1,16,1152]{2,1,0:T(8,128)(2,1)S(1)}, bf16[1,16,1152]{2,1,0:T(8,128)(2,1)S(1)}, u32[]{:S(2)}, u32[]{:S(2)}) %collective-permute-start) | collective-permute-done | bytes 36896 | tf_op jit(solution)/shard_map/ppermute | solution.py:409
  66.8 7.0 %collective-permute-start.1 = (bf16[1,16,1152]{2,1,0:T(8,128)(2,1)S(1)}, bf16[1,16,1152]{2,1,0:T(8,128)(2,1)S(1)}, u32[]{:S(2)}, u32[]{:S(2)}) collective-permute-start(bf16[1,16,1152]{2,1,0:T(8,128)(2,1)S(1)} %shard_map.88.one_ref), channel_id=1, source_target_pairs={{0,24},{1,9},{2,26},{3,11},{4,28},{5,13},{6,30},{7,15},{8,16},{9,1... | collective-permute-start | bytes 110600 | tf_op jit(solution)/shard_map/ppermute | solution.py:409
  73.8 2.4 %collective-permute-done.1.two_ref = bf16[1,16,1152]{2,1,0:T(8,128)(2,1)S(1)} collective-permute-done((bf16[1,16,1152]{2,1,0:T(8,128)(2,1)S(1)}, bf16[1,16,1152]{2,1,0:T(8,128)(2,1)S(1)}, u32[]{:S(2)}, u32[]{:S(2)}) %collective-permute-start.1) | collective-permute-done | bytes 36896 | tf_op jit(solution)/shard_map/ppermute | solution.py:409
  76.3 11.6 %all_to_all.21.in_ref = bf16[8,16,1152]{2,1,0:T(8,128)(2,1)S(1)} all-to-all(bf16[8,16,1152]{2,1,0:T(8,128)(2,1)S(1)} %shard_map.89), channel_id=1, replica_groups={{0,1,2,3,4,5,6,7},{8,9,10,11,12,13,14,15},{16,17,18,19,20,21,22,23},{24..., dimensions={0} | all-to-all | bytes 589824 | tf_op jit(solution)/shard_map/all_to_all | solution.py:370
  87.8 0.8 shard_map.90
  (9 shorter events, 0.1 us)
Async XLA Ops:
  2.3 9.4 %copy-start.4 = (bf16[8,128,128]{2,1,0:T(8,128)(2,1)S(1)}, bf16[8,128,128]{2,1,0:T(8,128)(2,1)}, u32[]{:S(2)}) copy-start(bf16[8,128,128]{2,1,0:T(8,128)(2,1)} %g_ref.2) | copy-start | bytes 786436
  2.4 20.6 %all-to-all-start = ((bf16[16,80,128]{2,1,0:T(8,128)(2,1)}), bf16[16,80,128]{2,1,0:T(8,128)(2,1)S(1)}, u32[]{:S(2)}, u32[]{:S(2)}) async-start(bf16[16,80,128]{2,1,0:T(8,128)(2,1)} %shard_map.82), calls=%async_computation | async-start | bytes 655360 | tf_op jit(solution)/shard_map/all_to_all | solution.py:370
  11.7 0.7 copy-start.5
  25.0 3.7 %copy-start.3 = (bf16[18,128,128]{2,1,0:T(8,128)(2,1)S(1)}, bf16[18,128,128]{2,1,0:T(8,128)(2,1)}, u32[]{:S(2)}) copy-start(bf16[18,128,128]{2,1,0:T(8,128)(2,1)} %g_ref.3) | copy-start | bytes 1769476
  25.0 3.7 %copy-start.6 = (f32[17]{0:T(128)S(1)}, f32[17]{0:T(128)}, u32[]{:S(2)}) copy-start(f32[17]{0:T(128)} %c_ref.3) | copy-start | bytes 208
  25.0 14.5 %all-to-all-start.1 = ((bf16[16,80,128]{2,1,0:T(8,128)(2,1)}), bf16[16,80,128]{2,1,0:T(8,128)(2,1)S(1)}, u32[]{:S(2)}, u32[]{:S(2)}) async-start(bf16[16,80,128]{2,1,0:T(8,128)(2,1)} %shard_map.84), calls=%async_computation.1 | async-start | bytes 655360 | tf_op jit(solution)/shard_map/all_to_all | solution.py:370
  28.8 10.8 %copy-start.1 = (f32[64,2304]{1,0:T(8,128)S(1)}, f32[64,2304]{1,0:T(8,128)}, u32[]{:S(2)}) copy-start(f32[64,2304]{1,0:T(8,128)} %refs_1_.1) | copy-start | bytes 1769476
  28.8 10.8 %copy-start.2 = (bf16[1,1,64,2304]{3,2,1,0:T(8,128)(2,1)S(1)}, bf16[1,1,64,2304]{3,2,1,0:T(8,128)(2,1)}, u32[]{:S(2)}) copy-start(bf16[1,1,64,2304]{3,2,1,0:T(8,128)(2,1)} %refs_0_.1) | copy-start | bytes 884740
  55.3 32.6 %copy-start = (s32[1,64,2304]{2,1,0:T(8,128)S(1)}, s32[1,64,2304]{2,1,0:T(8,128)}, u32[]{:S(2)}) copy-start(s32[1,64,2304]{2,1,0:T(8,128)} %mask_ref.1) | copy-start | bytes 1769476
  55.3 11.5 %collective-permute-start = (bf16[1,16,1152]{2,1,0:T(8,128)(2,1)S(1)}, bf16[1,16,1152]{2,1,0:T(8,128)(2,1)S(1)}, u32[]{:S(2)}, u32[]{:S(2)}) collective-permute-start(bf16[1,16,1152]{2,1,0:T(8,128)(2,1)S(1)} %shard_map.87.one_ref), channel_id=1, source_target_pairs={{0,8},{1,25},{2,10},{3,27},{4,12},{5,29},{6,14},{7,31},{8,0},{9,17... | collective-permute-start | bytes 110600 | tf_op jit(solution)/shard_map/ppermute | solution.py:409
  66.8 9.4 %collective-permute-start.1 = (bf16[1,16,1152]{2,1,0:T(8,128)(2,1)S(1)}, bf16[1,16,1152]{2,1,0:T(8,128)(2,1)S(1)}, u32[]{:S(2)}, u32[]{:S(2)}) collective-permute-start(bf16[1,16,1152]{2,1,0:T(8,128)(2,1)S(1)} %shard_map.88.one_ref), channel_id=1, source_target_pairs={{0,24},{1,9},{2,26},{3,11},{4,28},{5,13},{6,30},{7,15},{8,16},{9,1... | collective-permute-start | bytes 110600 | tf_op jit(solution)/shard_map/ppermute | solution.py:409

commit v5 on v4

--- a/solution.py
+++ b/solution.py
@@ -13,6 +13,7 @@
 NSTEP = 7
 HALF = 64
 EXTRA = 16
+FOLD = EXTRA // 2
 F32 = jnp.float32
 BF16 = jnp.bfloat16
 GROUP = BLOCK // (2 * NSTEP)
@@ -244,6 +245,14 @@
     return run_steps(lines, nb, pow_ref, map_f_ref, rows_ref, turned_ref, False)
 
 
+def beside(left, right):
+    return jnp.where(lax.broadcasted_iota(jnp.int32, left.shape, 1) < HALF, left, right)
+
+
+def swap(tile):
+    return pltpu.roll(tile, HALF, 1)
+
+
 def start_kernel(increment_hbm, mask_hbm, members_hbm, weight_hbm, out_ref,
                  increment_ref, mask_ref, members_ref, weight_ref, arrived):
     copies = [
@@ -266,7 +275,8 @@
         tail = values(slice((shares + half) * BLOCK, (shares + half + 1) * BLOCK))
         turned = jnp.concatenate([tail, tail], axis=0).T
         for s in range(8):
-            out_ref[half * 8 + s, HALF:HALF + EXTRA, :] = turned[s * EXTRA:(s + 1) * EXTRA].astype(BF16)
+            out_ref[half * 8 + s, HALF:HALF + FOLD, :] = beside(
+                turned[s * EXTRA:s * EXTRA + FOLD], turned[s * EXTRA + FOLD:(s + 1) * EXTRA]).astype(BF16)
     for s in range(shares):
         out_ref[s, 0:HALF, :] = values(slice(s * BLOCK, (s + 1) * BLOCK)).astype(BF16)
 
@@ -277,19 +287,20 @@
         at = slice(j * BLOCK, (j + 1) * BLOCK)
         square = jnp.concatenate([in_ref[2 * j, 0:HALF, :], in_ref[2 * j + 1, 0:HALF, :]], axis=0)
         lines[0:BLOCK, at] = square.astype(F32).T.astype(BF16)
-        lane = lax.broadcasted_iota(jnp.int32, (EXTRA, BLOCK), 1)
-        tail = jnp.where(lane < HALF, in_ref[2 * j, HALF:HALF + EXTRA, :].astype(F32),
-                         in_ref[2 * j + 1, HALF:HALF + EXTRA, :].astype(F32))
+        even = in_ref[2 * j, HALF:HALF + FOLD, :].astype(F32)
+        odd = in_ref[2 * j + 1, HALF:HALF + FOLD, :].astype(F32)
+        tail = jnp.concatenate([beside(even, swap(odd)), beside(swap(even), odd)], axis=0)
         lines[BLOCK:BLOCK + EXTRA, at] = tail.astype(BF16)
     for j, block in enumerate(run_both(lines, nb, *tables)):
         square = block[0:BLOCK].T.astype(BF16)
-        tail = block[BLOCK:BLOCK + EXTRA].astype(BF16)
+        top, bottom = block[BLOCK:BLOCK + FOLD], block[BLOCK + FOLD:BLOCK + EXTRA]
+        tails = beside(top, swap(bottom)), beside(swap(top), bottom)
         for half in range(2):
             out_ref[2 * j + half, 0:HALF, :] = square[half * HALF:(half + 1) * HALF]
-            out_ref[2 * j + half, HALF:HALF + EXTRA, :] = tail
-
-
-def row_kernel(nb, parity_ref, in_ref, *refs):
+            out_ref[2 * j + half, HALF:HALF + FOLD, :] = tails[half].astype(BF16)
+
+
+def row_kernel(nb, in_ref, *refs):
     members_hbm, weight_hbm, *tables, out_ref, members_ref, weight_ref, lines, arrived = refs
     copies = [pltpu.make_async_copy(members_hbm, members_ref, arrived.at[0]),
               pltpu.make_async_copy(weight_hbm, weight_ref, arrived.at[1])]
@@ -298,55 +309,38 @@
     shares = in_ref.shape[0]
     for s in range(shares):
         lines[:, s * BLOCK:(s + 1) * BLOCK] = in_ref[s, 0:HALF, :]
-    odd = parity_ref[0] == 1
     for half in range(2):
-        tail = jnp.concatenate(
-            [in_ref[half * 8 + s, HALF:HALF + EXTRA, :] for s in range(8)], axis=0).astype(F32).T
-        tail = jnp.where(odd, tail[HALF:BLOCK], tail[0:HALF])
+        folded = [in_ref[half * 8 + s, HALF:HALF + FOLD, :].astype(F32) for s in range(8)]
+        tail = jnp.concatenate([part for tile in folded for part in (tile, swap(tile))], axis=0).T[0:HALF]
         at = (shares + half) * BLOCK
         lines[:, at:at + BLOCK] = tail.astype(BF16)
-    takers, middle = out_ref.shape[0], nb // 2
     blocks = run_both(lines, nb, *tables)
     for copy in copies:
         copy.wait()
-    for j in range(middle):
-        left, right = slice(j * BLOCK, (j + 1) * BLOCK), slice((middle + j) * BLOCK, (middle + j + 1) * BLOCK)
-        term_left = members_ref[0, 0, :, left].astype(F32) * weight_ref[:, left] * blocks[j]
-        term_right = members_ref[0, 0, :, right].astype(F32) * weight_ref[:, right] * blocks[middle + j]
-        for taker in range(takers):
-            rows = slice(taker * 8, taker * 8 + 8)
-            out_ref[taker, :, left] = jnp.concatenate([term_left[rows], term_right[rows]], axis=0).astype(BF16)
-
-
-def sum_kernel(scale, in_ref, out_ref):
+    for j in range(nb):
+        at = slice(j * BLOCK, (j + 1) * BLOCK)
+        term = members_ref[0, 0, :, at].astype(F32) * weight_ref[:, at] * blocks[j]
+        for taker in range(out_ref.shape[0]):
+            out_ref[taker, :, at] = term[taker * 8:taker * 8 + 8].astype(BF16)
+
+
+def sum_kernel(in_ref, out_ref):
     total = in_ref[0].astype(F32)
     for source in range(1, in_ref.shape[0]):
         total += in_ref[source].astype(F32)
-    if scale is not None:
-        total = total / scale
-    total = total.astype(BF16)
+    out_ref[0] = total.astype(BF16)
+
+
+def add_kernel(one_ref, two_ref, out_ref):
+    out_ref[0] = (one_ref[0].astype(F32) + two_ref[0].astype(F32)).astype(BF16)
+
+
+def final_kernel(scale, own_ref, one_ref, two_ref, mask_ref, out_ref):
+    rows = out_ref.shape[1]
+    mask = mask_ref[0, pl.ds(pl.multiple_of(own_ref[0] * rows, rows), rows), :].astype(F32)
+    total = (mask * (one_ref[0].astype(F32) + two_ref[0].astype(F32)) / scale).astype(BF16)
     for target in range(out_ref.shape[0]):
         out_ref[target] = total
-
-
-def add_kernel(scale, one_ref, two_ref, out_ref):
-    total = one_ref[0].astype(F32) + two_ref[0].astype(F32)
-    if scale is not None:
-        total = total / scale
-    total = total.astype(BF16)
-    for target in range(out_ref.shape[0]):
-        out_ref[target] = total
-
-
-def final_kernel(mask_ref, in_ref, out_ref):
-    shares, _, width = in_ref.shape
-    for pair in range(shares // 2):
-        one, two = in_ref[2 * pair].astype(F32), in_ref[2 * pair + 1].astype(F32)
-        rows = slice(pair * 16, pair * 16 + 16)
-        left = jnp.concatenate([one[0:8], two[0:8]], axis=0)
-        right = jnp.concatenate([one[8:16], two[8:16]], axis=0)
-        out_ref[0, rows, 0:width] = (left * mask_ref[0, rows, 0:width].astype(F32)).astype(BF16)
-        out_ref[0, rows, width:2 * width] = (right * mask_ref[0, rows, width:2 * width].astype(F32)).astype(BF16)
 
 
 def call(kernel, out_shape, operands, scratch=(), spaces=(), limit=VMEM_LIMIT):
@@ -378,7 +372,7 @@
     apart = mem // close
     near_groups = [[z * close + i for i in range(close)] for z in range(apart)]
     far_groups = [[z * close + i for z in range(apart)] for i in range(close)]
-    share = (HALF + EXTRA, BLOCK)
+    share = (HALF + FOLD, BLOCK)
 
     y_tables = prepare(y_inverse, y_coupling)
     x_tables = prepare(x_inverse, x_coupling)
@@ -391,27 +385,27 @@
     sent = call(functools.partial(column_kernel, y_blocks), (space,) + share, (got,) + tuple(y_tables),
                 [pltpu.VMEM((BLOCK + EXTRA, y_blocks * BLOCK), BF16)])
     got = exchange(sent, "space")
-    parity = (lax.axis_index("space") % 2).astype(jnp.int32)[None]
-    packed = (16, columns // 2)
+    own = (lax.axis_index("mem") % close).astype(jnp.int32)[None]
+    packed = (rows // close, columns)
     inputs = (members, weight)
     near, arrived = landing(inputs)
     terms = call(functools.partial(row_kernel, x_blocks), (close,) + packed,
-                 (parity, got) + inputs + tuple(x_tables),
+                 (got,) + inputs + tuple(x_tables),
                  near + [pltpu.VMEM((rows, columns), BF16), arrived],
-                 [pltpu.SMEM, pltpu.VMEM, pltpu.HBM, pltpu.HBM])
+                 [pltpu.VMEM, pltpu.HBM, pltpu.HBM])
     terms = exchange(terms, "mem", near_groups)
-    part = call(functools.partial(sum_kernel, None), (1,) + packed, (terms,))
+    part = call(sum_kernel, (1,) + packed, (terms,))
     for step in range(2):
         pairs = []
         for device in range(mem):
             z, odd = device // close, (device + step) % 2
             pairs.append((device, ((z ^ 1) if odd == 0 else ((z - 1) ^ 1) + 1) % apart * close + device % close))
         other = lax.ppermute(part, "mem", pairs)
-        copies, scale = (1, None) if step == 0 else (close, float(mem - 1))
-        part = call(functools.partial(add_kernel, scale), (copies,) + packed, (part, other))
-    terms = part
-    terms = exchange(terms, "mem", near_groups)
-    return call(final_kernel, (1, rows, columns), (mask, terms))
+        if step == 0:
+            part = call(add_kernel, (1,) + packed, (part, other))
+    result = call(functools.partial(final_kernel, float(mem - 1)), (close,) + packed, (own, part, other, mask),
+                  spaces=[pltpu.SMEM])
+    return exchange(result, "mem", near_groups).reshape(1, rows, columns)
 
 
 def solution(mesh):

time: 89.1 us -> 87.8 us (0.985)
    pallas_call x7 -> x6, Pallas kernels: 7 us -> 6.27 us  [call(): pl.pallas_call(kernel, out_shape=jax.ShapeDtypeStruct(out_shape, BF16), i...]
where the time goes in v5:
time: 87.8 us; the launch traced here: 87.4 us
  starting transfers between devices  30.1 us (34%)
  blocking collectives  25.4 us (29%)
  waiting for transfers between devices  17.6 us (20%)
  Pallas kernels  13.4 us (15%)
    all_to_all x2, blocking collectives, exchange(): lax.all_to_all(array, axis, split_axis=0, concat_axis=0, tiled=True, axis...  25.4 us
    ppermute x2, starting transfers between devices, local(): other = lax.ppermute(part, 'mem', pairs)  16.9 us
    all_to_all x2, waiting for transfers between devices, exchange(): lax.all_to_all(array, axis, split_axis=0, concat_axis=0, tiled=True, axis...  13.6 us
    all_to_all x2, starting transfers between devices, exchange(): lax.all_to_all(array, axis, split_axis=0, concat_axis=0, tiled=True, axis...  13.2 us
    pallas_call x2, Pallas kernels, prepare(): pl.pallas_call(functools.partial(prepare_kernel, nb), out_shape=tuple((ja...  7.15 us
    pallas_call x6, Pallas kernels, call(): pl.pallas_call(kernel, out_shape=jax.ShapeDtypeStruct(out_shape, BF16), i...  6.27 us
    ppermute x2, waiting for transfers between devices, local(): other = lax.ppermute(part, 'mem', pairs)  3.94 us
  transfers between devices with their start and end apart: 4, of which 4 were waited for; matrix products, arithmetic and copies ran while one was open for 0% of the time, Pallas kernels for 8%

profile of v5, /device:TPU:1, one launch (start us, length us, event | category | flops | bytes accessed | tf_op | source)
XLA Modules:
  0.0 87.4 jit_solution(4363598733143579091)
XLA Ops:
  0.0 2.3 %shard_map.82 = bf16[16,72,128]{2,1,0:T(8,128)(2,1)} custom-call(bf16[1,64,2304]{2,1,0:T(8,128)(2,1)} %increment_hbm.1, s32[1,64,2304]{2,1,0:T(8,128)} %mask_ref.1, bf16[1,1,64,2304]{3,2,1,0:T(8,128)(2,1)} %refs_0_.1, f32[64,2304]{1,0:T(8,128)} %refs_1_.1), custom_call_target="tpu_custom_call" | custom-call | flops 1000000 | bytes 2000000 | tf_op jit(solution)/shard_map/pallas_call | solution.py:348
  2.3 0.0 copy-start.4
  2.3 0.0 copy-start.5
  2.4 9.3 %all-to-all-start = ((bf16[16,72,128]{2,1,0:T(8,128)(2,1)}), bf16[16,72,128]{2,1,0:T(8,128)(2,1)S(1)}, u32[]{:S(2)}, u32[]{:S(2)}) async-start(bf16[16,72,128]{2,1,0:T(8,128)(2,1)} %shard_map.82), calls=%async_computation | async-start | bytes 589824 | tf_op jit(solution)/shard_map/all_to_all | solution.py:364
  11.7 0.0 copy-done.4
  11.7 0.0 copy-done.5
  11.7 2.6 %shard_map.83 = (bf16[8,128,128]{2,1,0:T(8,128)(2,1)S(1)}, bf16[128,128]{1,0:T(8,128)(2,1)S(1)}, bf16[128,128]{1,0:T(8,128)(2,1)S(1)}, bf16[128,128]{1,0:T(8,128...) custom-call(f32[7]{0:T(128)S(1)} %copy-done.5, bf16[8,128,128]{2,1,0:T(8,128)(2,1)S(1)} %copy-done.4), custom_call_target="tpu_custom_call" | custom-call | flops 6710886400 | bytes 4000000 | tf_op jit(solution)/shard_map/pallas_call | solution.py:188
  14.4 7.9 %all-to-all-done.in_ref = bf16[16,72,128]{2,1,0:T(8,128)(2,1)S(1)} async-done(((bf16[16,72,128]{2,1,0:T(8,128)(2,1)}), bf16[16,72,128]{2,1,0:T(8,128)(2,1)S(1)}, u32[]{:S(2)}, u32[]{:S(2)}) %all-to-all-start) | async-done | bytes 294944 | tf_op jit(solution)/shard_map/all_to_all | solution.py:364
  22.3 2.1 %shard_map.84 = bf16[16,72,128]{2,1,0:T(8,128)(2,1)} custom-call(bf16[16,72,128]{2,1,0:T(8,128)(2,1)S(1)} %all-to-all-done.in_ref, bf16[8,128,128]{2,1,0:T(8,128)(2,1)S(1)} %get-tuple-element.17.refs_0_, bf16[128,128]{1,0:T(8,128)(2,1)S(1)} %get-tuple-element.18.refs_1_, bf16[128,128]{1,0:T(8,128)(2,1)S(1)} %get-tuple-element.19.refs_2_, ...), custom_call_target="tpu_custom_call" | custom-call | flops 1000000 | bytes 2000000 | tf_op jit(solution)/shard_map/pallas_call | solution.py:348
  24.4 3.9 %all-to-all-start.1 = ((bf16[16,72,128]{2,1,0:T(8,128)(2,1)}), bf16[16,72,128]{2,1,0:T(8,128)(2,1)S(1)}, u32[]{:S(2)}, u32[]{:S(2)}) async-start(bf16[16,72,128]{2,1,0:T(8,128)(2,1)} %shard_map.84), calls=%async_computation.1 | async-start | bytes 589824 | tf_op jit(solution)/shard_map/all_to_all | solution.py:364
  28.3 0.0 copy-done.3
  28.3 0.0 copy-start
  28.3 0.0 copy-start.2
  28.3 4.5 %shard_map.85 = (bf16[18,128,128]{2,1,0:T(8,128)(2,1)S(1)}, bf16[256,256]{1,0:T(8,128)(2,1)S(1)}, bf16[256,256]{1,0:T(8,128)(2,1)S(1)}, bf16[256,128]{1,0:T(8,12...) custom-call(f32[17]{0:T(128)S(1)} %copy-done.6, bf16[18,128,128]{2,1,0:T(8,128)(2,1)S(1)} %copy-done.3), custom_call_target="tpu_custom_call" | custom-call | flops 15099494400 | bytes 4000000 | tf_op jit(solution)/shard_map/pallas_call | solution.py:188
  32.8 5.7 %all-to-all-done.1.in_ref = bf16[16,72,128]{2,1,0:T(8,128)(2,1)S(1)} async-done(((bf16[16,72,128]{2,1,0:T(8,128)(2,1)}), bf16[16,72,128]{2,1,0:T(8,128)(2,1)S(1)}, u32[]{:S(2)}, u32[]{:S(2)}) %all-to-all-start.1) | async-done | bytes 294944 | tf_op jit(solution)/shard_map/all_to_all | solution.py:364
  38.5 1.8 %shard_map.86 = bf16[8,8,2304]{2,1,0:T(8,128)(2,1)S(1)} custom-call(bf16[16,72,128]{2,1,0:T(8,128)(2,1)S(1)} %all-to-all-done.1.in_ref, bf16[1,1,64,2304]{3,2,1,0:T(8,128)(2,1)S(1)} %copy-done.2, f32[64,2304]{1,0:T(8,128)S(1)} %copy-done, bf16[18,128,128]{2,1,0:T(8,128)(2,1)S(1)} %get-tuple-element.23.refs_2_, ...), custom_call_target="tpu_custom_call" | custom-call | flops 1000000 | bytes 2000000 | tf_op jit(solution)/shard_map/pallas_call | solution.py:348
  40.3 0.0 copy-start.1
  40.3 13.7 %all_to_all.20.in_ref = bf16[8,8,2304]{2,1,0:T(8,128)(2,1)S(1)} all-to-all(bf16[8,8,2304]{2,1,0:T(8,128)(2,1)S(1)} %shard_map.86), channel_id=1, replica_groups={{0,1,2,3,4,5,6,7},{8,9,10,11,12,13,14,15},{16,17,18,19,20,21,22,23},{24..., dimensions={0} | all-to-all | bytes 589824 | tf_op jit(solution)/shard_map/all_to_all | solution.py:364
  54.1 9.8 %collective-permute-start = (bf16[1,8,2304]{2,1,0:T(8,128)(2,1)S(1)}, bf16[1,8,2304]{2,1,0:T(8,128)(2,1)S(1)}, u32[]{:S(2)}, u32[]{:S(2)}) collective-permute-start(bf16[1,8,2304]{2,1,0:T(8,128)(2,1)S(1)} %shard_map.87.one_ref), channel_id=1, source_target_pairs={{0,8},{1,25},{2,10},{3,27},{4,12},{5,29},{6,14},{7,31},{8,0},{9,17... | collective-permute-start | bytes 110600 | tf_op jit(solution)/shard_map/ppermute | solution.py:403
  63.8 1.6 %collective-permute-done.two_ref = bf16[1,8,2304]{2,1,0:T(8,128)(2,1)S(1)} collective-permute-done((bf16[1,8,2304]{2,1,0:T(8,128)(2,1)S(1)}, bf16[1,8,2304]{2,1,0:T(8,128)(2,1)S(1)}, u32[]{:S(2)}, u32[]{:S(2)}) %collective-permute-start) | collective-permute-done | bytes 36896 | tf_op jit(solution)/shard_map/ppermute | solution.py:403
  65.5 7.2 %collective-permute-start.1 = (bf16[1,8,2304]{2,1,0:T(8,128)(2,1)S(1)}, bf16[1,8,2304]{2,1,0:T(8,128)(2,1)S(1)}, u32[]{:S(2)}, u32[]{:S(2)}) collective-permute-start(bf16[1,8,2304]{2,1,0:T(8,128)(2,1)S(1)} %shard_map.88.one_ref), channel_id=1, source_target_pairs={{0,24},{1,9},{2,26},{3,11},{4,28},{5,13},{6,30},{7,15},{8,16},{9,1... | collective-permute-start | bytes 110600 | tf_op jit(solution)/shard_map/ppermute | solution.py:403
  72.7 2.3 %collective-permute-done.1.two_ref = bf16[1,8,2304]{2,1,0:T(8,128)(2,1)S(1)} collective-permute-done((bf16[1,8,2304]{2,1,0:T(8,128)(2,1)S(1)}, bf16[1,8,2304]{2,1,0:T(8,128)(2,1)S(1)}, u32[]{:S(2)}, u32[]{:S(2)}) %collective-permute-start.1) | collective-permute-done | bytes 36896 | tf_op jit(solution)/shard_map/ppermute | solution.py:403
  75.0 11.7 %all_to_all.21 = bf16[8,8,2304]{2,1,0:T(8,128)(2,1)S(1)} all-to-all(bf16[8,8,2304]{2,1,0:T(8,128)(2,1)S(1)} %shard_map.89), channel_id=1, replica_groups={{0,1,2,3,4,5,6,7},{8,9,10,11,12,13,14,15},{16,17,18,19,20,21,22,23},{24..., dimensions={0} | all-to-all | bytes 589824 | tf_op jit(solution)/shard_map/all_to_all | solution.py:364
  86.7 0.7 copy.10
  (9 shorter events, 0.1 us)
Async XLA Ops:
  2.3 9.4 %copy-start.4 = (bf16[8,128,128]{2,1,0:T(8,128)(2,1)S(1)}, bf16[8,128,128]{2,1,0:T(8,128)(2,1)}, u32[]{:S(2)}) copy-start(bf16[8,128,128]{2,1,0:T(8,128)(2,1)} %g_ref.2) | copy-start | bytes 786436
  2.3 9.4 %copy-start.5 = (f32[7]{0:T(128)S(1)}, f32[7]{0:T(128)}, u32[]{:S(2)}) copy-start(f32[7]{0:T(128)} %c_ref.2) | copy-start | bytes 88
  2.4 19.9 %all-to-all-start = ((bf16[16,72,128]{2,1,0:T(8,128)(2,1)}), bf16[16,72,128]{2,1,0:T(8,128)(2,1)S(1)}, u32[]{:S(2)}, u32[]{:S(2)}) async-start(bf16[16,72,128]{2,1,0:T(8,128)(2,1)} %shard_map.82), calls=%async_computation | async-start | bytes 589824 | tf_op jit(solution)/shard_map/all_to_all | solution.py:364
  22.3 6.0 %copy-start.3 = (bf16[18,128,128]{2,1,0:T(8,128)(2,1)S(1)}, bf16[18,128,128]{2,1,0:T(8,128)(2,1)}, u32[]{:S(2)}) copy-start(bf16[18,128,128]{2,1,0:T(8,128)(2,1)} %g_ref.3) | copy-start | bytes 1769476
  24.4 3.9 %copy-start.6 = (f32[17]{0:T(128)S(1)}, f32[17]{0:T(128)}, u32[]{:S(2)}) copy-start(f32[17]{0:T(128)} %c_ref.3) | copy-start | bytes 208
  24.4 14.2 %all-to-all-start.1 = ((bf16[16,72,128]{2,1,0:T(8,128)(2,1)}), bf16[16,72,128]{2,1,0:T(8,128)(2,1)S(1)}, u32[]{:S(2)}, u32[]{:S(2)}) async-start(bf16[16,72,128]{2,1,0:T(8,128)(2,1)} %shard_map.84), calls=%async_computation.1 | async-start | bytes 589824 | tf_op jit(solution)/shard_map/all_to_all | solution.py:364
  28.3 10.3 %copy-start = (f32[64,2304]{1,0:T(8,128)S(1)}, f32[64,2304]{1,0:T(8,128)}, u32[]{:S(2)}) copy-start(f32[64,2304]{1,0:T(8,128)} %refs_1_.1) | copy-start | bytes 1769476
  28.3 10.3 %copy-start.2 = (bf16[1,1,64,2304]{3,2,1,0:T(8,128)(2,1)S(1)}, bf16[1,1,64,2304]{3,2,1,0:T(8,128)(2,1)}, u32[]{:S(2)}) copy-start(bf16[1,1,64,2304]{3,2,1,0:T(8,128)(2,1)} %refs_0_.1) | copy-start | bytes 884740
  40.3 34.7 %copy-start.1 = (s32[1,64,2304]{2,1,0:T(8,128)S(1)}, s32[1,64,2304]{2,1,0:T(8,128)}, u32[]{:S(2)}) copy-start(s32[1,64,2304]{2,1,0:T(8,128)} %mask_ref.1) | copy-start | bytes 1769476
  54.1 11.4 %collective-permute-start = (bf16[1,8,2304]{2,1,0:T(8,128)(2,1)S(1)}, bf16[1,8,2304]{2,1,0:T(8,128)(2,1)S(1)}, u32[]{:S(2)}, u32[]{:S(2)}) collective-permute-start(bf16[1,8,2304]{2,1,0:T(8,128)(2,1)S(1)} %shard_map.87.one_ref), channel_id=1, source_target_pairs={{0,8},{1,25},{2,10},{3,27},{4,12},{5,29},{6,14},{7,31},{8,0},{9,17... | collective-permute-start | bytes 110600 | tf_op jit(solution)/shard_map/ppermute | solution.py:403
  65.5 9.5 %collective-permute-start.1 = (bf16[1,8,2304]{2,1,0:T(8,128)(2,1)S(1)}, bf16[1,8,2304]{2,1,0:T(8,128)(2,1)S(1)}, u32[]{:S(2)}, u32[]{:S(2)}) collective-permute-start(bf16[1,8,2304]{2,1,0:T(8,128)(2,1)S(1)} %shard_map.88.one_ref), channel_id=1, source_target_pairs={{0,24},{1,9},{2,26},{3,11},{4,28},{5,13},{6,30},{7,15},{8,16},{9,1... | collective-permute-start | bytes 110600 | tf_op jit(solution)/shard_map/ppermute | solution.py:403

commit v6 on v5

--- a/solution.py
+++ b/solution.py
@@ -320,8 +320,9 @@
     for j in range(nb):
         at = slice(j * BLOCK, (j + 1) * BLOCK)
         term = members_ref[0, 0, :, at].astype(F32) * weight_ref[:, at] * blocks[j]
-        for taker in range(out_ref.shape[0]):
-            out_ref[taker, :, at] = term[taker * 8:taker * 8 + 8].astype(BF16)
+        half, at = j // (nb // 2), slice(j % (nb // 2) * BLOCK, (j % (nb // 2) + 1) * BLOCK)
+        for taker in range(out_ref.shape[0] // 2):
+            out_ref[2 * taker + half, :, at] = term[taker * 8:taker * 8 + 8].astype(BF16)
 
 
 def sum_kernel(in_ref, out_ref):
@@ -331,16 +332,20 @@
     out_ref[0] = total.astype(BF16)
 
 
-def add_kernel(one_ref, two_ref, out_ref):
-    out_ref[0] = (one_ref[0].astype(F32) + two_ref[0].astype(F32)).astype(BF16)
-
-
-def final_kernel(scale, own_ref, one_ref, two_ref, mask_ref, out_ref):
-    rows = out_ref.shape[1]
-    mask = mask_ref[0, pl.ds(pl.multiple_of(own_ref[0] * rows, rows), rows), :].astype(F32)
-    total = (mask * (one_ref[0].astype(F32) + two_ref[0].astype(F32)) / scale).astype(BF16)
+def add_kernel(scale, one_ref, two_ref, out_ref):
+    total = ((one_ref[0].astype(F32) + two_ref[0].astype(F32)) / scale).astype(BF16)
     for target in range(out_ref.shape[0]):
         out_ref[target] = total
+
+
+def final_kernel(mask_ref, in_ref, out_ref):
+    width = in_ref.shape[2]
+    for group in range(in_ref.shape[0] // 4):
+        rows = slice(group * 16, group * 16 + 16)
+        for half in range(2):
+            at = slice(half * width, (half + 1) * width)
+            part = jnp.concatenate([in_ref[4 * group + half].astype(F32), in_ref[4 * group + 2 + half].astype(F32)], axis=0)
+            out_ref[0, rows, at] = (part * mask_ref[0, rows, at].astype(F32)).astype(BF16)
 
 
 def call(kernel, out_shape, operands, scratch=(), spaces=(), limit=VMEM_LIMIT):
@@ -369,9 +374,9 @@
     space, mem = lax.axis_size("space"), lax.axis_size("mem")
     x_blocks, y_blocks = x_inverse.shape[0], y_inverse.shape[0]
     close = 8
-    apart = mem // close
-    near_groups = [[z * close + i for i in range(close)] for z in range(apart)]
-    far_groups = [[z * close + i for z in range(apart)] for i in range(close)]
+    half = mem // 2
+    halves = [list(range(half)), list(range(mem - close, mem)) + list(range(half, mem - close))]
+    twins = [(device, mem - close - device // close * close + device % close) for device in range(mem)]
     share = (HALF + FOLD, BLOCK)
 
     y_tables = prepare(y_inverse, y_coupling)
@@ -385,27 +390,17 @@
     sent = call(functools.partial(column_kernel, y_blocks), (space,) + share, (got,) + tuple(y_tables),
                 [pltpu.VMEM((BLOCK + EXTRA, y_blocks * BLOCK), BF16)])
     got = exchange(sent, "space")
-    own = (lax.axis_index("mem") % close).astype(jnp.int32)[None]
-    packed = (rows // close, columns)
+    packed = (2 * rows // half, columns // 2)
     inputs = (members, weight)
     near, arrived = landing(inputs)
-    terms = call(functools.partial(row_kernel, x_blocks), (close,) + packed,
+    terms = call(functools.partial(row_kernel, x_blocks), (half,) + packed,
                  (got,) + inputs + tuple(x_tables),
                  near + [pltpu.VMEM((rows, columns), BF16), arrived],
                  [pltpu.VMEM, pltpu.HBM, pltpu.HBM])
-    terms = exchange(terms, "mem", near_groups)
-    part = call(sum_kernel, (1,) + packed, (terms,))
-    for step in range(2):
-        pairs = []
-        for device in range(mem):
-            z, odd = device // close, (device + step) % 2
-            pairs.append((device, ((z ^ 1) if odd == 0 else ((z - 1) ^ 1) + 1) % apart * close + device % close))
-        other = lax.ppermute(part, "mem", pairs)
-        if step == 0:
-            part = call(add_kernel, (1,) + packed, (part, other))
-    result = call(functools.partial(final_kernel, float(mem - 1)), (close,) + packed, (own, part, other, mask),
-                  spaces=[pltpu.SMEM])
-    return exchange(result, "mem", near_groups).reshape(1, rows, columns)
+    part = call(sum_kernel, (1,) + packed, (exchange(terms, "mem", halves),))
+    other = lax.ppermute(part, "mem", twins)
+    result = call(functools.partial(add_kernel, float(mem - 1)), (half,) + packed, (part, other))
+    return call(final_kernel, (1, rows, columns), (mask, exchange(result, "mem", halves)))
 
 
 def solution(mesh):

time: 87.8 us -> 106 us (1.21)
  blocking collectives: 25.4 us -> 56.2 us
  starting transfers between devices: 30.1 us -> 15.3 us
  waiting for transfers between devices: 17.6 us -> 20.1 us
    all_to_all x2, blocking collectives: 25.4 us -> 56.2 us  [exchange(): lax.all_to_all(array, axis, split_axis=0, concat_axis=0, tiled=True, axis...]
    ppermute x2 -> x1, starting transfers between devices: 16.9 us -> 2.05 us  [local(): other = lax.ppermute(part, 'mem', twins)]
    ppermute x2 -> x1, waiting for transfers between devices: 3.94 us -> 6.48 us  [local(): other = lax.ppermute(part, 'mem', twins)]
  transfers between devices with their start and end apart: 4 -> 3, of which waited for: 4 -> 3; matrix products, arithmetic and copies ran while one was open for 0% -> 0% of each run, Pallas kernels for 8% -> 7%
where the time goes in v6:
time: 106 us
  blocking collectives  56.2 us (53%)
  waiting for transfers between devices  20.1 us (19%)
  starting transfers between devices  15.3 us (14%)
  Pallas kernels  14.2 us (13%)
    all_to_all x2, blocking collectives, exchange(): lax.all_to_all(array, axis, split_axis=0, concat_axis=0, tiled=True, axis...  56.2 us
    all_to_all x2, waiting for transfers between devices, exchange(): lax.all_to_all(array, axis, split_axis=0, concat_axis=0, tiled=True, axis...  13.6 us
    all_to_all x2, starting transfers between devices, exchange(): lax.all_to_all(array, axis, split_axis=0, concat_axis=0, tiled=True, axis...  13.2 us
    pallas_call x2, Pallas kernels, prepare(): pl.pallas_call(functools.partial(prepare_kernel, nb), out_shape=tuple((ja...  7.15 us
    pallas_call x6, Pallas kernels, call(): pl.pallas_call(kernel, out_shape=jax.ShapeDtypeStruct(out_shape, BF16), i...  7.07 us
    ppermute x1, waiting for transfers between devices, local(): other = lax.ppermute(part, 'mem', twins)  6.48 us
  transfers between devices with their start and end apart: 3, of which 3 were waited for; matrix products, arithmetic and copies ran while one was open for 0% of the time, Pallas kernels for 7%

profile of v6, /device:TPU:1, one launch (start us, length us, event | category | flops | bytes accessed | tf_op | source)
XLA Modules:
  0.0 106.0 jit_solution(4595916014532951072)
XLA Ops:
  0.0 2.3 %shard_map.82 = bf16[16,72,128]{2,1,0:T(8,128)(2,1)} custom-call(bf16[1,64,2304]{2,1,0:T(8,128)(2,1)} %increment_hbm.1, s32[1,64,2304]{2,1,0:T(8,128)} %mask_ref.1, bf16[1,1,64,2304]{3,2,1,0:T(8,128)(2,1)} %refs_0_.1, f32[64,2304]{1,0:T(8,128)} %refs_1_.1), custom_call_target="tpu_custom_call" | custom-call | flops 1000000 | bytes 2000000 | tf_op jit(solution)/shard_map/pallas_call | solution.py:353
  2.3 0.0 copy-start.4
  2.3 0.0 copy-start.5
  2.4 9.3 %all-to-all-start = ((bf16[16,72,128]{2,1,0:T(8,128)(2,1)}), bf16[16,72,128]{2,1,0:T(8,128)(2,1)S(1)}, u32[]{:S(2)}, u32[]{:S(2)}) async-start(bf16[16,72,128]{2,1,0:T(8,128)(2,1)} %shard_map.82), calls=%async_computation | async-start | bytes 589824 | tf_op jit(solution)/shard_map/all_to_all | solution.py:369
  11.7 0.0 copy-done.4
  11.7 0.0 copy-done.5
  11.7 2.6 %shard_map.83 = (bf16[8,128,128]{2,1,0:T(8,128)(2,1)S(1)}, bf16[128,128]{1,0:T(8,128)(2,1)S(1)}, bf16[128,128]{1,0:T(8,128)(2,1)S(1)}, bf16[128,128]{1,0:T(8,128...) custom-call(f32[7]{0:T(128)S(1)} %copy-done.5, bf16[8,128,128]{2,1,0:T(8,128)(2,1)S(1)} %copy-done.4), custom_call_target="tpu_custom_call" | custom-call | flops 6710886400 | bytes 4000000 | tf_op jit(solution)/shard_map/pallas_call | solution.py:188
  14.4 7.9 %all-to-all-done.in_ref = bf16[16,72,128]{2,1,0:T(8,128)(2,1)S(1)} async-done(((bf16[16,72,128]{2,1,0:T(8,128)(2,1)}), bf16[16,72,128]{2,1,0:T(8,128)(2,1)S(1)}, u32[]{:S(2)}, u32[]{:S(2)}) %all-to-all-start) | async-done | bytes 294944 | tf_op jit(solution)/shard_map/all_to_all | solution.py:369
  22.3 2.1 %shard_map.84 = bf16[16,72,128]{2,1,0:T(8,128)(2,1)} custom-call(bf16[16,72,128]{2,1,0:T(8,128)(2,1)S(1)} %all-to-all-done.in_ref, bf16[8,128,128]{2,1,0:T(8,128)(2,1)S(1)} %get-tuple-element.17.refs_0_, bf16[128,128]{1,0:T(8,128)(2,1)S(1)} %get-tuple-element.18.refs_1_, bf16[128,128]{1,0:T(8,128)(2,1)S(1)} %get-tuple-element.19.refs_2_, ...), custom_call_target="tpu_custom_call" | custom-call | flops 1000000 | bytes 2000000 | tf_op jit(solution)/shard_map/pallas_call | solution.py:353
  24.4 3.9 %all-to-all-start.1 = ((bf16[16,72,128]{2,1,0:T(8,128)(2,1)}), bf16[16,72,128]{2,1,0:T(8,128)(2,1)S(1)}, u32[]{:S(2)}, u32[]{:S(2)}) async-start(bf16[16,72,128]{2,1,0:T(8,128)(2,1)} %shard_map.84), calls=%async_computation.1 | async-start | bytes 589824 | tf_op jit(solution)/shard_map/all_to_all | solution.py:369
  28.3 0.0 copy-done.3
  28.3 0.0 copy-done.6
  28.3 0.0 copy-start
  28.3 0.0 copy-start.2
  28.3 4.5 %shard_map.85 = (bf16[18,128,128]{2,1,0:T(8,128)(2,1)S(1)}, bf16[256,256]{1,0:T(8,128)(2,1)S(1)}, bf16[256,256]{1,0:T(8,128)(2,1)S(1)}, bf16[256,128]{1,0:T(8,12...) custom-call(f32[17]{0:T(128)S(1)} %copy-done.6, bf16[18,128,128]{2,1,0:T(8,128)(2,1)S(1)} %copy-done.3), custom_call_target="tpu_custom_call" | custom-call | flops 15099494400 | bytes 4000000 | tf_op jit(solution)/shard_map/pallas_call | solution.py:188
  32.8 5.7 %all-to-all-done.1.in_ref = bf16[16,72,128]{2,1,0:T(8,128)(2,1)S(1)} async-done(((bf16[16,72,128]{2,1,0:T(8,128)(2,1)}), bf16[16,72,128]{2,1,0:T(8,128)(2,1)S(1)}, u32[]{:S(2)}, u32[]{:S(2)}) %all-to-all-start.1) | async-done | bytes 294944 | tf_op jit(solution)/shard_map/all_to_all | solution.py:369
  38.5 0.0 copy-done
  38.5 0.0 copy-done.2
  38.5 1.8 %shard_map.86 = bf16[16,8,1152]{2,1,0:T(8,128)(2,1)S(1)} custom-call(bf16[16,72,128]{2,1,0:T(8,128)(2,1)S(1)} %all-to-all-done.1.in_ref, bf16[1,1,64,2304]{3,2,1,0:T(8,128)(2,1)S(1)} %copy-done.2, f32[64,2304]{1,0:T(8,128)S(1)} %copy-done, bf16[18,128,128]{2,1,0:T(8,128)(2,1)S(1)} %get-tuple-element.23.refs_2_, ...), custom_call_target="tpu_custom_call" | custom-call | flops 1000000 | bytes 2000000 | tf_op jit(solution)/shard_map/pallas_call | solution.py:353
  40.3 34.0 %all_to_all.20.in_ref = bf16[16,8,1152]{2,1,0:T(8,128)(2,1)S(1)} all-to-all(bf16[16,8,1152]{2,1,0:T(8,128)(2,1)S(1)} %shard_map.86), channel_id=1, replica_groups={{0,1,2,3,4,5,6,7,8,9,10,11,12,13,14,15},{24,25,26,27,28,29,30,31,16,17,..., dimensions={0} | all-to-all | bytes 589824 | tf_op jit(solution)/shard_map/all_to_all | solution.py:369
  74.4 2.0 %collective-permute-start = (bf16[1,8,1152]{2,1,0:T(8,128)(2,1)S(1)}, bf16[1,8,1152]{2,1,0:T(8,128)(2,1)S(1)}, u32[]{:S(2)}, u32[]{:S(2)}) collective-permute-start(bf16[1,8,1152]{2,1,0:T(8,128)(2,1)S(1)} %shard_map.87.one_ref), channel_id=1, source_target_pairs={{0,24},{1,25},{2,26},{3,27},{4,28},{5,29},{6,30},{7,31},{8,16},{9,... | collective-permute-start | bytes 55304 | tf_op jit(solution)/shard_map/ppermute | solution.py:401
  76.4 6.5 %collective-permute-done.two_ref = bf16[1,8,1152]{2,1,0:T(8,128)(2,1)S(1)} collective-permute-done((bf16[1,8,1152]{2,1,0:T(8,128)(2,1)S(1)}, bf16[1,8,1152]{2,1,0:T(8,128)(2,1)S(1)}, u32[]{:S(2)}, u32[]{:S(2)}) %collective-permute-start) | collective-permute-done | bytes 18464 | tf_op jit(solution)/shard_map/ppermute | solution.py:401
  82.9 22.3 %all_to_all.21.in_ref = bf16[16,8,1152]{2,1,0:T(8,128)(2,1)S(1)} all-to-all(bf16[16,8,1152]{2,1,0:T(8,128)(2,1)S(1)} %shard_map.88), channel_id=1, replica_groups={{0,1,2,3,4,5,6,7,8,9,10,11,12,13,14,15},{24,25,26,27,28,29,30,31,16,17,..., dimensions={0} | all-to-all | bytes 589824 | tf_op jit(solution)/shard_map/all_to_all | solution.py:369
  105.2 0.8 shard_map.89
  (6 shorter events, 0.1 us)
Async XLA Ops:
  2.3 9.4 %copy-start.4 = (bf16[8,128,128]{2,1,0:T(8,128)(2,1)S(1)}, bf16[8,128,128]{2,1,0:T(8,128)(2,1)}, u32[]{:S(2)}) copy-start(bf16[8,128,128]{2,1,0:T(8,128)(2,1)} %g_ref.2) | copy-start | bytes 786436
  2.3 9.4 %copy-start.5 = (f32[7]{0:T(128)S(1)}, f32[7]{0:T(128)}, u32[]{:S(2)}) copy-start(f32[7]{0:T(128)} %c_ref.2) | copy-start | bytes 88
  2.4 19.9 %all-to-all-start = ((bf16[16,72,128]{2,1,0:T(8,128)(2,1)}), bf16[16,72,128]{2,1,0:T(8,128)(2,1)S(1)}, u32[]{:S(2)}, u32[]{:S(2)}) async-start(bf16[16,72,128]{2,1,0:T(8,128)(2,1)} %shard_map.82), calls=%async_computation | async-start | bytes 589824 | tf_op jit(solution)/shard_map/all_to_all | solution.py:369
  22.3 6.0 %copy-start.3 = (bf16[18,128,128]{2,1,0:T(8,128)(2,1)S(1)}, bf16[18,128,128]{2,1,0:T(8,128)(2,1)}, u32[]{:S(2)}) copy-start(bf16[18,128,128]{2,1,0:T(8,128)(2,1)} %g_ref.3) | copy-start | bytes 1769476
  24.4 3.9 %copy-start.6 = (f32[17]{0:T(128)S(1)}, f32[17]{0:T(128)}, u32[]{:S(2)}) copy-start(f32[17]{0:T(128)} %c_ref.3) | copy-start | bytes 208
  24.4 14.2 %all-to-all-start.1 = ((bf16[16,72,128]{2,1,0:T(8,128)(2,1)}), bf16[16,72,128]{2,1,0:T(8,128)(2,1)S(1)}, u32[]{:S(2)}, u32[]{:S(2)}) async-start(bf16[16,72,128]{2,1,0:T(8,128)(2,1)} %shard_map.84), calls=%async_computation.1 | async-start | bytes 589824 | tf_op jit(solution)/shard_map/all_to_all | solution.py:369
  28.3 10.3 %copy-start = (f32[64,2304]{1,0:T(8,128)S(1)}, f32[64,2304]{1,0:T(8,128)}, u32[]{:S(2)}) copy-start(f32[64,2304]{1,0:T(8,128)} %refs_1_.1) | copy-start | bytes 1769476
  28.3 10.3 %copy-start.2 = (bf16[1,1,64,2304]{3,2,1,0:T(8,128)(2,1)S(1)}, bf16[1,1,64,2304]{3,2,1,0:T(8,128)(2,1)}, u32[]{:S(2)}) copy-start(bf16[1,1,64,2304]{3,2,1,0:T(8,128)(2,1)} %refs_0_.1) | copy-start | bytes 884740
  74.3 30.9 %copy-start.1 = (s32[1,64,2304]{2,1,0:T(8,128)S(1)}, s32[1,64,2304]{2,1,0:T(8,128)}, u32[]{:S(2)}) copy-start(s32[1,64,2304]{2,1,0:T(8,128)} %mask_ref.1) | copy-start | bytes 1769476
  74.4 8.5 %collective-permute-start = (bf16[1,8,1152]{2,1,0:T(8,128)(2,1)S(1)}, bf16[1,8,1152]{2,1,0:T(8,128)(2,1)S(1)}, u32[]{:S(2)}, u32[]{:S(2)}) collective-permute-start(bf16[1,8,1152]{2,1,0:T(8,128)(2,1)S(1)} %shard_map.87.one_ref), channel_id=1, source_target_pairs={{0,24},{1,25},{2,26},{3,27},{4,28},{5,29},{6,30},{7,31},{8,16},{9,... | collective-permute-start | bytes 55304 | tf_op jit(solution)/shard_map/ppermute | solution.py:401

commit v7 on v5

--- a/solution.py
+++ b/solution.py
@@ -381,7 +381,7 @@
     near, arrived = landing(inputs)
     sent = call(start_kernel, (space,) + share, inputs,
                 near + [arrived], [pltpu.HBM] * 4, WIDE_LIMIT)
-    got = exchange(sent, "space")
+    got, x_tables, y_tables = lax.optimization_barrier((exchange(sent, "space"), x_tables, y_tables))
     sent = call(functools.partial(column_kernel, y_blocks), (space,) + share, (got,) + tuple(y_tables),
                 [pltpu.VMEM((BLOCK + EXTRA, y_blocks * BLOCK), BF16)])
     got = exchange(sent, "space")

time: 87.8 us -> 86.8 us (0.989)
  blocking collectives: 25.4 us -> 39.3 us
  waiting for transfers between devices: 17.6 us -> 7.29 us
  starting transfers between devices: 30.1 us -> 26.3 us
    all_to_all x2 -> x3, blocking collectives: 25.4 us -> 39.3 us  [exchange(): lax.all_to_all(array, axis, split_axis=0, concat_axis=0, tiled=True, axis...]
    all_to_all x2 -> x1, waiting for transfers between devices: 13.6 us -> 3.35 us  [exchange(): lax.all_to_all(array, axis, split_axis=0, concat_axis=0, tiled=True, axis...]
    all_to_all x2 -> x1, starting transfers between devices: 13.2 us -> 9.33 us  [exchange(): lax.all_to_all(array, axis, split_axis=0, concat_axis=0, tiled=True, axis...]
  transfers between devices with their start and end apart: 4 -> 3, of which waited for: 4 -> 3; matrix products, arithmetic and copies ran while one was open for 0% -> 0% of each run, Pallas kernels for 8% -> 8%
where the time goes in v7:
time: 86.8 us; the launch traced here: 86.5 us
  blocking collectives  39.3 us (45%)
  starting transfers between devices  26.3 us (30%)
  Pallas kernels  12.7 us (15%)
  waiting for transfers between devices  7.29 us (8%)
    all_to_all x3, blocking collectives, exchange(): lax.all_to_all(array, axis, split_axis=0, concat_axis=0, tiled=True, axis...  39.3 us
    ppermute x2, starting transfers between devices, local(): other = lax.ppermute(part, 'mem', pairs)  16.9 us
    all_to_all x1, starting transfers between devices, exchange(): lax.all_to_all(array, axis, split_axis=0, concat_axis=0, tiled=True, axis...  9.33 us
    pallas_call x2, Pallas kernels, prepare(): pl.pallas_call(functools.partial(prepare_kernel, nb), out_shape=tuple((ja...  7.14 us
    pallas_call x6, Pallas kernels, call(): pl.pallas_call(kernel, out_shape=jax.ShapeDtypeStruct(out_shape, BF16), i...  5.53 us
    ppermute x2, waiting for transfers between devices, local(): other = lax.ppermute(part, 'mem', pairs)  3.94 us
    all_to_all x1, waiting for transfers between devices, exchange(): lax.all_to_all(array, axis, split_axis=0, concat_axis=0, tiled=True, axis...  3.35 us
  transfers between devices with their start and end apart: 3, of which 3 were waited for; matrix products, arithmetic and copies ran while one was open for 0% of the time, Pallas kernels for 8%

profile of v7, /device:TPU:1, one launch (start us, length us, event | category | flops | bytes accessed | tf_op | source)
XLA Modules:
  0.0 86.5 jit_solution(15363464836178204116)
XLA Ops:
  0.0 2.3 %shard_map.82 = bf16[16,72,128]{2,1,0:T(8,128)(2,1)} custom-call(bf16[1,64,2304]{2,1,0:T(8,128)(2,1)} %increment_hbm.1, s32[1,64,2304]{2,1,0:T(8,128)} %mask_ref.1, bf16[1,1,64,2304]{3,2,1,0:T(8,128)(2,1)} %refs_0_.1, f32[64,2304]{1,0:T(8,128)} %refs_1_.1), custom_call_target="tpu_custom_call" | custom-call | flops 1000000 | bytes 2000000 | tf_op jit(solution)/shard_map/pallas_call | solution.py:348
  2.3 0.0 copy-start.4
  2.3 0.0 copy-start.5
  2.4 9.3 %all-to-all-start = ((bf16[16,72,128]{2,1,0:T(8,128)(2,1)}), bf16[16,72,128]{2,1,0:T(8,128)(2,1)S(1)}, u32[]{:S(2)}, u32[]{:S(2)}) async-start(bf16[16,72,128]{2,1,0:T(8,128)(2,1)} %shard_map.82), calls=%async_computation | async-start | bytes 589824 | tf_op jit(solution)/shard_map/all_to_all | solution.py:364
  11.7 0.0 copy-start.3
  11.7 0.0 copy-start.6
  11.7 2.6 %shard_map.84 = (bf16[8,128,128]{2,1,0:T(8,128)(2,1)S(1)}, bf16[128,128]{1,0:T(8,128)(2,1)S(1)}, bf16[128,128]{1,0:T(8,128)(2,1)S(1)}, bf16[128,128]{1,0:T(8,128...) custom-call(f32[7]{0:T(128)S(1)} %copy-done.5, bf16[8,128,128]{2,1,0:T(8,128)(2,1)S(1)} %copy-done.4), custom_call_target="tpu_custom_call" | custom-call | flops 6710886400 | bytes 4000000 | tf_op jit(solution)/shard_map/pallas_call | solution.py:188
  14.4 0.0 copy-done.3
  14.4 0.0 copy-done.6
  14.4 4.5 %shard_map.83 = (bf16[18,128,128]{2,1,0:T(8,128)(2,1)S(1)}, bf16[256,256]{1,0:T(8,128)(2,1)S(1)}, bf16[256,256]{1,0:T(8,128)(2,1)S(1)}, bf16[256,128]{1,0:T(8,12...) custom-call(f32[17]{0:T(128)S(1)} %copy-done.6, bf16[18,128,128]{2,1,0:T(8,128)(2,1)S(1)} %copy-done.3), custom_call_target="tpu_custom_call" | custom-call | flops 15099494400 | bytes 4000000 | tf_op jit(solution)/shard_map/pallas_call | solution.py:188
  18.9 3.4 %all-to-all-done.in_ref = bf16[16,72,128]{2,1,0:T(8,128)(2,1)S(1)} async-done(((bf16[16,72,128]{2,1,0:T(8,128)(2,1)}), bf16[16,72,128]{2,1,0:T(8,128)(2,1)S(1)}, u32[]{:S(2)}, u32[]{:S(2)}) %all-to-all-start) | async-done | bytes 294944 | tf_op jit(solution)/shard_map/all_to_all | solution.py:364
  22.3 1.4 %shard_map.85 = bf16[16,72,128]{2,1,0:T(8,128)(2,1)S(1)} custom-call(bf16[16,72,128]{2,1,0:T(8,128)(2,1)S(1)} %all-to-all-done.in_ref, bf16[8,128,128]{2,1,0:T(8,128)(2,1)S(1)} %get-tuple-element.43.refs_0_, bf16[128,128]{1,0:T(8,128)(2,1)S(1)} %get-tuple-element.44.refs_1_, bf16[128,128]{1,0:T(8,128)(2,1)S(1)} %get-tuple-element.45.refs_2_, ...), custom_call_target="tpu_custom_call" | custom-call | flops 1000000 | bytes 2000000 | tf_op jit(solution)/shard_map/pallas_call | solution.py:348
  23.6 0.0 copy-start.2
  23.7 14.1 %all_to_all.20.in_ref = bf16[16,72,128]{2,1,0:T(8,128)(2,1)S(1)} all-to-all(bf16[16,72,128]{2,1,0:T(8,128)(2,1)S(1)} %shard_map.85), channel_id=1, replica_groups=mesh['space'=16,'mem'=32] {'space'}, dimensions={0} | all-to-all | bytes 589824 | tf_op jit(solution)/shard_map/all_to_all | solution.py:364
  37.8 1.8 %shard_map.86 = bf16[8,8,2304]{2,1,0:T(8,128)(2,1)S(1)} custom-call(bf16[16,72,128]{2,1,0:T(8,128)(2,1)S(1)} %all_to_all.20.in_ref, bf16[1,1,64,2304]{3,2,1,0:T(8,128)(2,1)S(1)} %copy-done.2, f32[64,2304]{1,0:T(8,128)S(1)} %copy-done, bf16[18,128,128]{2,1,0:T(8,128)(2,1)S(1)} %get-tuple-element.49.refs_2_, bf16[256,256]{1,0:T(8,128)(2,1)S(1)} %get-tuple-element.50.refs_3_, ...), custom_call_target="tpu_custom_call" | custom-call | flops 1000000 | bytes 2000000 | tf_op jit(solution)/shard_map/pallas_call | solution.py:348
  39.5 0.0 copy-start.1
  39.5 13.6 %all_to_all.21.in_ref = bf16[8,8,2304]{2,1,0:T(8,128)(2,1)S(1)} all-to-all(bf16[8,8,2304]{2,1,0:T(8,128)(2,1)S(1)} %shard_map.86), channel_id=1, replica_groups={{0,1,2,3,4,5,6,7},{8,9,10,11,12,13,14,15},{16,17,18,19,20,21,22,23},{24..., dimensions={0} | all-to-all | bytes 589824 | tf_op jit(solution)/shard_map/all_to_all | solution.py:364
  53.2 9.8 %collective-permute-start = (bf16[1,8,2304]{2,1,0:T(8,128)(2,1)S(1)}, bf16[1,8,2304]{2,1,0:T(8,128)(2,1)S(1)}, u32[]{:S(2)}, u32[]{:S(2)}) collective-permute-start(bf16[1,8,2304]{2,1,0:T(8,128)(2,1)S(1)} %shard_map.87.one_ref), channel_id=1, source_target_pairs={{0,8},{1,25},{2,10},{3,27},{4,12},{5,29},{6,14},{7,31},{8,0},{9,17... | collective-permute-start | bytes 110600 | tf_op jit(solution)/shard_map/ppermute | solution.py:403
  62.9 1.6 %collective-permute-done.two_ref = bf16[1,8,2304]{2,1,0:T(8,128)(2,1)S(1)} collective-permute-done((bf16[1,8,2304]{2,1,0:T(8,128)(2,1)S(1)}, bf16[1,8,2304]{2,1,0:T(8,128)(2,1)S(1)}, u32[]{:S(2)}, u32[]{:S(2)}) %collective-permute-start) | collective-permute-done | bytes 36896 | tf_op jit(solution)/shard_map/ppermute | solution.py:403
  64.6 7.2 %collective-permute-start.1 = (bf16[1,8,2304]{2,1,0:T(8,128)(2,1)S(1)}, bf16[1,8,2304]{2,1,0:T(8,128)(2,1)S(1)}, u32[]{:S(2)}, u32[]{:S(2)}) collective-permute-start(bf16[1,8,2304]{2,1,0:T(8,128)(2,1)S(1)} %shard_map.88.one_ref), channel_id=1, source_target_pairs={{0,24},{1,9},{2,26},{3,11},{4,28},{5,13},{6,30},{7,15},{8,16},{9,1... | collective-permute-start | bytes 110600 | tf_op jit(solution)/shard_map/ppermute | solution.py:403
  71.7 2.3 %collective-permute-done.1.two_ref = bf16[1,8,2304]{2,1,0:T(8,128)(2,1)S(1)} collective-permute-done((bf16[1,8,2304]{2,1,0:T(8,128)(2,1)S(1)}, bf16[1,8,2304]{2,1,0:T(8,128)(2,1)S(1)}, u32[]{:S(2)}, u32[]{:S(2)}) %collective-permute-start.1) | collective-permute-done | bytes 36896 | tf_op jit(solution)/shard_map/ppermute | solution.py:403
  74.1 0.0 copy-done.1
  74.1 11.6 %all_to_all.22 = bf16[8,8,2304]{2,1,0:T(8,128)(2,1)S(1)} all-to-all(bf16[8,8,2304]{2,1,0:T(8,128)(2,1)S(1)} %shard_map.89), channel_id=1, replica_groups={{0,1,2,3,4,5,6,7},{8,9,10,11,12,13,14,15},{16,17,18,19,20,21,22,23},{24..., dimensions={0} | all-to-all | bytes 589824 | tf_op jit(solution)/shard_map/all_to_all | solution.py:364
  85.7 0.7 copy.10
  (8 shorter events, 0.1 us)
Async XLA Ops:
  2.3 9.4 %copy-start.4 = (bf16[8,128,128]{2,1,0:T(8,128)(2,1)S(1)}, bf16[8,128,128]{2,1,0:T(8,128)(2,1)}, u32[]{:S(2)}) copy-start(bf16[8,128,128]{2,1,0:T(8,128)(2,1)} %g_ref.3) | copy-start | bytes 786436
  2.3 9.4 %copy-start.5 = (f32[7]{0:T(128)S(1)}, f32[7]{0:T(128)}, u32[]{:S(2)}) copy-start(f32[7]{0:T(128)} %c_ref.3) | copy-start | bytes 88
  2.4 19.9 %all-to-all-start = ((bf16[16,72,128]{2,1,0:T(8,128)(2,1)}), bf16[16,72,128]{2,1,0:T(8,128)(2,1)S(1)}, u32[]{:S(2)}, u32[]{:S(2)}) async-start(bf16[16,72,128]{2,1,0:T(8,128)(2,1)} %shard_map.82), calls=%async_computation | async-start | bytes 589824 | tf_op jit(solution)/shard_map/all_to_all | solution.py:364
  11.7 2.7 %copy-start.3 = (bf16[18,128,128]{2,1,0:T(8,128)(2,1)S(1)}, bf16[18,128,128]{2,1,0:T(8,128)(2,1)}, u32[]{:S(2)}) copy-start(bf16[18,128,128]{2,1,0:T(8,128)(2,1)} %g_ref.2) | copy-start | bytes 1769476
  11.7 2.7 %copy-start.6 = (f32[17]{0:T(128)S(1)}, f32[17]{0:T(128)}, u32[]{:S(2)}) copy-start(f32[17]{0:T(128)} %c_ref.2) | copy-start | bytes 208
  22.3 15.5 %copy-start = (f32[64,2304]{1,0:T(8,128)S(1)}, f32[64,2304]{1,0:T(8,128)}, u32[]{:S(2)}) copy-start(f32[64,2304]{1,0:T(8,128)} %refs_1_.1) | copy-start | bytes 1769476
  23.6 14.1 %copy-start.2 = (bf16[1,1,64,2304]{3,2,1,0:T(8,128)(2,1)S(1)}, bf16[1,1,64,2304]{3,2,1,0:T(8,128)(2,1)}, u32[]{:S(2)}) copy-start(bf16[1,1,64,2304]{3,2,1,0:T(8,128)(2,1)} %refs_0_.1) | copy-start | bytes 884740
  39.5 34.5 %copy-start.1 = (s32[1,64,2304]{2,1,0:T(8,128)S(1)}, s32[1,64,2304]{2,1,0:T(8,128)}, u32[]{:S(2)}) copy-start(s32[1,64,2304]{2,1,0:T(8,128)} %mask_ref.1) | copy-start | bytes 1769476
  53.2 11.4 %collective-permute-start = (bf16[1,8,2304]{2,1,0:T(8,128)(2,1)S(1)}, bf16[1,8,2304]{2,1,0:T(8,128)(2,1)S(1)}, u32[]{:S(2)}, u32[]{:S(2)}) collective-permute-start(bf16[1,8,2304]{2,1,0:T(8,128)(2,1)S(1)} %shard_map.87.one_ref), channel_id=1, source_target_pairs={{0,8},{1,25},{2,10},{3,27},{4,12},{5,29},{6,14},{7,31},{8,0},{9,17... | collective-permute-start | bytes 110600 | tf_op jit(solution)/shard_map/ppermute | solution.py:403
  64.6 9.5 %collective-permute-start.1 = (bf16[1,8,2304]{2,1,0:T(8,128)(2,1)S(1)}, bf16[1,8,2304]{2,1,0:T(8,128)(2,1)S(1)}, u32[]{:S(2)}, u32[]{:S(2)}) collective-permute-start(bf16[1,8,2304]{2,1,0:T(8,128)(2,1)S(1)} %shard_map.88.one_ref), channel_id=1, source_target_pairs={{0,24},{1,9},{2,26},{3,11},{4,28},{5,13},{6,30},{7,15},{8,16},{9,1... | collective-permute-start | bytes 110600 | tf_op jit(solution)/shard_map/ppermute | solution.py:403

commit v8 on v7

--- a/solution.py
+++ b/solution.py
@@ -343,13 +343,25 @@
         out_ref[target] = total
 
 
-def call(kernel, out_shape, operands, scratch=(), spaces=(), limit=VMEM_LIMIT):
+def leave_kernel(in_ref, out_hbm, left):
+    count = left.shape[0]
+    part = in_ref.shape[1] // count
+    copies = [
+        pltpu.make_async_copy(in_ref.at[:, pl.ds(at * part, part)], out_hbm.at[:, pl.ds(at * part, part)], left.at[at])
+        for at in range(count)]
+    for copy in copies:
+        copy.start()
+    for copy in copies:
+        copy.wait()
+
+
+def call(kernel, out_shape, operands, scratch=(), spaces=(), limit=VMEM_LIMIT, out_space=pltpu.VMEM):
     spaces = tuple(spaces) + (pltpu.VMEM,) * (len(operands) - len(spaces))
     return pl.pallas_call(
         kernel,
         out_shape=jax.ShapeDtypeStruct(out_shape, BF16),
         in_specs=[pl.BlockSpec(memory_space=space) for space in spaces],
-        out_specs=pl.BlockSpec(memory_space=pltpu.VMEM),
+        out_specs=pl.BlockSpec(memory_space=out_space),
         scratch_shapes=list(scratch),
         compiler_params=pltpu.CompilerParams(vmem_limit_bytes=limit),
         cost_estimate=pl.CostEstimate(flops=1000000, bytes_accessed=2000000, transcendentals=0),
@@ -405,7 +417,8 @@
             part = call(add_kernel, (1,) + packed, (part, other))
     result = call(functools.partial(final_kernel, float(mem - 1)), (close,) + packed, (own, part, other, mask),
                   spaces=[pltpu.SMEM])
-    return exchange(result, "mem", near_groups).reshape(1, rows, columns)
+    result = exchange(result, "mem", near_groups).reshape(1, rows, columns)
+    return call(leave_kernel, (1, rows, columns), (result,), [pltpu.SemaphoreType.DMA((4,))], out_space=pltpu.HBM)
 
 
 def solution(mesh):

time: 86.8 us -> 86.9 us (level)
    pallas_call x6 -> x7, Pallas kernels: 5.53 us -> 6.27 us  [call(): pl.pallas_call(kernel, out_shape=jax.ShapeDtypeStruct(out_shape, BF16), i...]
where the time goes in v8:
time: 86.9 us; the launch traced here: 86.5 us
  blocking collectives  39.3 us (45%)
  starting transfers between devices  26.3 us (30%)
  Pallas kernels  13.4 us (15%)
  waiting for transfers between devices  7.29 us (8%)
    all_to_all x3, blocking collectives, exchange(): lax.all_to_all(array, axis, split_axis=0, concat_axis=0, tiled=True, axis...  39.3 us
    ppermute x2, starting transfers between devices, local(): other = lax.ppermute(part, 'mem', pairs)  16.9 us
    all_to_all x1, starting transfers between devices, exchange(): lax.all_to_all(array, axis, split_axis=0, concat_axis=0, tiled=True, axis...  9.33 us
    pallas_call x2, Pallas kernels, prepare(): pl.pallas_call(functools.partial(prepare_kernel, nb), out_shape=tuple((ja...  7.14 us
    pallas_call x7, Pallas kernels, call(): pl.pallas_call(kernel, out_shape=jax.ShapeDtypeStruct(out_shape, BF16), i...  6.27 us
    ppermute x2, waiting for transfers between devices, local(): other = lax.ppermute(part, 'mem', pairs)  3.94 us
    all_to_all x1, waiting for transfers between devices, exchange(): lax.all_to_all(array, axis, split_axis=0, concat_axis=0, tiled=True, axis...  3.35 us
  transfers between devices with their start and end apart: 3, of which 3 were waited for; matrix products, arithmetic and copies ran while one was open for 0% of the time, Pallas kernels for 8%

profile of v8, /device:TPU:1, one launch (start us, length us, event | category | flops | bytes accessed | tf_op | source)
XLA Modules:
  0.0 86.5 jit_solution(11372064202206939600)
XLA Ops:
  0.0 2.3 %shard_map.82 = bf16[16,72,128]{2,1,0:T(8,128)(2,1)} custom-call(bf16[1,64,2304]{2,1,0:T(8,128)(2,1)} %increment_hbm.1, s32[1,64,2304]{2,1,0:T(8,128)} %mask_ref.1, bf16[1,1,64,2304]{3,2,1,0:T(8,128)(2,1)} %refs_0_.1, f32[64,2304]{1,0:T(8,128)} %refs_1_.1), custom_call_target="tpu_custom_call" | custom-call | flops 1000000 | bytes 2000000 | tf_op jit(solution)/shard_map/pallas_call | solution.py:360
  2.3 0.0 copy-start.4
  2.3 0.0 copy-start.5
  2.4 9.3 %all-to-all-start = ((bf16[16,72,128]{2,1,0:T(8,128)(2,1)}), bf16[16,72,128]{2,1,0:T(8,128)(2,1)S(1)}, u32[]{:S(2)}, u32[]{:S(2)}) async-start(bf16[16,72,128]{2,1,0:T(8,128)(2,1)} %shard_map.82), calls=%async_computation | async-start | bytes 589824 | tf_op jit(solution)/shard_map/all_to_all | solution.py:376
  11.7 0.0 copy-done.4
  11.7 0.0 copy-done.5
  11.7 0.0 copy-start.3
  11.7 0.0 copy-start.6
  11.7 2.6 %shard_map.84 = (bf16[8,128,128]{2,1,0:T(8,128)(2,1)S(1)}, bf16[128,128]{1,0:T(8,128)(2,1)S(1)}, bf16[128,128]{1,0:T(8,128)(2,1)S(1)}, bf16[128,128]{1,0:T(8,128...) custom-call(f32[7]{0:T(128)S(1)} %copy-done.5, bf16[8,128,128]{2,1,0:T(8,128)(2,1)S(1)} %copy-done.4), custom_call_target="tpu_custom_call" | custom-call | flops 6710886400 | bytes 4000000 | tf_op jit(solution)/shard_map/pallas_call | solution.py:188
  14.4 0.0 copy-done.3
  14.4 4.5 %shard_map.83 = (bf16[18,128,128]{2,1,0:T(8,128)(2,1)S(1)}, bf16[256,256]{1,0:T(8,128)(2,1)S(1)}, bf16[256,256]{1,0:T(8,128)(2,1)S(1)}, bf16[256,128]{1,0:T(8,12...) custom-call(f32[17]{0:T(128)S(1)} %copy-done.6, bf16[18,128,128]{2,1,0:T(8,128)(2,1)S(1)} %copy-done.3), custom_call_target="tpu_custom_call" | custom-call | flops 15099494400 | bytes 4000000 | tf_op jit(solution)/shard_map/pallas_call | solution.py:188
  18.9 3.4 %all-to-all-done.in_ref = bf16[16,72,128]{2,1,0:T(8,128)(2,1)S(1)} async-done(((bf16[16,72,128]{2,1,0:T(8,128)(2,1)}), bf16[16,72,128]{2,1,0:T(8,128)(2,1)S(1)}, u32[]{:S(2)}, u32[]{:S(2)}) %all-to-all-start) | async-done | bytes 294944 | tf_op jit(solution)/shard_map/all_to_all | solution.py:376
  22.3 1.4 %shard_map.85 = bf16[16,72,128]{2,1,0:T(8,128)(2,1)S(1)} custom-call(bf16[16,72,128]{2,1,0:T(8,128)(2,1)S(1)} %all-to-all-done.in_ref, bf16[8,128,128]{2,1,0:T(8,128)(2,1)S(1)} %get-tuple-element.43.refs_0_, bf16[128,128]{1,0:T(8,128)(2,1)S(1)} %get-tuple-element.44.refs_1_, bf16[128,128]{1,0:T(8,128)(2,1)S(1)} %get-tuple-element.45.refs_2_, ...), custom_call_target="tpu_custom_call" | custom-call | flops 1000000 | bytes 2000000 | tf_op jit(solution)/shard_map/pallas_call | solution.py:360
  23.6 0.0 copy-start.2
  23.7 14.1 %all_to_all.20.in_ref = bf16[16,72,128]{2,1,0:T(8,128)(2,1)S(1)} all-to-all(bf16[16,72,128]{2,1,0:T(8,128)(2,1)S(1)} %shard_map.85), channel_id=1, replica_groups=mesh['space'=16,'mem'=32] {'space'}, dimensions={0} | all-to-all | bytes 589824 | tf_op jit(solution)/shard_map/all_to_all | solution.py:376
  37.8 1.8 %shard_map.86 = bf16[8,8,2304]{2,1,0:T(8,128)(2,1)S(1)} custom-call(bf16[16,72,128]{2,1,0:T(8,128)(2,1)S(1)} %all_to_all.20.in_ref, bf16[1,1,64,2304]{3,2,1,0:T(8,128)(2,1)S(1)} %copy-done.2, f32[64,2304]{1,0:T(8,128)S(1)} %copy-done, bf16[18,128,128]{2,1,0:T(8,128)(2,1)S(1)} %get-tuple-element.49.refs_2_, bf16[256,256]{1,0:T(8,128)(2,1)S(1)} %get-tuple-element.50.refs_3_, ...), custom_call_target="tpu_custom_call" | custom-call | flops 1000000 | bytes 2000000 | tf_op jit(solution)/shard_map/pallas_call | solution.py:360
  39.5 0.0 copy-start.1
  39.5 13.6 %all_to_all.21.in_ref = bf16[8,8,2304]{2,1,0:T(8,128)(2,1)S(1)} all-to-all(bf16[8,8,2304]{2,1,0:T(8,128)(2,1)S(1)} %shard_map.86), channel_id=1, replica_groups={{0,1,2,3,4,5,6,7},{8,9,10,11,12,13,14,15},{16,17,18,19,20,21,22,23},{24..., dimensions={0} | all-to-all | bytes 589824 | tf_op jit(solution)/shard_map/all_to_all | solution.py:376
  53.2 9.8 %collective-permute-start = (bf16[1,8,2304]{2,1,0:T(8,128)(2,1)S(1)}, bf16[1,8,2304]{2,1,0:T(8,128)(2,1)S(1)}, u32[]{:S(2)}, u32[]{:S(2)}) collective-permute-start(bf16[1,8,2304]{2,1,0:T(8,128)(2,1)S(1)} %shard_map.87.one_ref), channel_id=1, source_target_pairs={{0,8},{1,25},{2,10},{3,27},{4,12},{5,29},{6,14},{7,31},{8,0},{9,17... | collective-permute-start | bytes 110600 | tf_op jit(solution)/shard_map/ppermute | solution.py:415
  62.9 1.6 %collective-permute-done.two_ref = bf16[1,8,2304]{2,1,0:T(8,128)(2,1)S(1)} collective-permute-done((bf16[1,8,2304]{2,1,0:T(8,128)(2,1)S(1)}, bf16[1,8,2304]{2,1,0:T(8,128)(2,1)S(1)}, u32[]{:S(2)}, u32[]{:S(2)}) %collective-permute-start) | collective-permute-done | bytes 36896 | tf_op jit(solution)/shard_map/ppermute | solution.py:415
  64.6 7.2 %collective-permute-start.1 = (bf16[1,8,2304]{2,1,0:T(8,128)(2,1)S(1)}, bf16[1,8,2304]{2,1,0:T(8,128)(2,1)S(1)}, u32[]{:S(2)}, u32[]{:S(2)}) collective-permute-start(bf16[1,8,2304]{2,1,0:T(8,128)(2,1)S(1)} %shard_map.88.one_ref), channel_id=1, source_target_pairs={{0,24},{1,9},{2,26},{3,11},{4,28},{5,13},{6,30},{7,15},{8,16},{9,1... | collective-permute-start | bytes 110600 | tf_op jit(solution)/shard_map/ppermute | solution.py:415
  71.7 2.3 %collective-permute-done.1.two_ref = bf16[1,8,2304]{2,1,0:T(8,128)(2,1)S(1)} collective-permute-done((bf16[1,8,2304]{2,1,0:T(8,128)(2,1)S(1)}, bf16[1,8,2304]{2,1,0:T(8,128)(2,1)S(1)}, u32[]{:S(2)}, u32[]{:S(2)}) %collective-permute-start.1) | collective-permute-done | bytes 36896 | tf_op jit(solution)/shard_map/ppermute | solution.py:415
  74.1 11.6 %all_to_all.22 = bf16[8,8,2304]{2,1,0:T(8,128)(2,1)S(1)} all-to-all(bf16[8,8,2304]{2,1,0:T(8,128)(2,1)S(1)} %shard_map.89), channel_id=1, replica_groups={{0,1,2,3,4,5,6,7},{8,9,10,11,12,13,14,15},{16,17,18,19,20,21,22,23},{24..., dimensions={0} | all-to-all | bytes 589824 | tf_op jit(solution)/shard_map/all_to_all | solution.py:376
  85.7 0.7 shard_map.90
  (8 shorter events, 0.1 us)
Async XLA Ops:
  2.3 9.4 %copy-start.4 = (bf16[8,128,128]{2,1,0:T(8,128)(2,1)S(1)}, bf16[8,128,128]{2,1,0:T(8,128)(2,1)}, u32[]{:S(2)}) copy-start(bf16[8,128,128]{2,1,0:T(8,128)(2,1)} %g_ref.3) | copy-start | bytes 786436
  2.3 9.4 %copy-start.5 = (f32[7]{0:T(128)S(1)}, f32[7]{0:T(128)}, u32[]{:S(2)}) copy-start(f32[7]{0:T(128)} %c_ref.3) | copy-start | bytes 88
  2.4 19.9 %all-to-all-start = ((bf16[16,72,128]{2,1,0:T(8,128)(2,1)}), bf16[16,72,128]{2,1,0:T(8,128)(2,1)S(1)}, u32[]{:S(2)}, u32[]{:S(2)}) async-start(bf16[16,72,128]{2,1,0:T(8,128)(2,1)} %shard_map.82), calls=%async_computation | async-start | bytes 589824 | tf_op jit(solution)/shard_map/all_to_all | solution.py:376
  11.7 2.7 %copy-start.3 = (bf16[18,128,128]{2,1,0:T(8,128)(2,1)S(1)}, bf16[18,128,128]{2,1,0:T(8,128)(2,1)}, u32[]{:S(2)}) copy-start(bf16[18,128,128]{2,1,0:T(8,128)(2,1)} %g_ref.2) | copy-start | bytes 1769476
  11.7 2.7 %copy-start.6 = (f32[17]{0:T(128)S(1)}, f32[17]{0:T(128)}, u32[]{:S(2)}) copy-start(f32[17]{0:T(128)} %c_ref.2) | copy-start | bytes 208
  22.3 15.5 %copy-start = (f32[64,2304]{1,0:T(8,128)S(1)}, f32[64,2304]{1,0:T(8,128)}, u32[]{:S(2)}) copy-start(f32[64,2304]{1,0:T(8,128)} %refs_1_.1) | copy-start | bytes 1769476
  23.6 14.1 %copy-start.2 = (bf16[1,1,64,2304]{3,2,1,0:T(8,128)(2,1)S(1)}, bf16[1,1,64,2304]{3,2,1,0:T(8,128)(2,1)}, u32[]{:S(2)}) copy-start(bf16[1,1,64,2304]{3,2,1,0:T(8,128)(2,1)} %refs_0_.1) | copy-start | bytes 884740
  39.5 34.5 %copy-start.1 = (s32[1,64,2304]{2,1,0:T(8,128)S(1)}, s32[1,64,2304]{2,1,0:T(8,128)}, u32[]{:S(2)}) copy-start(s32[1,64,2304]{2,1,0:T(8,128)} %mask_ref.1) | copy-start | bytes 1769476
  53.2 11.4 %collective-permute-start = (bf16[1,8,2304]{2,1,0:T(8,128)(2,1)S(1)}, bf16[1,8,2304]{2,1,0:T(8,128)(2,1)S(1)}, u32[]{:S(2)}, u32[]{:S(2)}) collective-permute-start(bf16[1,8,2304]{2,1,0:T(8,128)(2,1)S(1)} %shard_map.87.one_ref), channel_id=1, source_target_pairs={{0,8},{1,25},{2,10},{3,27},{4,12},{5,29},{6,14},{7,31},{8,0},{9,17... | collective-permute-start | bytes 110600 | tf_op jit(solution)/shard_map/ppermute | solution.py:415
  64.6 9.5 %collective-permute-start.1 = (bf16[1,8,2304]{2,1,0:T(8,128)(2,1)S(1)}, bf16[1,8,2304]{2,1,0:T(8,128)(2,1)S(1)}, u32[]{:S(2)}, u32[]{:S(2)}) collective-permute-start(bf16[1,8,2304]{2,1,0:T(8,128)(2,1)S(1)} %shard_map.88.one_ref), channel_id=1, source_target_pairs={{0,24},{1,9},{2,26},{3,11},{4,28},{5,13},{6,30},{7,15},{8,16},{9,1... | collective-permute-start | bytes 110600 | tf_op jit(solution)/shard_map/ppermute | solution.py:415
